TPU v7x, 32 devices: a whole 2x2x4 slice. The times are simulated.
32 devices in a mesh: dp: 2 (over y), row: 4 (over z), col: 4 (over x, core).
Axes of the slice: x: 2, y: 2, z: 4, core: 2. Of those that a mesh axis runs over, the one named last changes fastest.
Arguments:
- hidden_in: bfloat16 [1024, 768], P(('dp', 'row'), 'col'), may hold values from -6 to 6
- lengths: int32 [8], P('dp'), may hold values from 16 to 128, as said below
- w_attn: bfloat16 [2, 768, 3072], P(None, 'col', 'row'), as said below
- b_qv: bfloat16 [2, 2, 768], P(None, None, 'row'), may hold values from -3 to 3
- b_out: bfloat16 [2, 768], P(None, 'col'), may hold values from -2 to 2
- ln_gain: bfloat16 [2, 2, 768], P(None, None, 'col'), may hold values from 0.5 to 1.5
- ln_bias: bfloat16 [2, 2, 768], P(None, None, 'col'), may hold values from -2 to 2
- w_up: bfloat16 [2, 768, 3072], P(None, 'col', 'row'), may hold values from -0.21875 to 0.21875
- b_up: bfloat16 [2, 3072], P(None, 'row'), may hold values from -3 to 3
- w_down: bfloat16 [2, 768, 3072], P(None, 'col', 'row'), may hold values from -0.15625 to 0.15625
- b_down: bfloat16 [2, 768], P(None, 'col'), may hold values from -2 to 2
- cotangent: bfloat16 [1024, 768], P(('dp', 'row'), 'col'), may hold values from -6 to 6
Outputs:
- out_hidden: bfloat16 [1024, 768], P(('dp', 'row'), 'col')
- grad_input: float32 [1024, 768], P(('dp', 'row'), 'col')
- grad_w_attn: float32 [2, 768, 3072], P(None, 'col', 'row')
- grad_b_qv: float32 [2, 2, 768], P(None, None, 'row')
- grad_b_out: float32 [2, 768], P(None, 'col')
- grad_ln_gain: float32 [2, 2, 768], P(None, None, 'col')
- grad_ln_bias: float32 [2, 2, 768], P(None, None, 'col')
- grad_w_up: float32 [2, 768, 3072], P(None, 'col', 'row')
- grad_b_up: float32 [2, 3072], P(None, 'row')
- grad_w_down: float32 [2, 768, 3072], P(None, 'col', 'row')
- grad_b_down: float32 [2, 768], P(None, 'col')
Inputs may be any that keep to these rules, and one draw needn't show every extreme that they name: `lengths`: each sequence's number of leading valid tokens; only keys before it are attended to. `w_attn`: independent entries.
All inputs are finite; a program needn't handle non-finite values.
Results may differ from a plain program's by a relative error of at most 0.03.
Values may be sent and summed in bfloat16 or wider, within the bound.
No kernel may reach another device: no remote copies, remote signals or barrier semaphores. Data moves between devices by JAX's collectives and lax.ppermute only.
A program may use at most 64 MiB of HBM per device.

v0:
```python
from functools import partial

import jax
import jax.numpy as jnp
from jax import lax
from jax.sharding import PartitionSpec as P

D = 768
HEAD_DIM = 64


epsilon = 1e-05
masked_score = -1e30


def times_transposed(left_side, right_side):
    return lax.dot_general(
        left_side, right_side, (((1,), (1,)), ((), ())), preferred_element_type=jnp.float32
    )


def inner_rows(left_side, right_side):
    return lax.dot_general(
        left_side, right_side, (((0,), (0,)), ((), ())), preferred_element_type=jnp.float32
    )


def spread_in(operand, weight):
    gathered = lax.all_gather(operand, "row", axis=0, tiled=True)
    own_rows = lax.all_to_all(gathered, "col", split_axis=0, concat_axis=1, tiled=True)
    summed = jnp.dot(
        own_rows,
        lax.all_gather(weight, "col", axis=0, tiled=True),
        preferred_element_type=jnp.float32,
    )
    return (operand, summed)


def spread_out(operand, weight_turned):
    gathered = lax.all_gather(operand, "col", axis=0, tiled=True)

    def partial_term(row_start, row_count):
        return times_transposed(gathered, weight_turned)

    summed = lax.psum_scatter(
        partial_term(jnp.int32(0), lax.axis_size("row") * operand.shape[0]).astype(jnp.bfloat16),
        "row",
        scatter_dimension=0,
        tiled=True,
    ).astype(jnp.float32)
    return (operand, summed)


def back_in(grad_low, weight, kept_in):
    grad_all = lax.all_gather(grad_low, "col", axis=0, tiled=True)
    source = lax.all_gather(kept_in, "row", axis=0, tiled=True)
    weight_grad = inner_rows(source, grad_all)
    bias_grad = jnp.sum(grad_all, axis=0, dtype=jnp.float32)

    def partial_term(row_start, row_count):
        return times_transposed(grad_all, weight)

    input_grad = lax.psum_scatter(
        partial_term(jnp.int32(0), lax.axis_size("row") * grad_low.shape[0]).astype(jnp.bfloat16),
        "row",
        scatter_dimension=0,
        tiled=True,
    ).astype(jnp.float32)
    return (weight_grad, bias_grad, input_grad)


def back_out(grad_low, weight_turned, kept_in):
    grad_all = lax.all_gather(grad_low, "row", axis=0, tiled=True)
    source = lax.all_gather(kept_in, "col", axis=0, tiled=True)
    weight_grad = inner_rows(grad_all, source)
    bias_grad = jnp.sum(grad_all, axis=0, dtype=jnp.float32)

    def partial_term(row_start, row_count):
        return jnp.dot(grad_all, weight_turned, preferred_element_type=jnp.float32)

    input_grad = lax.psum_scatter(
        partial_term(jnp.int32(0), lax.axis_size("col") * grad_low.shape[0]).astype(jnp.bfloat16),
        "col",
        scatter_dimension=0,
        tiled=True,
    ).astype(jnp.float32)
    return (weight_grad, bias_grad, input_grad)


def feature_total(members):
    return lax.psum(members, "col")


def norm_forward(operand, gain_row, shift_row):
    average = feature_total((jnp.sum(operand, axis=-1),))[0] / D
    centred = operand - average[:, None]
    variance = feature_total((jnp.sum(centred * centred, axis=-1),))[0] / D
    inverse_dev = lax.rsqrt(variance + epsilon)[:, None]
    normed = centred * inverse_dev
    return (normed * gain_row + shift_row, normed, inverse_dev)


def norm_back(grad_flow, normed, inverse_dev, gain_row):
    scaled = grad_flow * gain_row
    totals = feature_total((jnp.sum(scaled, axis=-1), jnp.sum(scaled * normed, axis=-1)))
    return inverse_dev * (scaled - totals[0][:, None] / D - normed * totals[1][:, None] / D)


def head_view(matrix):
    return matrix.reshape(matrix.shape[0], matrix.shape[1] // HEAD_DIM, HEAD_DIM)


def attention_scores(queries, keyset, length):
    scores = jnp.einsum(
        "qhd,khd->hqk", head_view(queries), head_view(keyset), preferred_element_type=jnp.float32
    ) * HEAD_DIM ** (-0.5)
    visible = lax.iota(jnp.int32, keyset.shape[0]) < length
    return jnp.where(visible[None, None, :], scores, masked_score)


def attention_forward(queries, keyset, values, length):
    scores = attention_scores(queries, keyset, length)
    highest = jnp.max(scores, axis=-1, keepdims=True)
    raised = jnp.exp(scores - highest)
    row_total = jnp.sum(raised, axis=-1, keepdims=True)
    weights = (raised / row_total).astype(jnp.bfloat16)
    mixture = jnp.einsum(
        "hqk,khd->qhd", weights, head_view(values), preferred_element_type=jnp.float32
    )
    return (mixture.reshape(queries.shape).astype(jnp.bfloat16), highest + jnp.log(row_total))


def attention_back(queries, keyset, values, length, log_total, grad_low):
    scale_factor = HEAD_DIM ** (-0.5)
    weights = jnp.exp(attention_scores(queries, keyset, length) - log_total)
    grad_view = head_view(grad_low)
    value_grad = jnp.einsum(
        "hqk,qhd->khd", weights.astype(jnp.bfloat16), grad_view, preferred_element_type=jnp.float32
    )
    prob_grad = jnp.einsum(
        "qhd,khd->hqk", grad_view, head_view(values), preferred_element_type=jnp.float32
    )
    score_grad = weights * (prob_grad - jnp.sum(weights * prob_grad, axis=-1, keepdims=True))
    score_low = score_grad.astype(jnp.bfloat16)
    query_grad = (
        jnp.einsum("hqk,khd->qhd", score_low, head_view(keyset), preferred_element_type=jnp.float32)
        * scale_factor
    )
    key_grad = (
        jnp.einsum(
            "hqk,qhd->khd", score_low, head_view(queries), preferred_element_type=jnp.float32
        )
        * scale_factor
    )
    flat_shape = queries.shape
    return jnp.concatenate(
        [
            query_grad.reshape(flat_shape),
            key_grad.reshape(flat_shape),
            value_grad.reshape(flat_shape),
        ],
        axis=1,
    ).astype(jnp.bfloat16)


def per_device(
    hidden_in, lengths, w_attn, b_qv, b_out, ln_gain, ln_bias, w_up, b_up, w_down, b_down, cotangent
):
    layers = w_attn.shape[0]
    head_width = w_attn.shape[2] // 4
    length = lax.dynamic_index_in_dim(lengths, lax.axis_index("col"), 0, keepdims=False)
    hidden = hidden_in.astype(jnp.float32)
    saved_state = []
    for layer_at in range(layers):
        w_in = w_attn[layer_at, :, : 3 * head_width]
        w_out_turned = w_attn[layer_at, :, 3 * head_width :]
        kept_in, projected = spread_in(hidden.astype(jnp.bfloat16), w_in)
        bias_in = jnp.concatenate(
            [b_qv[layer_at, 0], jnp.zeros((head_width,), jnp.bfloat16), b_qv[layer_at, 1]]
        )
        heads_all = (projected + bias_in).astype(jnp.bfloat16)
        queries = heads_all[:, :head_width]
        keyset = heads_all[:, head_width : 2 * head_width]
        values = heads_all[:, 2 * head_width :]
        mixture, log_total = attention_forward(queries, keyset, values, length)
        kept_mix, branch = spread_out(mixture, w_out_turned)
        normed_one, unit_one, inverse_one = norm_forward(
            hidden + branch + b_out[layer_at], ln_gain[layer_at, 0], ln_bias[layer_at, 0]
        )
        kept_normed, inner_sum = spread_in(normed_one.astype(jnp.bfloat16), w_up[layer_at])
        inner_pre = inner_sum + b_up[layer_at]
        active = jax.nn.gelu(inner_pre, approximate=False).astype(jnp.bfloat16)
        kept_active, outer_sum = spread_out(active, w_down[layer_at])
        hidden, unit_two, inverse_two = norm_forward(
            normed_one + outer_sum + b_down[layer_at], ln_gain[layer_at, 1], ln_bias[layer_at, 1]
        )
        saved_state.append(
            (
                w_in,
                w_out_turned,
                kept_in,
                queries,
                keyset,
                values,
                log_total,
                kept_mix,
                unit_one,
                inverse_one,
                kept_normed,
                inner_pre,
                kept_active,
                unit_two,
                inverse_two,
            )
        )
    out_hidden = hidden.astype(jnp.bfloat16)
    grad_flow = cotangent.astype(jnp.float32)
    layer_grads = [None] * layers
    gain_grads = [None] * layers
    shift_grads = [None] * layers
    for layer_at in reversed(range(layers)):
        (
            w_in,
            w_out_turned,
            kept_in,
            queries,
            keyset,
            values,
            log_total,
            kept_mix,
            unit_one,
            inverse_one,
            kept_normed,
            inner_pre,
            kept_active,
            unit_two,
            inverse_two,
        ) = saved_state[layer_at]
        gain_two = jnp.sum(grad_flow * unit_two, axis=0)
        shift_two = jnp.sum(grad_flow, axis=0)
        grad_sum_in = norm_back(grad_flow, unit_two, inverse_two, ln_gain[layer_at, 1])
        down_w, down_b, grad_active = back_out(
            grad_sum_in.astype(jnp.bfloat16), w_down[layer_at], kept_active
        )
        _, gelu_pull = jax.vjp(partial(jax.nn.gelu, approximate=False), inner_pre)
        grad_inner = gelu_pull(grad_active)[0].astype(jnp.bfloat16)
        up_w, up_b, grad_normed = back_in(grad_inner, w_up[layer_at], kept_normed)
        grad_normed = grad_sum_in + grad_normed
        gain_one = jnp.sum(grad_normed * unit_one, axis=0)
        shift_one = jnp.sum(grad_normed, axis=0)
        grad_attended = norm_back(grad_normed, unit_one, inverse_one, ln_gain[layer_at, 0])
        out_w, out_b, grad_mix = back_out(
            grad_attended.astype(jnp.bfloat16), w_out_turned, kept_mix
        )
        grad_heads = attention_back(
            queries, keyset, values, length, log_total, grad_mix.astype(jnp.bfloat16)
        )
        in_w, in_b, grad_hidden = back_in(grad_heads, w_in, kept_in)
        grad_flow = grad_attended + grad_hidden
        attn_w = jnp.concatenate([in_w, out_w], axis=1)
        qv_b = jnp.stack([in_b[:head_width], in_b[2 * head_width :]])
        layer_grads[layer_at] = (
            lax.psum(attn_w.astype(jnp.bfloat16), "dp").astype(jnp.float32),
            lax.psum(qv_b.astype(jnp.bfloat16), "dp").astype(jnp.float32),
            lax.psum(out_b.astype(jnp.bfloat16), "dp").astype(jnp.float32),
            lax.psum(up_w.astype(jnp.bfloat16), "dp").astype(jnp.float32),
            lax.psum(up_b.astype(jnp.bfloat16), "dp").astype(jnp.float32),
            lax.psum(down_w.astype(jnp.bfloat16), "dp").astype(jnp.float32),
            lax.psum(down_b.astype(jnp.bfloat16), "dp").astype(jnp.float32),
        )
        gain_grads[layer_at] = jnp.stack([gain_one, gain_two])
        shift_grads[layer_at] = jnp.stack([shift_one, shift_two])
    norm_totals = lax.psum((jnp.stack(gain_grads), jnp.stack(shift_grads)), ("dp", "row"))
    stacked = [
        jnp.stack([layer_grads[layer_at][member] for layer_at in range(layers)])
        for member in range(7)
    ]
    return (
        out_hidden,
        grad_flow,
        stacked[0],
        stacked[1],
        stacked[2],
        norm_totals[0],
        norm_totals[1],
        stacked[3],
        stacked[4],
        stacked[5],
        stacked[6],
    )


def solution(mesh):
    in_specs = (
        P(("dp", "row"), "col"),
        P("dp"),
        P(None, "col", "row"),
        P(None, None, "row"),
        P(None, "col"),
        P(None, None, "col"),
        P(None, None, "col"),
        P(None, "col", "row"),
        P(None, "row"),
        P(None, "col", "row"),
        P(None, "col"),
        P(("dp", "row"), "col"),
    )
    out_specs = (
        P(("dp", "row"), "col"),
        P(("dp", "row"), "col"),
        P(None, "col", "row"),
        P(None, None, "row"),
        P(None, "col"),
        P(None, None, "col"),
        P(None, None, "col"),
        P(None, "col", "row"),
        P(None, "row"),
        P(None, "col", "row"),
        P(None, "col"),
    )
    return jax.shard_map(
        per_device, mesh=mesh, in_specs=in_specs, out_specs=out_specs, check_vma=False
    )
```

profile of v0, /device:TPU:2, one launch (start us, length us, event | category | flops | bytes accessed | tf_op | source)
XLA Modules:
  0.0 655.2 jit_solution(8937819722365865595)
XLA Ops:
  8.0 13.1 %all_gather.68 = bf16[512,192]{0,1:T(8,128)(2,1)S(1)} all-gather(bf16[128,192]{0,1:T(8,128)(2,1)} %param.12), channel_id=1, replica_groups=mesh['dp'=2,'row'=4,'col'=4] {'row'}, dimensions={0}, use_global_device_ids=true | all-gather | bytes 245760 | tf_op jit(solution)/shard_map/all_gather | solution.py:29
  27.2 9.6 %all-gather = bf16[1,768,576]{2,1,0:T(8,128)(2,1)S(1)} all-gather(bf16[1,192,576]{2,1,0:T(8,128)(2,1)S(1)} %get-tuple-element.73), channel_id=2, replica_groups=mesh['dp'=2,'row'=4,'col'=4] {'col'}, dimensions={1}, use_global_device_ids=true | all-gather | bytes 1105920 | tf_op jit(solution)/shard_map/all_gather | solution.py:33
  48.0 18.5 %reduce-scatter.37.cloned.1.call-done = bf16[128,192]{1,0:T(8,128)(2,1)} async-done(((bf16[512,192]{1,0:T(8,128)(2,1)}), bf16[128,192]{1,0:T(8,128)(2,1)}) %reduce-scatter.37.cloned.1.call-update) | async-done | bytes 49168
  79.4 12.5 %all_gather.71 = bf16[512,192]{0,1:T(8,128)(2,1)S(1)} all-gather(bf16[128,192]{0,1:T(8,128)(2,1)S(1)} %fusion.74), channel_id=1, replica_groups=mesh['dp'=2,'row'=4,'col'=4] {'row'}, dimensions={0}, use_global_device_ids=true | all-gather | bytes 245760 | tf_op jit(solution)/shard_map/all_gather | solution.py:29
  114.3 18.3 %reduce-scatter.39.cloned.1.call-done = bf16[128,192]{1,0:T(8,128)(2,1)} async-done(((bf16[512,192]{1,0:T(8,128)(2,1)}), bf16[128,192]{1,0:T(8,128)(2,1)}) %reduce-scatter.39.cloned.1.call-update) | async-done | bytes 49168
  145.6 12.5 %all_gather.74 = bf16[512,192]{0,1:T(8,128)(2,1)S(1)} all-gather(bf16[128,192]{0,1:T(8,128)(2,1)S(1)} %fusion.75), channel_id=1, replica_groups=mesh['dp'=2,'row'=4,'col'=4] {'row'}, dimensions={0}, use_global_device_ids=true | all-gather | bytes 245760 | tf_op jit(solution)/shard_map/all_gather | solution.py:29
  163.3 9.8 %all-gather.2 = bf16[1,768,576]{2,1,0:T(8,128)(2,1)S(1)} all-gather(bf16[1,192,576]{2,1,0:T(8,128)(2,1)S(1)} %get-tuple-element.72), channel_id=4, replica_groups=mesh['dp'=2,'row'=4,'col'=4] {'col'}, dimensions={1}, use_global_device_ids=true | all-gather | bytes 1105920 | tf_op jit(solution)/shard_map/all_gather | solution.py:33
  181.6 17.9 %reduce-scatter.41.cloned.1.call-done = bf16[128,192]{1,0:T(8,128)(2,1)} async-done(((bf16[512,192]{1,0:T(8,128)(2,1)}), bf16[128,192]{1,0:T(8,128)(2,1)}) %reduce-scatter.41.cloned.1.call-update) | async-done | bytes 49168
  212.4 12.5 %all_gather.77 = bf16[512,192]{0,1:T(8,128)(2,1)S(1)} all-gather(bf16[128,192]{0,1:T(8,128)(2,1)S(1)} %fusion.76), channel_id=1, replica_groups=mesh['dp'=2,'row'=4,'col'=4] {'row'}, dimensions={0}, use_global_device_ids=true | all-gather | bytes 245760 | tf_op jit(solution)/shard_map/all_gather | solution.py:29
  247.3 18.3 %reduce-scatter.43.cloned.1.call-done = bf16[128,192]{1,0:T(8,128)(2,1)} async-done(((bf16[512,192]{1,0:T(8,128)(2,1)}), bf16[128,192]{1,0:T(8,128)(2,1)}) %reduce-scatter.43.cloned.1.call-update) | async-done | bytes 49168
  284.9 12.6 %all_gather.80 = bf16[512,192]{0,1:T(8,128)(2,1)S(1)} all-gather(bf16[128,192]{0,1:T(8,128)(2,1)S(1)} %fusion.82), channel_id=1, replica_groups=mesh['dp'=2,'row'=4,'col'=4] {'row'}, dimensions={0}, use_global_device_ids=true | all-gather | bytes 245760 | tf_op jit(solution)/shard_map/all_gather | solution.py:73
  298.8 20.7 %reduce-scatter.33.cloned.1.call-done = bf16[128,768]{1,0:T(8,128)(2,1)} async-done(((bf16[512,768]{1,0:T(8,128)(2,1)}), bf16[128,768]{1,0:T(8,128)(2,1)}) %reduce-scatter.33.cloned.1.call-update) | async-done | bytes 196624 | tf_op jit(solution)/shard_map/reduce_scatter | solution.py:81
  320.9 9.0 %all_gather.81 = bf16[512,768]{1,0:T(8,128)(2,1)S(1)} all-gather(bf16[128,768]{1,0:T(8,128)(2,1)S(1)} %fusion.22), channel_id=1, replica_groups=mesh['dp'=2,'row'=4,'col'=4] {'col'}, dimensions={0}, use_global_device_ids=true | all-gather | bytes 983040 | tf_op jit(solution)/shard_map/all_gather | solution.py:55
  332.2 20.7 %reduce-scatter.45.cloned.1.call-done = bf16[128,192]{1,0:T(8,128)(2,1)} async-done(((bf16[512,192]{1,0:T(8,128)(2,1)}), bf16[128,192]{1,0:T(8,128)(2,1)}) %reduce-scatter.45.cloned.1.call-update) | async-done | bytes 49168
  361.9 13.4 %all_gather.82 = bf16[512,192]{0,1:T(8,128)(2,1)} all-gather(bf16[128,192]{0,1:T(8,128)(2,1)S(1)} %fusion.88), channel_id=1, replica_groups=mesh['dp'=2,'row'=4,'col'=4] {'row'}, dimensions={0}, use_global_device_ids=true | all-gather | bytes 245760 | tf_op jit(solution)/shard_map/all_gather | solution.py:73
  378.1 16.6 %reduce-scatter.47.cloned.1.call-done = bf16[128,192]{1,0:T(8,128)(2,1)} async-done(((bf16[512,192]{1,0:T(8,128)(2,1)}), bf16[128,192]{1,0:T(8,128)(2,1)}) %reduce-scatter.47.cloned.1.call-update) | async-done | bytes 49168
  407.3 20.7 %reduce-scatter.49.cloned.1.call-done = bf16[128,192]{1,0:T(8,128)(2,1)} async-done(((bf16[512,192]{1,0:T(8,128)(2,1)}), bf16[128,192]{1,0:T(8,128)(2,1)}) %reduce-scatter.49.cloned.1.call-update) | async-done | bytes 49168
  438.7 12.5 %all_gather.84 = bf16[512,192]{0,1:T(8,128)(2,1)S(1)} all-gather(bf16[128,192]{0,1:T(8,128)(2,1)S(1)} %fusion.89), channel_id=1, replica_groups=mesh['dp'=2,'row'=4,'col'=4] {'row'}, dimensions={0}, use_global_device_ids=true | all-gather | bytes 245760 | tf_op jit(solution)/shard_map/all_gather | solution.py:73
  455.7 18.4 %reduce-scatter.35.cloned.1.call-done = bf16[128,768]{1,0:T(8,128)(2,1)} async-done(((bf16[512,768]{1,0:T(8,128)(2,1)}), bf16[128,768]{1,0:T(8,128)(2,1)}) %reduce-scatter.35.cloned.1.call-update) | async-done | bytes 196624 | tf_op jit(solution)/shard_map/reduce_scatter | solution.py:81
  490.9 16.8 %reduce-scatter.51.cloned.1.call-done = bf16[128,192]{1,0:T(8,128)(2,1)} async-done(((bf16[512,192]{1,0:T(8,128)(2,1)}), bf16[128,192]{1,0:T(8,128)(2,1)}) %reduce-scatter.51.cloned.1.call-update) | async-done | bytes 49168
  519.1 12.5 %all_gather.86 = bf16[512,192]{0,1:T(8,128)(2,1)S(1)} all-gather(bf16[128,192]{0,1:T(8,128)(2,1)S(1)} %fusion.87), channel_id=1, replica_groups=mesh['dp'=2,'row'=4,'col'=4] {'row'}, dimensions={0}, use_global_device_ids=true | all-gather | bytes 245760 | tf_op jit(solution)/shard_map/all_gather | solution.py:73
  539.6 12.3 %reduce-scatter.53.cloned.1.call-done = bf16[128,192]{1,0:T(8,128)(2,1)} async-done(((bf16[512,192]{1,0:T(8,128)(2,1)}), bf16[128,192]{1,0:T(8,128)(2,1)}) %reduce-scatter.53.cloned.1.call-update) | async-done | bytes 49168
  569.2 22.6 %all-reduce = (f32[2,2,192]{2,1,0:T(2,128)}, f32[2,2,192]{2,1,0:T(2,128)}) all-reduce(f32[2,2,192]{2,1,0:T(2,128)S(1)} %pad_maximum_fusion.2, f32[2,2,192]{2,1,0:T(2,128)S(1)} %pad_maximum_fusion.3), channel_id=1, replica_groups=mesh['dp'=2,'row'=4,'col'=4] {'dp','row'}, use_global_device_ids=true, to_apply=%region_64.65 | all-reduce | flops 1536 | bytes 12288 | tf_op jit(solution)/shard_map/psum | solution.py:273
  603.1 41.2 %all-reduce.9.cloned.1.call-done = (bf16[1,192,768]{2,1,0:T(8,128)(2,1)}, bf16[1,192,768]{2,1,0:T(8,128)(2,1)}, bf16[1,192,768]{2,1,0:T(8,128)(2,1)}, bf16[1,192...) async-done(((bf16[1,192,768]{2,1,0:T(8,128)(2,1)}, bf16[1,192,768]{2,1,0:T(8,128)(2,1)}, bf16[1,192,768]{2,1,0:T(8,128)(2,1)}, ...) | async-done | bytes 1769488 | tf_op jit(solution)/shard_map/psum | solution.py:263
  (376 shorter events, 245.7 us)
Async XLA Ops:
  22.5 15.6 %all-to-all-start = ((bf16[4,128,192]{1,2,0:T(8,128)(2,1)}), bf16[4,128,192]{1,2,0:T(8,128)(2,1)S(1)}, u32[]{:S(2)}, u32[]{:S(2)}) async-start(bf16[4,128,192]{1,2,0:T(8,128)(2,1)} %copy_bitcast_fusion.3), calls=%async_computation | async-start | bytes 393216 | tf_op jit(solution)/shard_map/all_to_all | solution.py:30
  26.4 40.1 %reduce-scatter.37.cloned.1.call-start = ((), (), s32[]{:S(2)}) async-start(), calls=%async_computation.20 | async-start | bytes 327680
  46.4 54.5 %all-gather.7.cloned.1.call-start = ((), (), s32[]{:S(2)}) async-start(), calls=%async_computation.18 | async-start | bytes 1474560 | tf_op jit(solution)/shard_map/all_gather | solution.py:33
  47.4 237.4 %copy-start.50 = (f32[1,1,192]{2,1,0:T(1,128)}, f32[1,1,192]{2,1,0:T(1,128)S(1)}, u32[]{:S(2)}) copy-start(f32[1,1,192]{2,1,0:T(1,128)S(1)} %get-tuple-element.85) | copy-start | bytes 2308
  67.4 66.1 %copy-start.6 = (bf16[128,192]{0,1:T(8,128)(2,1)}, bf16[128,192]{0,1:T(8,128)(2,1)S(1)}, u32[]{:S(2)}) copy-start(bf16[128,192]{0,1:T(8,128)(2,1)S(1)} %copy.96) | copy-start | bytes 147460
  73.3 60.2 %copy-start.42 = (f32[128]{0:T(128)}, f32[128]{0:T(128)S(1)}, u32[]{:S(2)}) copy-start(f32[128]{0:T(128)S(1)} %broadcast_multiply_fusion.7) | copy-start | bytes 1540
  92.6 8.2 %all-to-all-start.1 = ((bf16[4,128,192]{1,2,0:T(8,128)(2,1)}), bf16[4,128,192]{1,2,0:T(8,128)(2,1)S(1)}, u32[]{:S(2)}, u32[]{:S(2)}) async-start(bf16[4,128,192]{1,2,0:T(8,128)(2,1)} %copy_bitcast_fusion.2), calls=%async_computation.1 | async-start | bytes 393216 | tf_op jit(solution)/shard_map/all_to_all | solution.py:30
  97.2 35.4 %reduce-scatter.39.cloned.1.call-start = ((), (), s32[]{:S(2)}) async-start(), calls=%async_computation.21 | async-start | bytes 327680
  139.6 60.8 %copy-start.44 = (f32[128]{0:T(128)}, f32[128]{0:T(128)S(1)}, u32[]{:S(2)}) copy-start(f32[128]{0:T(128)S(1)} %broadcast_multiply_fusion.6) | copy-start | bytes 1540
  158.8 14.3 %all-to-all-start.2 = ((bf16[4,128,192]{1,2,0:T(8,128)(2,1)}), bf16[4,128,192]{1,2,0:T(8,128)(2,1)S(1)}, u32[]{:S(2)}, u32[]{:S(2)}) async-start(bf16[4,128,192]{1,2,0:T(8,128)(2,1)} %copy_bitcast_fusion.1), calls=%async_computation.2 | async-start | bytes 393216 | tf_op jit(solution)/shard_map/all_to_all | solution.py:30
  163.3 36.1 %reduce-scatter.41.cloned.1.call-start = ((), (), s32[]{:S(2)}) async-start(), calls=%async_computation.22 | async-start | bytes 327680
  181.0 49.2 %all-gather.9.cloned.1.call-start = ((), (), s32[]{:S(2)}) async-start(), calls=%async_computation.19 | async-start | bytes 1474560 | tf_op jit(solution)/shard_map/all_gather | solution.py:33
  225.7 8.1 %all-to-all-start.3 = ((bf16[4,128,192]{1,2,0:T(8,128)(2,1)}), bf16[4,128,192]{1,2,0:T(8,128)(2,1)S(1)}, u32[]{:S(2)}, u32[]{:S(2)}) async-start(bf16[4,128,192]{1,2,0:T(8,128)(2,1)} %copy_bitcast_fusion), calls=%async_computation.3 | async-start | bytes 393216 | tf_op jit(solution)/shard_map/all_to_all | solution.py:30
  230.2 35.4 %reduce-scatter.43.cloned.1.call-start = ((), (), s32[]{:S(2)}) async-start(), calls=%async_computation.23 | async-start | bytes 327680
  247.2 72.3 %reduce-scatter.33.cloned.1.call-start = ((), (), s32[]{:S(2)}) async-start(), calls=%async_computation.16 | async-start | bytes 983040 | tf_op jit(solution)/shard_map/reduce_scatter | solution.py:81
  298.8 54.1 %reduce-scatter.45.cloned.1.call-start = ((), (), s32[]{:S(2)}) async-start(), calls=%async_computation.24 | async-start | bytes 327680
  332.2 62.6 %reduce-scatter.47.cloned.1.call-start = ((), (), s32[]{:S(2)}) async-start(), calls=%async_computation.25 | async-start | bytes 327680
  377.4 50.7 %reduce-scatter.49.cloned.1.call-start = ((), (), s32[]{:S(2)}) async-start(), calls=%async_computation.26 | async-start | bytes 327680
  407.3 66.8 %reduce-scatter.35.cloned.1.call-start = ((), (), s32[]{:S(2)}) async-start(), calls=%async_computation.17 | async-start | bytes 983040 | tf_op jit(solution)/shard_map/reduce_scatter | solution.py:81
  451.2 85.1 %copy-start.1 = (bf16[512,192]{0,1:T(8,128)(2,1)}, bf16[512,192]{0,1:T(8,128)(2,1)S(1)}, u32[]{:S(2)}) copy-start(bf16[512,192]{0,1:T(8,128)(2,1)S(1)} %all_gather.84) | copy-start | bytes 589828
  453.6 54.2 %reduce-scatter.51.cloned.1.call-start = ((), (), s32[]{:S(2)}) async-start(), calls=%async_computation.27 | async-start | bytes 327680
  487.0 64.9 %reduce-scatter.53.cloned.1.call-start = ((), (), s32[]{:S(2)}) async-start(), calls=%async_computation.28 | async-start | bytes 327680
  534.4 66.8 %reduce-scatter.55.cloned.1.call-start = ((), (), s32[]{:S(2)}) async-start(), calls=%async_computation.29 | async-start | bytes 327680
  564.4 79.9 %all-reduce.9.cloned.1.call-start = ((), (), s32[]{:S(2)}) async-start(), calls=%async_computation.30 | async-start | bytes 3538944 | tf_op jit(solution)/shard_map/psum | solution.py:263
  (78 other events, 1261.0 us)
Sparse Core Ops, SparseCore 0:
  46.5 19.8 reduce-scatter.36
  114.4 18.1 reduce-scatter.38
  181.1 18.3 reduce-scatter.40
  247.4 18.1 reduce-scatter.42
  332.3 20.5 reduce-scatter.44
  407.4 20.5 reduce-scatter.48
  487.1 20.5 reduce-scatter.50
  564.5 20.9 reduce-scatter.54
  589.3 54.9 all-reduce.8
Sparse Core Ops, SparseCore 1:
  49.1 16.3 all-gather.6
  183.7 14.8 all-gather.8
  298.9 20.6 reduce-scatter.32
  377.4 17.2 reduce-scatter.46
  453.6 20.4 reduce-scatter.34
  534.5 17.3 reduce-scatter.52
where the time goes:
time: 659 us; the launch traced here: 655 us
  blocking collectives  283 us (43%)
  waiting for transfers between devices  248 us (38%)
  matrix products  32.6 us (5%)
  local copies, waits for them, and re-layouts  30.6 us (5%)
  other arithmetic  25.9 us (4%)
  starting transfers between devices  17.9 us (3%)
  between operations  16.5 us (3%)
    unnamed x25, waiting for transfers between devices  161 us
    psum x12, blocking collectives, feature_total(): return lax.psum(members, 'col')  70.1 us
    all_gather x4, blocking collectives, back_out(): grad_all = lax.all_gather(grad_low, 'row', axis=0, tiled=True)  51 us
    all_gather x4, blocking collectives, spread_in(): gathered = lax.all_gather(operand, 'row', axis=0, tiled=True)  50.6 us
    psum x1, waiting for transfers between devices, per_device(): lax.psum(attn_w.astype(jnp.bfloat16), 'dp').astype(jnp.float32)  41.2 us
    reduce_scatter x2, waiting for transfers between devices, back_out(): lax.psum_scatter(partial_term(jnp.int32(0), lax.axis_size('col') * grad_l...  39.1 us
    all_gather x4, blocking collectives, back_in(): grad_all = lax.all_gather(grad_low, 'col', axis=0, tiled=True)  33.5 us
    all_gather x4, blocking collectives, spread_out(): gathered = lax.all_gather(operand, 'col', axis=0, tiled=True)  28.8 us
  transfers between devices with their start and end apart: 19, of which 14 were waited for; matrix products, arithmetic and copies ran while one was open for 4% of the time, Pallas kernels for 0%

commit v1 on v0

v1 whole, which is shorter than its diff:
```python
from functools import partial

import jax
import jax.numpy as jnp
from jax import lax
from jax.experimental import pallas as pl
from jax.experimental.pallas import tpu as pltpu
from jax.sharding import PartitionSpec as P


HEAD_DIM = 64
EPS = 1e-5
MASKED = -1e30
F32 = jnp.float32
BF16 = jnp.bfloat16


def exchange(x, axis, bit):
    n = lax.axis_size(axis)
    return lax.ppermute(x, axis, [(i, i ^ bit) for i in range(n)])


def turned(x, bit):
    n = lax.axis_size("row")
    pairs = [(a * n + b, (b ^ bit) * n + a) for a in range(n) for b in range(n)]
    return lax.ppermute(x, ("row", "col"), pairs)


def turned_back(x, bit):
    n = lax.axis_size("row")
    pairs = [(a * n + b, b * n + (a ^ bit)) for a in range(n) for b in range(n)]
    return lax.ppermute(x, ("row", "col"), pairs)


def gather_col(x):
    far = exchange(x, "col", 2)
    return [x, exchange(x, "col", 1), far, exchange(far, "col", 1)]


def gather_row(x):
    return [x] + [exchange(x, "row", k) for k in range(1, lax.axis_size("row"))]


def scatter_row(pieces):
    return [pieces[0]] + [exchange(pieces[k], "row", k) for k in range(1, len(pieces))]


def call(kernel, outs, *args, scalars=None):
    vmem = pl.BlockSpec(memory_space=pltpu.VMEM)
    specs = [vmem] * len(args)
    if scalars is not None:
        args = (scalars,) + args
        specs = [pl.BlockSpec(memory_space=pltpu.SMEM)] + specs
    read = sum(a.size * a.dtype.itemsize for a in args)
    wrote = sum(o.size * o.dtype.itemsize for o in outs)
    return pl.pallas_call(
        kernel,
        out_shape=outs,
        in_specs=specs,
        out_specs=[vmem] * len(outs),
        compiler_params=pltpu.CompilerParams(vmem_limit_bytes=40 * 1024 * 1024),
        cost_estimate=pl.CostEstimate(
            flops=200_000_000, bytes_accessed=read + wrote, transcendentals=0
        ),
    )(*args)


def sds(shape, dtype):
    return jax.ShapeDtypeStruct(shape, dtype)


def rows_of(refs):
    return jnp.concatenate([r[...] for r in refs], axis=0)


def lanes_of(refs):
    return jnp.concatenate([r[...] for r in refs], axis=1)


def dot(a, b):
    return jnp.dot(a, b, preferred_element_type=F32)


def dot_t(a, b):
    return lax.dot_general(a, b, (((1,), (1,)), ((), ())), preferred_element_type=F32)


def t_dot(a, b):
    return lax.dot_general(a, b, (((0,), (0,)), ((), ())), preferred_element_type=F32)


def prep_kernel(n, sc, *refs):
    pieces, outs, full = refs[:n], refs[n : 2 * n], refs[2 * n]
    row, col = sc[0], sc[1]
    width = pieces[0].shape[1]
    block = outs[0].shape[0]
    for k in range(n):
        for j in range(n):

            @pl.when((col ^ row ^ k) == j)
            def _():
                full[:, j * width : (j + 1) * width] = pieces[k][...].astype(F32)

    for k in range(n):
        outs[k][...] = full[pl.ds(pl.multiple_of((row ^ k) * block, block), block), :].astype(BF16)


def turn_in_kernel(n, sc, *refs):
    pieces, out = refs[:n], refs[n]
    row, col = sc[0], sc[1]
    width = pieces[0].shape[1]
    for k in range(n):
        for j in range(n):

            @pl.when((col ^ row ^ k) == j)
            def _():
                out[:, j * width : (j + 1) * width] = pieces[k][...].astype(F32)


def turn_out_kernel(n, sc, x, *outs):
    row, col = sc[0], sc[1]
    width = outs[0].shape[1]
    for k in range(n):
        for j in range(n):

            @pl.when((col ^ row ^ k) == j)
            def _():
                outs[k][...] = x[:, j * width : (j + 1) * width].astype(outs[k].dtype)


def sum_turn_out_kernel(n, sc, *refs):
    pieces, base, outs = refs[:n], refs[n], refs[n + 1 : 2 * n + 1]
    total = refs[2 * n + 1]
    total[...] = base[...] + tree(pieces)
    turn_out_kernel(n, sc, total, *outs)


def assemble_kernel(n, sc, *refs):
    pieces, out = refs[:n], refs[n]
    col = sc[1]
    block = pieces[0].shape[0]
    for k in range(n):
        out[pl.ds(pl.multiple_of((col ^ k) * block, block), block), :] = pieces[k][...]


def tree(pieces):
    values = [p[...].astype(F32) for p in pieces]
    while len(values) > 1:
        values = [values[i] + values[i + 1] for i in range(0, len(values), 2)]
    return values[0]


def attend_kernel(n, m, layer, sc, *refs):
    x_refs, w_refs = refs[:n], refs[n : n + m]
    bias = refs[n + m]
    outs = refs[n + m + 1 :]
    z_refs, (qkv_ref, p_ref, o_ref) = outs[:n], outs[n:]
    row, length = sc[0], sc[2]
    x = rows_of(x_refs)
    w = rows_of(w_refs)
    width = w.shape[1] // 4
    both = bias[layer].astype(F32)
    shift = jnp.concatenate([both[0:1], jnp.zeros((1, width), F32), both[1:2]], axis=1)
    qkv = (dot(x, w[:, : 3 * width]) + shift).astype(BF16)
    qkv_ref[...] = qkv
    tokens = x.shape[0]
    block = tokens // n
    key_at = lax.broadcasted_iota(jnp.int32, (tokens, tokens), 1)
    place = ((key_at // block) ^ row) * block + key_at % block
    visible = place < length
    mixed = []
    for h in range(width // HEAD_DIM):
        q = qkv[:, h * HEAD_DIM : (h + 1) * HEAD_DIM]
        k = qkv[:, width + h * HEAD_DIM : width + (h + 1) * HEAD_DIM]
        v = qkv[:, 2 * width + h * HEAD_DIM : 2 * width + (h + 1) * HEAD_DIM]
        s = jnp.where(visible, dot_t(q, k) * HEAD_DIM ** (-0.5), MASKED)
        e = jnp.exp(s - jnp.max(s, axis=-1, keepdims=True))
        p = e / jnp.sum(e, axis=-1, keepdims=True)
        p_ref[h] = p
        mixed.append(dot(p.astype(BF16), v))
    o = jnp.concatenate(mixed, axis=1).astype(BF16)
    o_ref[...] = o
    z = dot_t(o, w[:, 3 * width :])
    for k in range(n):
        z_refs[k][...] = z[k * block : (k + 1) * block].astype(z_refs[k].dtype)


def norm_kernel(n, at, *refs):
    pieces, base, bias, gain, shift = refs[:n], refs[n], refs[n + 1], refs[n + 2], refs[n + 3]
    out32, out16, unit, inverse = refs[n + 4 :]
    layer, which = at
    b = bias[layer : layer + 1, :].astype(F32)
    g = gain[2 * layer + which : 2 * layer + which + 1, :].astype(F32)
    c = shift[2 * layer + which : 2 * layer + which + 1, :].astype(F32)
    v = base[...].astype(F32) + (tree(pieces) + b)
    mean = jnp.mean(v, axis=-1, keepdims=True)
    centred = v - mean
    r = lax.rsqrt(jnp.mean(centred * centred, axis=-1, keepdims=True) + EPS)
    normed = centred * r
    y = normed * g + c
    out32[...] = y
    out16[...] = y.astype(BF16)
    unit[...] = normed
    inverse[...] = jnp.broadcast_to(r, inverse.shape)


def norm_back_kernel(n, at, *refs):
    pieces, base, unit, inverse, gain = refs[:n], refs[n], refs[n + 1], refs[n + 2], refs[n + 3]
    out32, out16, sums = refs[n + 4 :]
    layer, which = at
    g = gain[2 * layer + which : 2 * layer + which + 1, :].astype(F32)
    e = base[...]
    if n:
        e = e + tree(pieces)
    normed = unit[...]
    r = inverse[:, 0:1]
    c = e * g
    grad = r * (
        c
        - jnp.mean(c, axis=-1, keepdims=True)
        - normed * jnp.mean(c * normed, axis=-1, keepdims=True)
    )
    low = grad.astype(BF16)
    out32[...] = grad
    out16[...] = low
    sums[0:1, :] = jnp.sum(e * normed, axis=0, keepdims=True)
    sums[1:2, :] = jnp.sum(e, axis=0, keepdims=True)
    sums[2:3, :] = jnp.sum(low.astype(F32), axis=0, keepdims=True)
    sums[3:8, :] = jnp.zeros((5, sums.shape[1]), F32)


def feed_kernel(n, m, layer, *refs):
    h_refs, up_refs, down_refs = refs[:n], refs[n : n + m], refs[n + m : n + 2 * m]
    bias = refs[n + 2 * m]
    outs = refs[n + 2 * m + 1 :]
    f_refs, (g_ref, slope_ref) = outs[:n], outs[n:]
    u = dot(rows_of(h_refs), rows_of(up_refs)) + bias[layer : layer + 1, :].astype(F32)
    cdf = 0.5 * (1.0 + lax.erf(u * (0.5**0.5)))
    g = (u * cdf).astype(BF16)
    g_ref[...] = g
    slope_ref[...] = cdf + u * (jnp.exp(-0.5 * u * u) * 0.3989422804014327)
    f = dot_t(g, rows_of(down_refs))
    block = f_refs[0].shape[0]
    for k in range(n):
        f_refs[k][...] = f[k * block : (k + 1) * block].astype(f_refs[k].dtype)


def feed_back_kernel(n, m, *refs):
    d_refs, up_refs, down_refs = refs[:n], refs[n : n + m], refs[n + m : n + 2 * m]
    slope = refs[n + 2 * m]
    outs = refs[n + 2 * m + 1 :]
    h_refs, du_ref = outs[:n], outs[n]
    dg = dot(rows_of(d_refs), rows_of(down_refs))
    du = (dg * slope[...]).astype(BF16)
    du_ref[...] = du
    dh = dot_t(du, rows_of(up_refs))
    block = h_refs[0].shape[0]
    for k in range(n):
        h_refs[k][...] = dh[k * block : (k + 1) * block].astype(h_refs[k].dtype)


def split_blocks(grad, m, at, keep, send):
    block = grad.shape[0] // m
    half = m // 2
    for k in range(m):
        target = send if k % 2 else keep
        start = (at * half + k // 2) * block
        target[start : start + block, :] = grad[k * block : (k + 1) * block].astype(target.dtype)


def feed_weight_kernel(n, m, *refs):
    d_refs, h_refs, g, du = refs[:n], refs[n : 2 * n], refs[2 * n], refs[2 * n + 1]
    keep, send, sums = refs[2 * n + 2 :]
    split_blocks(t_dot(rows_of(d_refs), g[...]), m, 0, keep, send)
    split_blocks(t_dot(rows_of(h_refs), du[...]), m, 1, keep, send)
    sums[0:1, :] = jnp.sum(du[...].astype(F32), axis=0, keepdims=True)
    sums[1:8, :] = jnp.zeros((7, sums.shape[1]), F32)


def attend_back_kernel(n, m, *refs):
    d_refs, w_refs = refs[:n], refs[n : n + m]
    qkv_ref, p_ref = refs[n + m], refs[n + m + 1]
    outs = refs[n + m + 2 :]
    x_refs, grads = outs[:n], outs[n]
    w = rows_of(w_refs)
    width = w.shape[1] // 4
    do = dot(rows_of(d_refs), w[:, 3 * width :]).astype(BF16)
    qkv = qkv_ref[...]
    dq, dk, dv = [], [], []
    for h in range(width // HEAD_DIM):
        q = qkv[:, h * HEAD_DIM : (h + 1) * HEAD_DIM]
        k = qkv[:, width + h * HEAD_DIM : width + (h + 1) * HEAD_DIM]
        v = qkv[:, 2 * width + h * HEAD_DIM : 2 * width + (h + 1) * HEAD_DIM]
        d = do[:, h * HEAD_DIM : (h + 1) * HEAD_DIM]
        p = p_ref[h]
        dv.append(t_dot(p.astype(BF16), d))
        dp = dot_t(d, v)
        ds = (p * (dp - jnp.sum(p * dp, axis=-1, keepdims=True))).astype(BF16)
        dq.append(dot(ds, k) * HEAD_DIM ** (-0.5))
        dk.append(t_dot(ds, q) * HEAD_DIM ** (-0.5))
    low = jnp.concatenate(dq + dk + dv, axis=1).astype(BF16)
    grads[...] = low
    dx = dot_t(low, w[:, : 3 * width])
    block = x_refs[0].shape[0]
    for k in range(n):
        x_refs[k][...] = dx[k * block : (k + 1) * block].astype(x_refs[k].dtype)


def attend_weight_kernel(n, m, *refs):
    x_refs, d_refs, o, grads = refs[:n], refs[n : 2 * n], refs[2 * n], refs[2 * n + 1]
    keep, send, sums = refs[2 * n + 2 :]
    low = grads[...]
    first = t_dot(rows_of(x_refs), low)
    second = t_dot(rows_of(d_refs), o[...])
    split_blocks(jnp.concatenate([first, second], axis=1), m, 0, keep, send)
    sums[...] = jnp.zeros(sums.shape, F32)
    sums[0:1, 0 : low.shape[1]] = jnp.sum(low.astype(F32), axis=0, keepdims=True)


def reduce_dp(x):
    bit = 1
    while bit < lax.axis_size("dp"):
        x = x + exchange(x, "dp", bit)
        bit *= 2
    return x


def reduce_blocks(keep, send, parts):
    total = keep + exchange(send, "col", 1).astype(F32)
    block = keep.shape[0] // (2 * parts)
    total = total.reshape(parts, 2, block, keep.shape[1])
    mine = total[:, 0] + exchange(total[:, 1].astype(BF16), "col", 2).astype(F32)
    low = mine.astype(BF16)
    if lax.axis_size("dp") == 2:
        return low.astype(F32) + exchange(low, "dp", 1).astype(F32)
    return reduce_dp(low.astype(F32))


def per_device(
    hidden_in, lengths, w_attn, b_qv, b_out, ln_gain, ln_bias, w_up, b_up, w_down, b_down, cotangent
):
    layers = w_attn.shape[0]
    n, m = lax.axis_size("row"), lax.axis_size("col")
    row, col = lax.axis_index("row"), lax.axis_index("col")
    tokens, piece = hidden_in.shape
    block = tokens // n
    model = piece * m
    hidden = w_up.shape[2]
    length = lax.dynamic_index_in_dim(lengths, col, 0, keepdims=False)
    scalars = jnp.stack([row, col, length]).astype(jnp.int32)

    x_in = [turned(hidden_in, k) for k in range(n)]
    attn = [gather_col(w_attn[0])]
    rows = jnp.concatenate(
        [
            b_out,
            b_down,
            ln_gain.reshape(2 * layers, piece),
            ln_bias.reshape(2 * layers, piece),
        ]
    )
    rows = jnp.concatenate(gather_col(rows), axis=1)
    b_out_all, b_down_all = rows[:layers], rows[layers : 2 * layers]
    gains, shifts = rows[2 * layers : 4 * layers], rows[4 * layers :]
    ups, downs = [], []
    for layer in range(layers):
        if layer:
            attn.append(gather_col(w_attn[layer]))
        ups.append(gather_col(w_up[layer]))
        downs.append(gather_col(w_down[layer]))
    ct_in = [
        turned(lax.dynamic_slice_in_dim(cotangent, (col ^ k) * block, block, 0), k)
        for k in range(n)
    ]

    low_block = sds((block, model), BF16)
    full_block = sds((block, model), F32)
    pieces_out = [full_block] + [low_block] * (n - 1)
    inverse_out = sds((block, 128), F32)
    norm_out = [full_block, low_block, full_block, inverse_out]

    *x_low, _ = call(
        partial(prep_kernel, n),
        [low_block] * n + [sds((tokens, model), F32)],
        *x_in,
        scalars=scalars,
    )
    base = x_low[0]
    saved = []
    for layer in range(layers):
        *z, qkv, probs, mixed = call(
            partial(attend_kernel, n, m, layer),
            pieces_out
            + [
                sds((tokens, 3 * piece), BF16),
                sds((piece // HEAD_DIM, tokens, tokens), F32),
                sds((tokens, piece), BF16),
            ],
            *x_low,
            *attn[layer],
            b_qv,
            scalars=scalars,
        )
        z = scatter_row(z)
        h32, h16, unit_one, inverse_one = call(
            partial(norm_kernel, n, (layer, 0)), norm_out, *z, base, b_out_all, gains, shifts
        )
        h_low = gather_row(h16)
        *f, active, slope = call(
            partial(feed_kernel, n, m, layer),
            pieces_out + [sds((tokens, hidden), BF16), sds((tokens, hidden), F32)],
            *h_low,
            *ups[layer],
            *downs[layer],
            b_up,
        )
        f = scatter_row(f)
        base, low, unit_two, inverse_two = call(
            partial(norm_kernel, n, (layer, 1)), norm_out, *f, h32, b_down_all, gains, shifts
        )
        saved.append(
            (x_low, qkv, probs, mixed, unit_one, inverse_one, h_low, active, slope, unit_two, inverse_two)
        )
        if layer + 1 < layers:
            x_low = gather_row(low)

    outs = call(
        partial(turn_out_kernel, n), [sds((block, piece), BF16)] * n, base, scalars=scalars
    )
    (out_hidden,) = call(
        partial(assemble_kernel, n),
        [sds((tokens, piece), BF16)],
        *[turned_back(o, k) for k, o in enumerate(outs)],
        scalars=scalars,
    )

    (flow,) = call(partial(turn_in_kernel, n), [full_block], *ct_in, scalars=scalars)
    sums_out = sds((8, model), F32)
    back_out = [full_block, low_block, sums_out]
    flow_pieces = []
    norm_sums, up_sums, qv_sums = [None] * layers, [None] * layers, [None] * layers
    attn_grads, up_grads, down_grads = [None] * layers, [None] * layers, [None] * layers
    for layer in reversed(range(layers)):
        x_low, qkv, probs, mixed, unit_one, inverse_one, h_low, active, slope, unit_two, inverse_two = (
            saved[layer]
        )
        df, df_low, sums_two = call(
            partial(norm_back_kernel, len(flow_pieces), (layer, 1)),
            back_out,
            *flow_pieces,
            flow,
            unit_two,
            inverse_two,
            gains,
        )
        df_all = gather_row(df_low)
        *dh, du = call(
            partial(feed_back_kernel, n, m),
            pieces_out + [sds((tokens, hidden), BF16)],
            *df_all,
            *ups[layer],
            *downs[layer],
            slope,
        )
        dh = scatter_row(dh)
        keep, send, up_sums[layer] = call(
            partial(feed_weight_kernel, n, m),
            [sds((model, hidden), F32), sds((model, hidden), BF16), sds((8, hidden), F32)],
            *df_all,
            *h_low,
            active,
            du,
        )
        both = reduce_blocks(keep, send, 2)
        down_grads[layer], up_grads[layer] = both[0], both[1]
        da, da_low, sums_one = call(
            partial(norm_back_kernel, n, (layer, 0)),
            back_out,
            *dh,
            df,
            unit_one,
            inverse_one,
            gains,
        )
        norm_sums[layer] = (sums_one, sums_two)
        da_all = gather_row(da_low)
        *dx, grads = call(
            partial(attend_back_kernel, n, m),
            pieces_out + [sds((tokens, 3 * piece), BF16)],
            *da_all,
            *attn[layer],
            qkv,
            probs,
        )
        flow_pieces = scatter_row(dx)
        flow = da
        keep, send, qv_sums[layer] = call(
            partial(attend_weight_kernel, n, m),
            [
                sds((model // 2, 4 * piece), F32),
                sds((model // 2, 4 * piece), BF16),
                sds((8, model), F32),
            ],
            *x_low,
            *da_all,
            mixed,
            grads,
        )
        attn_grads[layer] = reduce_blocks(keep, send, 1)[0]

    *outs, _ = call(
        partial(sum_turn_out_kernel, n),
        [sds((block, piece), F32)] * n + [full_block],
        *flow_pieces,
        flow,
        scalars=scalars,
    )
    (grad_input,) = call(
        partial(assemble_kernel, n),
        [sds((tokens, piece), F32)],
        *[turned_back(o, k) for k, o in enumerate(outs)],
        scalars=scalars,
    )

    sums = jnp.concatenate([s[:3] for pair in norm_sums for s in pair])
    others = [exchange(sums, "row", k) for k in range(1, n)]
    sums = (sums + others[0]) + (others[1] + others[2])
    sums = sums.reshape(sums.shape[0], m, piece)
    sums = sums[:, 0::2] + exchange(sums[:, 1::2], "col", 1)
    sums = sums[:, 0] + exchange(sums[:, 1], "col", 2)
    sums = reduce_dp(sums).reshape(layers, 2, 3, piece)
    wide = jnp.concatenate([s[0:1] for s in up_sums] + [s[0:1] for s in qv_sums])
    wide = wide + exchange(wide, "col", 1)
    wide = wide + exchange(wide, "col", 2)
    wide = reduce_dp(wide)
    qv = wide[layers:, : 3 * piece].reshape(layers, 3, piece)
    return (
        out_hidden,
        grad_input,
        jnp.stack(attn_grads),
        qv[:, 0::2],
        sums[:, 0, 2],
        sums[:, :, 0],
        sums[:, :, 1],
        jnp.stack(up_grads),
        wide[:layers],
        jnp.stack(down_grads),
        sums[:, 1, 2],
    )


def solution(mesh):
    in_specs = (
        P(("dp", "row"), "col"),
        P("dp"),
        P(None, "col", "row"),
        P(None, None, "row"),
        P(None, "col"),
        P(None, None, "col"),
        P(None, None, "col"),
        P(None, "col", "row"),
        P(None, "row"),
        P(None, "col", "row"),
        P(None, "col"),
        P(("dp", "row"), "col"),
    )
    out_specs = (
        P(("dp", "row"), "col"),
        P(("dp", "row"), "col"),
        P(None, "col", "row"),
        P(None, None, "row"),
        P(None, "col"),
        P(None, None, "col"),
        P(None, None, "col"),
        P(None, "col", "row"),
        P(None, "row"),
        P(None, "col", "row"),
        P(None, "col"),
    )
    return jax.shard_map(
        per_device, mesh=mesh, in_specs=in_specs, out_specs=out_specs, check_vma=False
    )
```

time: 659 us -> 337 us (0.51)
  blocking collectives: 283 us -> 0 us
  waiting for transfers between devices: 248 us -> 136 us
  starting transfers between devices: 17.9 us -> 111 us
  matrix products: 32.6 us -> 0 us
  Pallas kernels: 0 us -> 28.9 us
  between operations: 16.5 us -> 2.52 us
  other arithmetic: 25.9 us -> 14 us
  local copies, waits for them, and re-layouts: 30.6 us -> 40.4 us
    all_gather x18 -> x0, blocking collectives: 183 us -> none  [the longest x4 51 us: back_out(): grad_all = lax.all_gather(grad_low, 'row', axis=0, tiled=True)]
    unnamed x25 -> x0, waiting for transfers between devices: 161 us -> none
    ppermute x0 -> x103, waiting for transfers between devices: none -> 136 us  [the longest x87 130 us: exchange(): return lax.ppermute(x, axis, [(i, i ^ bit) for i in range(n)])]
    ppermute x0 -> x103, starting transfers between devices: none -> 111 us  [the longest x87 80.2 us: exchange(): return lax.ppermute(x, axis, [(i, i ^ bit) for i in range(n)])]
    psum x14 -> x0, blocking collectives: 100 us -> none  [the longest x12 70.1 us: feature_total(): return lax.psum(members, 'col')]
    psum x1 -> x0, waiting for transfers between devices: 41.2 us -> none  [per_device(): lax.psum(attn_w.astype(jnp.bfloat16), 'dp').astype(jnp.float32)]
    reduce_scatter x2 -> x0, waiting for transfers between devices: 39.1 us -> none  [back_out(): lax.psum_scatter(partial_term(jnp.int32(0), lax.axis_size('col') * grad_l...]
    dot_general x36 -> x0, matrix products: 32.6 us -> none  [the longest x8 10.8 us: inner_rows(): lax.dot_general(left_side, right_side, (((0,), (0,)), ((), ())), preferre...]
  transfers between devices with their start and end apart: 19 -> 103, of which waited for: 14 -> 43; matrix products, arithmetic and copies ran while one was open for 4% -> 8% of each run, Pallas kernels for 0% -> 6%
where the time goes in v1:
time: 337 us; the launch traced here: 333 us
  waiting for transfers between devices  136 us (40%)
  starting transfers between devices  111 us (33%)
  local copies, waits for them, and re-layouts  40.4 us (12%)
  Pallas kernels  28.9 us (9%)
  other arithmetic  14 us (4%)
    ppermute x87, waiting for transfers between devices, exchange(): return lax.ppermute(x, axis, [(i, i ^ bit) for i in range(n)])  130 us
    ppermute x87, starting transfers between devices, exchange(): return lax.ppermute(x, axis, [(i, i ^ bit) for i in range(n)])  80.2 us
    unnamed x310, local copies, waits for them, and re-layouts  33.4 us
    pallas_call x26, Pallas kernels, call(): pl.pallas_call(kernel, out_shape=outs, in_specs=specs, out_specs=[vmem] *...  28.9 us
    ppermute x8, starting transfers between devices, turned(): return lax.ppermute(x, ('row', 'col'), pairs)  18.2 us
    ppermute x8, starting transfers between devices, turned_back(): return lax.ppermute(x, ('row', 'col'), pairs)  12.7 us
  transfers between devices with their start and end apart: 103, of which 43 were waited for; matrix products, arithmetic and copies ran while one was open for 8% of the time, Pallas kernels for 6%

profile of v1, /device:TPU:2, one launch (start us, length us, event | category | flops | bytes accessed | tf_op | source)
XLA Modules:
  0.0 333.4 jit_solution(17089023643775836008)
XLA Ops:
  2.7 3.1 collective-permute-start.3
  11.3 5.9 %collective-permute-start = (bf16[128,192]{1,0:T(8,128)(2,1)}, bf16[128,192]{1,0:T(8,128)(2,1)S(1)}, u32[]{:S(2)}, u32[]{:S(2)}) collective-permute-start(bf16[128,192]{1,0:T(8,128)(2,1)} %copy.38), channel_id=1, source_target_pairs={{0,0},{1,4},{2,8},{3,12},{4,1},{5,5},{6,9},{7,13},{8,2},{9,6},{10,... | collective-permute-start | bytes 147464 | tf_op jit(solution)/shard_map/ppermute | solution.py:26
  26.4 7.5 %collective-permute-done.11 = bf16[12,192]{1,0:T(8,128)(2,1)S(1)} collective-permute-done((bf16[12,192]{1,0:T(8,128)(2,1)S(1)}, bf16[12,192]{1,0:T(8,128)(2,1)S(1)}, u32[]{:S(2)}, u32[]{:S(2)}) %collective-permute-start.11) | collective-permute-done | bytes 4640 | tf_op jit(solution)/shard_map/ppermute | solution.py:20
  38.1 3.3 collective-permute-done.8.refs_2_
  54.0 4.1 %collective-permute-done.13.refs_1_.refs_5_ = bf16[32,768]{1,0:T(8,128)(2,1)S(1)} collective-permute-done((bf16[32,768]{1,0:T(8,128)(2,1)S(1)}, bf16[32,768]{1,0:T(8,128)(2,1)S(1)}, u32[]{:S(2)}, u32[]{:S(2)}) %collective-permute-start.13) | collective-permute-done | bytes 49184 | tf_op jit(solution)/shard_map/ppermute | solution.py:20
  59.0 4.1 %collective-permute-done.22.refs_1_ = bf16[32,768]{1,0:T(8,128)(2,1)S(1)} collective-permute-done((bf16[32,768]{1,0:T(8,128)(2,1)S(1)}, bf16[32,768]{1,0:T(8,128)(2,1)S(1)}, u32[]{:S(2)}, u32[]{:S(2)}) %collective-permute-start.22) | collective-permute-done | bytes 49184 | tf_op jit(solution)/shard_map/ppermute | solution.py:20
  63.3 5.1 %collective-permute-done.23.refs_2_ = bf16[32,768]{1,0:T(8,128)(2,1)S(1)} collective-permute-done((bf16[32,768]{1,0:T(8,128)(2,1)S(1)}, bf16[32,768]{1,0:T(8,128)(2,1)S(1)}, u32[]{:S(2)}, u32[]{:S(2)}) %collective-permute-start.23) | collective-permute-done | bytes 49184 | tf_op jit(solution)/shard_map/ppermute | solution.py:20
  70.2 4.1 %collective-permute-done.24.refs_3_ = bf16[32,768]{1,0:T(8,128)(2,1)S(1)} collective-permute-done((bf16[32,768]{1,0:T(8,128)(2,1)S(1)}, bf16[32,768]{1,0:T(8,128)(2,1)S(1)}, u32[]{:S(2)}, u32[]{:S(2)}) %collective-permute-start.24) | collective-permute-done | bytes 49184 | tf_op jit(solution)/shard_map/ppermute | solution.py:20
  77.1 3.9 %collective-permute-done.27.refs_3_ = bf16[32,768]{1,0:T(8,128)(2,1)S(1)} collective-permute-done((bf16[32,768]{1,0:T(8,128)(2,1)S(1)}, bf16[32,768]{1,0:T(8,128)(2,1)S(1)}, u32[]{:S(2)}, u32[]{:S(2)}) %collective-permute-start.27) | collective-permute-done | bytes 49184 | tf_op jit(solution)/shard_map/ppermute | solution.py:20
  82.5 4.1 %collective-permute-done.25.refs_1_ = bf16[32,768]{1,0:T(8,128)(2,1)S(1)} collective-permute-done((bf16[32,768]{1,0:T(8,128)(2,1)S(1)}, bf16[32,768]{1,0:T(8,128)(2,1)S(1)}, u32[]{:S(2)}, u32[]{:S(2)}) %collective-permute-start.25) | collective-permute-done | bytes 49184 | tf_op jit(solution)/shard_map/ppermute | solution.py:20
  88.4 4.1 %collective-permute-done.31.refs_1_ = bf16[32,768]{1,0:T(8,128)(2,1)S(1)} collective-permute-done((bf16[32,768]{1,0:T(8,128)(2,1)S(1)}, bf16[32,768]{1,0:T(8,128)(2,1)S(1)}, u32[]{:S(2)}, u32[]{:S(2)}) %collective-permute-start.31) | collective-permute-done | bytes 49184 | tf_op jit(solution)/shard_map/ppermute | solution.py:20
  92.8 5.1 %collective-permute-done.32.refs_2_ = bf16[32,768]{1,0:T(8,128)(2,1)S(1)} collective-permute-done((bf16[32,768]{1,0:T(8,128)(2,1)S(1)}, bf16[32,768]{1,0:T(8,128)(2,1)S(1)}, u32[]{:S(2)}, u32[]{:S(2)}) %collective-permute-start.32) | collective-permute-done | bytes 49184 | tf_op jit(solution)/shard_map/ppermute | solution.py:20
  99.7 4.3 %collective-permute-done.33.refs_3_ = bf16[32,768]{1,0:T(8,128)(2,1)S(1)} collective-permute-done((bf16[32,768]{1,0:T(8,128)(2,1)S(1)}, bf16[32,768]{1,0:T(8,128)(2,1)S(1)}, u32[]{:S(2)}, u32[]{:S(2)}) %collective-permute-start.33) | collective-permute-done | bytes 49184 | tf_op jit(solution)/shard_map/ppermute | solution.py:20
  128.4 4.2 %collective-permute-start.50 = (bf16[32,192]{1,0:T(8,128)(2,1)}, bf16[32,192]{1,0:T(8,128)(2,1)}, u32[]{:S(2)}, u32[]{:S(2)}) collective-permute-start(bf16[32,192]{1,0:T(8,128)(2,1)} %copy.58), channel_id=1, source_target_pairs={{0,0},{1,4},{2,8},{3,12},{4,1},{5,5},{6,9},{7,13},{8,2},{9,6},{10,... | collective-permute-start | bytes 36872 | tf_op jit(solution)/shard_map/ppermute | solution.py:26
  149.7 3.4 %collective-permute-start.56 = (bf16[32,768]{1,0:T(8,128)(2,1)S(1)}, bf16[32,768]{1,0:T(8,128)(2,1)S(1)}, u32[]{:S(2)}, u32[]{:S(2)}) collective-permute-start(bf16[32,768]{1,0:T(8,128)(2,1)S(1)} %get-tuple-element.141.refs_0_), channel_id=1, source_target_pairs={{0,12},{4,8},{8,4},{12,0},{1,13},{5,9},{9,5},{13,1},{2,14},{6,10},... | collective-permute-start | bytes 147464 | tf_op jit(solution)/shard_map/ppermute | solution.py:20
  166.1 3.0 collective-permute-done.59.refs_3_
  182.4 3.1 collective-permute-done.64.refs_2_
  196.9 3.4 %collective-permute-start.49 = (bf16[32,192]{1,0:T(8,128)(2,1)S(1)}, bf16[32,192]{1,0:T(8,128)(2,1)S(1)}, u32[]{:S(2)}, u32[]{:S(2)}) collective-permute-start(bf16[32,192]{1,0:T(8,128)(2,1)S(1)} %get-tuple-element.138), channel_id=1, source_target_pairs={{0,3},{1,7},{2,11},{3,15},{4,2},{5,6},{6,10},{7,14},{8,1},{9,5},{1... | collective-permute-start | bytes 36872 | tf_op jit(solution)/shard_map/ppermute | solution.py:32
  243.7 3.7 %collective-permute-done.95 = f32[12,192]{1,0:T(8,128)S(1)} collective-permute-done((f32[12,192]{1,0:T(8,128)S(1)}, f32[12,192]{1,0:T(8,128)S(1)}, u32[]{:S(2)}, u32[]{:S(2)}) %collective-permute-start.95) | collective-permute-done | bytes 9248 | tf_op jit(solution)/shard_map/ppermute | solution.py:20
  247.4 3.6 %collective-permute-done.89 = f32[4,768]{1,0:T(4,128)S(1)} collective-permute-done((f32[4,768]{1,0:T(4,128)S(1)}, f32[4,768]{1,0:T(4,128)S(1)}, u32[]{:S(2)}, u32[]{:S(2)}) %collective-permute-start.89) | collective-permute-done | bytes 12320 | tf_op jit(solution)/shard_map/ppermute | solution.py:20
  280.8 3.6 %collective-permute-done.83 = bf16[1,192,768]{2,1,0:T(8,128)(2,1)S(1)} collective-permute-done((bf16[1,192,768]{2,1,0:T(8,128)(2,1)S(1)}, bf16[1,192,768]{2,1,0:T(8,128)(2,1)S(1)}, u32[]{:S(2)}, u32[]{:S(2)}) %collective-permute-start.83) | collective-permute-done | bytes 294944 | tf_op jit(solution)/shard_map/ppermute | solution.py:20
  291.9 12.2 %collective-permute-done.101 = bf16[2,192,768]{2,1,0:T(8,128)(2,1)S(1)} collective-permute-done((bf16[2,192,768]{2,1,0:T(8,128)(2,1)S(1)}, bf16[2,192,768]{2,1,0:T(8,128)(2,1)S(1)}, u32[]{:S(2)}, u32[]{:S(2)}) %collective-permute-start.101) | collective-permute-done | bytes 589856 | tf_op jit(solution)/shard_map/ppermute | solution.py:20
  305.9 10.5 %collective-permute-done.98 = bf16[2,192,768]{2,1,0:T(8,128)(2,1)S(1)} collective-permute-done((bf16[2,192,768]{2,1,0:T(8,128)(2,1)S(1)}, bf16[2,192,768]{2,1,0:T(8,128)(2,1)S(1)}, u32[]{:S(2)}, u32[]{:S(2)}) %collective-permute-start.98) | collective-permute-done | bytes 589856 | tf_op jit(solution)/shard_map/ppermute | solution.py:20
  319.5 12.1 %collective-permute-done.99 = bf16[2,192,768]{2,1,0:T(8,128)(2,1)S(1)} collective-permute-done((bf16[2,192,768]{2,1,0:T(8,128)(2,1)S(1)}, bf16[2,192,768]{2,1,0:T(8,128)(2,1)S(1)}, u32[]{:S(2)}, u32[]{:S(2)}) %collective-permute-start.99) | collective-permute-done | bytes 589856 | tf_op jit(solution)/shard_map/ppermute | solution.py:20
  (577 shorter events, 209.5 us)
Async XLA Ops:
  17.2 20.0 %collective-permute-start.17 = (bf16[192,768]{1,0:T(8,128)(2,1)S(1)}, bf16[192,768]{1,0:T(8,128)(2,1)S(1)}, u32[]{:S(2)}, u32[]{:S(2)}) collective-permute-start(bf16[192,768]{1,0:T(8,128)(2,1)S(1)} %get-tuple-element.234.refs_4_), channel_id=1, source_target_pairs={{0,2},{1,3},{2,0},{3,1},{4,6},{5,7},{6,4},{7,5},{8,10},{9,11},{10,... | collective-permute-start | bytes 884744 | tf_op jit(solution)/shard_map/ppermute | solution.py:20
  17.3 20.3 %collective-permute-start.20 = (bf16[192,768]{1,0:T(8,128)(2,1)S(1)}, bf16[192,768]{1,0:T(8,128)(2,1)S(1)}, u32[]{:S(2)}, u32[]{:S(2)}) collective-permute-start(bf16[192,768]{1,0:T(8,128)(2,1)S(1)} %get-tuple-element.232.refs_8_), channel_id=1, source_target_pairs={{0,2},{1,3},{2,0},{3,1},{4,6},{5,7},{6,4},{7,5},{8,10},{9,11},{10,... | collective-permute-start | bytes 884744 | tf_op jit(solution)/shard_map/ppermute | solution.py:20
  47.7 28.6 %collective-permute-start.28 = (bf16[192,768]{1,0:T(8,128)(2,1)S(1)}, bf16[192,768]{1,0:T(8,128)(2,1)S(1)}, u32[]{:S(2)}, u32[]{:S(2)}) collective-permute-start(bf16[192,768]{1,0:T(8,128)(2,1)S(1)} %get-tuple-element.235.refs_4_), channel_id=1, source_target_pairs={{0,1},{1,0},{2,3},{3,2},{4,5},{5,4},{6,7},{7,6},{8,9},{9,8},{10,11... | collective-permute-start | bytes 884744 | tf_op jit(solution)/shard_map/ppermute | solution.py:20
  47.8 28.6 %collective-permute-start.38 = (bf16[192,768]{1,0:T(8,128)(2,1)S(1)}, bf16[192,768]{1,0:T(8,128)(2,1)}, u32[]{:S(2)}, u32[]{:S(2)}) collective-permute-start(bf16[192,768]{1,0:T(8,128)(2,1)S(1)} %get-tuple-element.233.refs_4_), channel_id=1, source_target_pairs={{0,2},{1,3},{2,0},{3,1},{4,6},{5,7},{6,4},{7,5},{8,10},{9,11},{10,... | collective-permute-start | bytes 884744 | tf_op jit(solution)/shard_map/ppermute | solution.py:20
  48.2 28.7 %collective-permute-start.41 = (bf16[192,768]{1,0:T(8,128)(2,1)S(1)}, bf16[192,768]{1,0:T(8,128)(2,1)}, u32[]{:S(2)}, u32[]{:S(2)}) collective-permute-start(bf16[192,768]{1,0:T(8,128)(2,1)S(1)} %get-tuple-element.231.refs_8_), channel_id=1, source_target_pairs={{0,2},{1,3},{2,0},{3,1},{4,6},{5,7},{6,4},{7,5},{8,10},{9,11},{10,... | collective-permute-start | bytes 884744 | tf_op jit(solution)/shard_map/ppermute | solution.py:20
  52.5 24.4 %collective-permute-start.30 = (bf16[192,768]{1,0:T(8,128)(2,1)S(1)}, bf16[192,768]{1,0:T(8,128)(2,1)S(1)}, u32[]{:S(2)}, u32[]{:S(2)}) collective-permute-start(bf16[192,768]{1,0:T(8,128)(2,1)S(1)} %collective-permute-done.29.refs_6_), channel_id=1, source_target_pairs={{0,1},{1,0},{2,3},{3,2},{4,5},{5,4},{6,7},{7,6},{8,9},{9,8},{10,11... | collective-permute-start | bytes 884744 | tf_op jit(solution)/shard_map/ppermute | solution.py:20
  76.4 32.0 %collective-permute-start.37 = (bf16[192,768]{1,0:T(8,128)(2,1)S(1)}, bf16[192,768]{1,0:T(8,128)(2,1)S(1)}, u32[]{:S(2)}, u32[]{:S(2)}) collective-permute-start(bf16[192,768]{1,0:T(8,128)(2,1)S(1)} %get-tuple-element.233.refs_4_), channel_id=1, source_target_pairs={{0,1},{1,0},{2,3},{3,2},{4,5},{5,4},{6,7},{7,6},{8,9},{9,8},{10,11... | collective-permute-start | bytes 884744 | tf_op jit(solution)/shard_map/ppermute | solution.py:20
  76.4 32.7 %collective-permute-start.40 = (bf16[192,768]{1,0:T(8,128)(2,1)S(1)}, bf16[192,768]{1,0:T(8,128)(2,1)S(1)}, u32[]{:S(2)}, u32[]{:S(2)}) collective-permute-start(bf16[192,768]{1,0:T(8,128)(2,1)S(1)} %get-tuple-element.231.refs_8_), channel_id=1, source_target_pairs={{0,1},{1,0},{2,3},{3,2},{4,5},{5,4},{6,7},{7,6},{8,9},{9,8},{10,11... | collective-permute-start | bytes 884744 | tf_op jit(solution)/shard_map/ppermute | solution.py:20
  76.9 35.7 %collective-permute-start.39 = (bf16[192,768]{1,0:T(8,128)(2,1)}, bf16[192,768]{1,0:T(8,128)(2,1)}, u32[]{:S(2)}, u32[]{:S(2)}) collective-permute-start(bf16[192,768]{1,0:T(8,128)(2,1)} %collective-permute-done.38.refs_6_), channel_id=1, source_target_pairs={{0,1},{1,0},{2,3},{3,2},{4,5},{5,4},{6,7},{7,6},{8,9},{9,8},{10,11... | collective-permute-start | bytes 884744 | tf_op jit(solution)/shard_map/ppermute | solution.py:20
  81.0 31.6 %collective-permute-start.42 = (bf16[192,768]{1,0:T(8,128)(2,1)}, bf16[192,768]{1,0:T(8,128)(2,1)}, u32[]{:S(2)}, u32[]{:S(2)}) collective-permute-start(bf16[192,768]{1,0:T(8,128)(2,1)} %collective-permute-done.41.refs_10_), channel_id=1, source_target_pairs={{0,1},{1,0},{2,3},{3,2},{4,5},{5,4},{6,7},{7,6},{8,9},{9,8},{10,11... | collective-permute-start | bytes 884744 | tf_op jit(solution)/shard_map/ppermute | solution.py:20
  121.7 23.7 %collective-permute-start.43 = (bf16[32,768]{1,0:T(8,128)(2,1)}, bf16[32,768]{1,0:T(8,128)(2,1)}, u32[]{:S(2)}, u32[]{:S(2)}) collective-permute-start(bf16[32,768]{1,0:T(8,128)(2,1)} %get-tuple-element.130), channel_id=1, source_target_pairs={{0,4},{4,0},{8,12},{12,8},{1,5},{5,1},{9,13},{13,9},{2,6},{6,2},{1... | collective-permute-start | bytes 147464 | tf_op jit(solution)/shard_map/ppermute | solution.py:20
  123.7 21.7 %collective-permute-start.44 = (bf16[32,768]{1,0:T(8,128)(2,1)}, bf16[32,768]{1,0:T(8,128)(2,1)}, u32[]{:S(2)}, u32[]{:S(2)}) collective-permute-start(bf16[32,768]{1,0:T(8,128)(2,1)} %get-tuple-element.131), channel_id=1, source_target_pairs={{0,8},{4,12},{8,0},{12,4},{1,9},{5,13},{9,1},{13,5},{2,10},{6,14},... | collective-permute-start | bytes 147464 | tf_op jit(solution)/shard_map/ppermute | solution.py:20
  124.3 21.1 %collective-permute-start.45 = (bf16[32,768]{1,0:T(8,128)(2,1)}, bf16[32,768]{1,0:T(8,128)(2,1)}, u32[]{:S(2)}, u32[]{:S(2)}) collective-permute-start(bf16[32,768]{1,0:T(8,128)(2,1)} %get-tuple-element.132), channel_id=1, source_target_pairs={{0,12},{4,8},{8,4},{12,0},{1,13},{5,9},{9,5},{13,1},{2,14},{6,10},... | collective-permute-start | bytes 147464 | tf_op jit(solution)/shard_map/ppermute | solution.py:20
  222.0 40.6 %collective-permute-start.85 = (bf16[384,768]{1,0:T(8,128)(2,1)}, bf16[384,768]{1,0:T(8,128)(2,1)}, u32[]{:S(2)}, u32[]{:S(2)}) collective-permute-start(bf16[384,768]{1,0:T(8,128)(2,1)} %get-tuple-element.188), channel_id=1, source_target_pairs={{0,1},{1,0},{2,3},{3,2},{4,5},{5,4},{6,7},{7,6},{8,9},{9,8},{10,11... | collective-permute-start | bytes 1769480 | tf_op jit(solution)/shard_map/ppermute | solution.py:20
  236.4 19.0 %collective-permute-start.75 = (bf16[32,768]{1,0:T(8,128)(2,1)}, bf16[32,768]{1,0:T(8,128)(2,1)S(1)}, u32[]{:S(2)}, u32[]{:S(2)}) collective-permute-start(bf16[32,768]{1,0:T(8,128)(2,1)} %get-tuple-element.173), channel_id=1, source_target_pairs={{0,4},{4,0},{8,12},{12,8},{1,5},{5,1},{9,13},{13,9},{2,6},{6,2},{1... | collective-permute-start | bytes 147464 | tf_op jit(solution)/shard_map/ppermute | solution.py:20
  236.9 19.1 %collective-permute-start.76 = (bf16[32,768]{1,0:T(8,128)(2,1)}, bf16[32,768]{1,0:T(8,128)(2,1)S(1)}, u32[]{:S(2)}, u32[]{:S(2)}) collective-permute-start(bf16[32,768]{1,0:T(8,128)(2,1)} %get-tuple-element.174), channel_id=1, source_target_pairs={{0,8},{4,12},{8,0},{12,4},{1,9},{5,13},{9,1},{13,5},{2,10},{6,14},... | collective-permute-start | bytes 147464 | tf_op jit(solution)/shard_map/ppermute | solution.py:20
  238.5 19.0 %collective-permute-start.77 = (bf16[32,768]{1,0:T(8,128)(2,1)}, bf16[32,768]{1,0:T(8,128)(2,1)S(1)}, u32[]{:S(2)}, u32[]{:S(2)}) collective-permute-start(bf16[32,768]{1,0:T(8,128)(2,1)} %get-tuple-element.175), channel_id=1, source_target_pairs={{0,12},{4,8},{8,4},{12,0},{1,13},{5,9},{9,5},{13,1},{2,14},{6,10},... | collective-permute-start | bytes 147464 | tf_op jit(solution)/shard_map/ppermute | solution.py:20
  255.4 30.6 %collective-permute-start.100 = (bf16[768,768]{1,0:T(8,128)(2,1)}, bf16[768,768]{1,0:T(8,128)(2,1)}, u32[]{:S(2)}, u32[]{:S(2)}) collective-permute-start(bf16[768,768]{1,0:T(8,128)(2,1)} %copy-done.104), channel_id=1, source_target_pairs={{0,1},{1,0},{2,3},{3,2},{4,5},{5,4},{6,7},{7,6},{8,9},{9,8},{10,11... | collective-permute-start | bytes 3538952 | tf_op jit(solution)/shard_map/ppermute | solution.py:20
  270.5 17.6 %collective-permute-start.97 = (bf16[768,768]{1,0:T(8,128)(2,1)S(1)}, bf16[768,768]{1,0:T(8,128)(2,1)}, u32[]{:S(2)}, u32[]{:S(2)}) collective-permute-start(bf16[768,768]{1,0:T(8,128)(2,1)S(1)} %copy-done.106), channel_id=1, source_target_pairs={{0,1},{1,0},{2,3},{3,2},{4,5},{5,4},{6,7},{7,6},{8,9},{9,8},{10,11... | collective-permute-start | bytes 3538952 | tf_op jit(solution)/shard_map/ppermute | solution.py:20
  285.5 20.3 %collective-permute-start.84 = (bf16[1,192,768]{2,1,0:T(8,128)(2,1)S(1)}, bf16[1,192,768]{2,1,0:T(8,128)(2,1)S(1)}, u32[]{:S(2)}, u32[]{:S(2)}) collective-permute-start(bf16[1,192,768]{2,1,0:T(8,128)(2,1)S(1)} %fusion.9), channel_id=1, source_target_pairs={{0,16},{16,0},{1,17},{17,1},{2,18},{18,2},{3,19},{19,3},{4,20},{20... | collective-permute-start | bytes 884744 | tf_op jit(solution)/shard_map/ppermute | solution.py:20
  287.9 16.2 %collective-permute-start.101 = (bf16[2,192,768]{2,1,0:T(8,128)(2,1)S(1)}, bf16[2,192,768]{2,1,0:T(8,128)(2,1)S(1)}, u32[]{:S(2)}, u32[]{:S(2)}) collective-permute-start(bf16[2,192,768]{2,1,0:T(8,128)(2,1)S(1)} %fusion.5), channel_id=1, source_target_pairs={{0,2},{1,3},{2,0},{3,1},{4,6},{5,7},{6,4},{7,5},{8,10},{9,11},{10,... | collective-permute-start | bytes 1769480 | tf_op jit(solution)/shard_map/ppermute | solution.py:20
  289.9 26.5 %collective-permute-start.98 = (bf16[2,192,768]{2,1,0:T(8,128)(2,1)S(1)}, bf16[2,192,768]{2,1,0:T(8,128)(2,1)S(1)}, u32[]{:S(2)}, u32[]{:S(2)}) collective-permute-start(bf16[2,192,768]{2,1,0:T(8,128)(2,1)S(1)} %fusion.4), channel_id=1, source_target_pairs={{0,2},{1,3},{2,0},{3,1},{4,6},{5,7},{6,4},{7,5},{8,10},{9,11},{10,... | collective-permute-start | bytes 1769480 | tf_op jit(solution)/shard_map/ppermute | solution.py:20
  304.2 15.0 %collective-permute-start.102 = (bf16[2,192,768]{2,1,0:T(8,128)(2,1)S(1)}, bf16[2,192,768]{2,1,0:T(8,128)(2,1)S(1)}, u32[]{:S(2)}, u32[]{:S(2)}) collective-permute-start(bf16[2,192,768]{2,1,0:T(8,128)(2,1)S(1)} %fusion.1), channel_id=1, source_target_pairs={{0,16},{16,0},{1,17},{17,1},{2,18},{18,2},{3,19},{19,3},{4,20},{20... | collective-permute-start | bytes 1769480 | tf_op jit(solution)/shard_map/ppermute | solution.py:20
  316.5 15.1 %collective-permute-start.99 = (bf16[2,192,768]{2,1,0:T(8,128)(2,1)S(1)}, bf16[2,192,768]{2,1,0:T(8,128)(2,1)S(1)}, u32[]{:S(2)}, u32[]{:S(2)}) collective-permute-start(bf16[2,192,768]{2,1,0:T(8,128)(2,1)S(1)} %fusion.3), channel_id=1, source_target_pairs={{0,16},{16,0},{1,17},{17,1},{2,18},{18,2},{3,19},{19,3},{4,20},{20... | collective-permute-start | bytes 1769480 | tf_op jit(solution)/shard_map/ppermute | solution.py:20
  (229 other events, 2545.2 us)

commit v2 on v0

v2 whole, which is shorter than its diff:
```python
import math
from functools import partial

import jax
import jax.numpy as jnp
from jax import lax
from jax.experimental import pallas as pl
from jax.experimental.pallas import tpu as pltpu
from jax.sharding import PartitionSpec as P


HEAD_DIM = 64
EPS = 1e-5
MASKED = -1e30
F32 = jnp.float32
BF16 = jnp.bfloat16


def exchange(x, axis, bit):
    n = lax.axis_size(axis)
    return lax.ppermute(x, axis, [(i, i ^ bit) for i in range(n)])


def turned(x, bit):
    n = lax.axis_size("row")
    pairs = [(a * n + b, (b ^ bit) * n + a) for a in range(n) for b in range(n)]
    return lax.ppermute(x, ("row", "col"), pairs)


def last_of_dp(low):
    bit = 1
    while 2 * bit < lax.axis_size("dp"):
        low = (low.astype(F32) + exchange(low, "dp", bit).astype(F32)).astype(BF16)
        bit *= 2
    return low, exchange(low, "dp", bit)


def sds(shape, dtype):
    return jax.ShapeDtypeStruct(shape, dtype)


def whole(array):
    return (array, array.shape, (0,) * array.ndim)


def call(kernel, outs, ins, scratch=(), after=(), final=False):
    vmem = pl.BlockSpec(memory_space=pltpu.VMEM)
    specs, args = [], []
    moved = 0
    for item in ins:
        if isinstance(item, tuple):
            array, shape, index = item
            specs.append(pl.BlockSpec(shape, lambda i, index=index: index))
            moved += math.prod(shape) * array.dtype.itemsize
            args.append(array)
            continue
        args.append(item)
        if item.dtype == jnp.int32:
            specs.append(pl.BlockSpec(memory_space=pltpu.SMEM))
        else:
            specs.append(vmem)
            moved += item.size * item.dtype.itemsize
    moved += sum(o.size * o.dtype.itemsize for o in outs)
    n_in, n_after, n_out = len(ins), len(after), len(outs)

    def body(*refs):
        kernel(
            refs[:n_in],
            refs[n_in + n_after : n_in + n_after + n_out],
            refs[n_in + n_after + n_out :],
        )

    return pl.pallas_call(
        body,
        grid=(1,),
        out_shape=outs,
        in_specs=specs + [pl.BlockSpec(memory_space=pl.ANY)] * n_after,
        out_specs=[
            pl.BlockSpec(o.shape, lambda i, d=len(o.shape): (0,) * d) if final else vmem
            for o in outs
        ],
        scratch_shapes=list(scratch),
        compiler_params=pltpu.CompilerParams(vmem_limit_bytes=32 * 1024 * 1024),
        cost_estimate=pl.CostEstimate(
            flops=200_000_000, bytes_accessed=moved, transcendentals=0
        ),
    )(*args, *after)


def rows_of(refs):
    rows = refs[0].shape[0] // 64 * 64
    return jnp.concatenate([r[:rows, :] for r in refs], axis=0)


def dot(a, b):
    return jnp.dot(a, b, preferred_element_type=F32)


def dot_t(a, b):
    return lax.dot_general(a, b, (((1,), (1,)), ((), ())), preferred_element_type=F32)


def t_dot(a, b):
    return lax.dot_general(a, b, (((0,), (0,)), ((), ())), preferred_element_type=F32)


def f32(ref):
    return ref[...].astype(F32)


def tree(refs):
    values = [f32(r) for r in refs]
    while len(values) > 1:
        values = [values[i] + values[i + 1] for i in range(0, len(values), 2)]
    return values[0]


def params_of(prm, layer, which):
    rows = (2 * which + layer, 4 + 2 * layer + which, 8 + 2 * layer + which)
    return [prm[i : i + 1, :] for i in rows]


def norm_of(v):
    mean = jnp.mean(v, axis=-1, keepdims=True)
    centred = v - mean
    r = lax.rsqrt(jnp.mean(centred * centred, axis=-1, keepdims=True) + EPS)
    return centred * r, r


def norm_back(e, unit, r, gain):
    c = e * gain
    return r * (
        c
        - jnp.mean(c, axis=-1, keepdims=True)
        - unit * jnp.mean(c * unit, axis=-1, keepdims=True)
    )


def put_unit(ref, unit, r):
    model = unit.shape[1]
    ref[:, :model] = unit
    ref[:, model:] = jnp.broadcast_to(r, (unit.shape[0], 128))


def get_unit(ref):
    model = ref.shape[1] - 128
    return ref[:, :model], ref[:, model : model + 1]


def put_sums(ref, e, unit, low):
    ref[0:1, :] = jnp.sum(e * unit, axis=0, keepdims=True)
    ref[1:2, :] = jnp.sum(e, axis=0, keepdims=True)
    ref[2:3, :] = jnp.sum(low.astype(F32), axis=0, keepdims=True)
    ref[3:8, :] = jnp.zeros((5, ref.shape[1]), F32)


def place_features(sc, pieces, target):
    place = sc[0] ^ sc[1]
    width = pieces[0].shape[1]
    for k, piece in enumerate(pieces):
        for j in range(len(pieces)):

            @pl.when((place ^ k) == j)
            def _():
                target[:, j * width : (j + 1) * width] = piece[...].astype(target.dtype)


def pick_features(at, count, value, target):
    width = value.shape[1] // count
    for j in range(count):

        @pl.when(at == j)
        def _():
            target[...] = value[:, j * width : (j + 1) * width].astype(target.dtype)


def project(sc, layer, x, w, rowwise, qkv_ref, p_ref):
    tokens = x.shape[0]
    width = w.shape[1] // 4
    b = rowwise[2 + layer : 3 + layer, : 2 * width].astype(F32)
    shift = jnp.concatenate([b[:, :width], jnp.zeros((1, width), F32), b[:, width:]], axis=1)
    qkv = (dot(x, w[:, : 3 * width]) + shift).astype(BF16)
    qkv_ref[...] = qkv
    visible = lax.broadcasted_iota(jnp.int32, (tokens, tokens), 1) < sc[2]
    mixed = []
    for h in range(width // HEAD_DIM):
        q = qkv[:, h * HEAD_DIM : (h + 1) * HEAD_DIM]
        k = qkv[:, width + h * HEAD_DIM : width + (h + 1) * HEAD_DIM]
        v = qkv[:, 2 * width + h * HEAD_DIM : 2 * width + (h + 1) * HEAD_DIM]
        s = jnp.where(visible, dot_t(q, k) * HEAD_DIM ** (-0.5), MASKED)
        e = jnp.exp(s - jnp.max(s, axis=-1, keepdims=True))
        p = e / jnp.sum(e, axis=-1, keepdims=True)
        p_ref[h] = p
        mixed.append(dot(p.astype(BF16), v))
    return jnp.concatenate(mixed, axis=1).astype(BF16)


def mix_out(o, w):
    return dot_t(o, w[:, 3 * (w.shape[1] // 4) :])


def attend_back(d, w, qkv_ref, p_ref):
    width = w.shape[1] // 4
    do = dot(d, w[:, 3 * width :]).astype(BF16)
    qkv = qkv_ref[...]
    dq, dk, dv = [], [], []
    for h in range(width // HEAD_DIM):
        q = qkv[:, h * HEAD_DIM : (h + 1) * HEAD_DIM]
        k = qkv[:, width + h * HEAD_DIM : width + (h + 1) * HEAD_DIM]
        v = qkv[:, 2 * width + h * HEAD_DIM : 2 * width + (h + 1) * HEAD_DIM]
        g = do[:, h * HEAD_DIM : (h + 1) * HEAD_DIM]
        p = p_ref[h]
        dv.append(t_dot(p.astype(BF16), g))
        dp = dot_t(g, v)
        ds = (p * (dp - jnp.sum(p * dp, axis=-1, keepdims=True))).astype(BF16)
        dq.append(dot(ds, k) * HEAD_DIM ** (-0.5))
        dk.append(t_dot(ds, q) * HEAD_DIM ** (-0.5))
    return jnp.concatenate(dq + dk + dv, axis=1).astype(BF16)


def heads_back(low, w):
    return dot_t(low, w[:, : 3 * (w.shape[1] // 4)])


def raise_hidden(layer, h, up, rowwise):
    u = dot(h, up) + rowwise[layer : layer + 1, :].astype(F32)
    cdf = 0.5 * (1.0 + lax.erf(u * (0.5**0.5)))
    slope = cdf + u * (jnp.exp(-0.5 * u * u) * 0.3989422804014327)
    return (u * cdf).astype(BF16), slope


def split_blocks(grad, count, part, parts, keep, send):
    block = grad.shape[0] // count
    each = keep.shape[0] // (2 * parts)
    for k in range(count):
        target = send if k % 2 else keep
        start = ((k // 2) * parts + part) * each
        target[start : start + block, :] = grad[k * block : (k + 1) * block].astype(BF16)


def k_start(ins, outs, scr):
    w, b_out, b_down, gain, shift, b_up, b_qv, hidden_in, cotangent = ins
    block, rowwise, pair = outs
    rows, piece = w.shape[1], b_out.shape[1]
    block[:rows, :] = w[0]
    norms = [b_out[...], b_down[...], gain[0], gain[1], shift[0], shift[1]]
    norms = jnp.concatenate([x.astype(F32) for x in norms] + [jnp.zeros((4, piece), F32)], axis=0)
    block[rows:, :piece] = norms.astype(BF16)
    block[rows:, piece:] = jnp.zeros((16, block.shape[1] - piece), BF16)
    qv = [b_qv[i].astype(F32) for i in range(2)]
    qv = [jnp.concatenate([x[0:1], x[1:2]], axis=1) for x in qv]
    rest = b_up.shape[1] - qv[0].shape[1]
    qv = jnp.concatenate([jnp.concatenate(qv, axis=0), jnp.zeros((2, rest), F32)], axis=1)
    low = jnp.concatenate([b_up[...].astype(F32), qv, jnp.zeros((12, b_up.shape[1]), F32)], axis=0)
    rowwise[...] = low.astype(BF16)
    tokens = hidden_in.shape[0]
    pair[:tokens, :] = hidden_in[...]
    pair[tokens:, :] = cotangent[...]


def k_pack(ins, outs, scr):
    at = 0
    for ref in ins:
        value = ref[0] if len(ref.shape) == 3 else ref[...]
        outs[0][at : at + value.shape[0], :] = value
        at += value.shape[0]


def k_prep(ins, outs, scr):
    sc, *pieces = ins
    tokens = outs[0].shape[0]
    place_features(sc, [p.at[:tokens] for p in pieces], outs[0])
    place_features(sc, [p.at[tokens:] for p in pieces], outs[1])


def k_sum(ins, outs, scr):
    outs[0][...] = (f32(ins[0]) + f32(ins[1])).astype(BF16)


def k_attend_first(m, ins, outs, scr):
    sc, x = ins[:2]
    w_refs, rowwise = ins[2 : 2 + m], ins[2 + m]
    z_ref, prm, o_ref, qkv, p = outs
    piece = w_refs[0].shape[0] - 16
    prm[...] = jnp.concatenate([w[piece:, :piece].astype(F32) for w in w_refs], axis=1)
    w = rows_of(w_refs)
    o = project(sc, 0, x[...], w, rowwise, qkv, p)
    o_ref[...] = o
    z_ref[...] = mix_out(o, w).astype(BF16)


def k_feed(m, layer, ins, outs, scr):
    z, z_other, base = ins[:3]
    up, down = ins[3 : 3 + m], ins[3 + m : 3 + 2 * m]
    rowwise, prm = ins[3 + 2 * m :]
    f_ref, unit_ref, h_ref, g_ref, slope_ref = outs
    if layer:
        _, gain, shift = params_of(prm, layer - 1, 1)
        x = get_unit(base)[0] * gain + shift
    else:
        x = f32(base)
    bias, gain, shift = params_of(prm, layer, 0)
    unit, r = norm_of(x + (f32(z) + f32(z_other) + bias))
    put_unit(unit_ref, unit, r)
    h = (unit * gain + shift).astype(BF16)
    h_ref[...] = h
    g, slope = raise_hidden(layer, h, rows_of(up), rowwise)
    g_ref[...] = g
    slope_ref[...] = slope
    f_ref[...] = dot_t(g, rows_of(down)).astype(BF16)


def k_attend(m, layer, ins, outs, scr):
    sc, f, f_other, unit_ref = ins[:4]
    own = ins[4 : 4 + m]
    rowwise, prm = ins[4 + m :]
    z_ref, unit_out, x_ref, o_ref, qkv, p = outs
    _, gain, shift = params_of(prm, layer - 1, 0)
    h = get_unit(unit_ref)[0] * gain + shift
    bias, gain, shift = params_of(prm, layer - 1, 1)
    unit, r = norm_of(h + (f32(f) + f32(f_other) + bias))
    put_unit(unit_out, unit, r)
    x = (unit * gain + shift).astype(BF16)
    x_ref[...] = x
    w = rows_of(own)
    o = project(sc, layer, x, w, rowwise, qkv, p)
    o_ref[...] = o
    z_ref[...] = mix_out(o, w).astype(BF16)


def feed_back(e, unit, r, gain, ws, slope, outs):
    up, down = ws
    df_ref, low_ref, dh_ref, du_ref, sums = outs
    df = norm_back(e, unit, r, gain)
    low = df.astype(BF16)
    df_ref[...] = df
    low_ref[...] = low
    put_sums(sums, e, unit, low)
    du = (dot(low, rows_of(down)) * slope[...]).astype(BF16)
    du_ref[...] = du
    dh_ref[...] = dot_t(du, rows_of(up)).astype(BF16)


def k_turn(m, layer, ins, outs, scr):
    sc, f, f_other, unit_ref, cotan = ins[:5]
    ws = [ins[5 + i * m : 5 + (i + 1) * m] for i in range(2)]
    slope, prm = ins[5 + 2 * m :]
    _, gain, shift = params_of(prm, layer, 0)
    h = get_unit(unit_ref)[0] * gain + shift
    bias, gain, shift = params_of(prm, layer, 1)
    unit, r = norm_of(h + (f32(f) + f32(f_other) + bias))
    pick_features(sc[0] ^ sc[1], m, unit * gain + shift, outs[0])
    feed_back(f32(cotan), unit, r, gain, ws, slope, outs[1:])


def k_feed_back(m, layer, ins, outs, scr):
    dx, dx_other, da, full = ins[:4]
    ws = [ins[4 + i * m : 4 + (i + 1) * m] for i in range(2)]
    slope, prm = ins[4 + 2 * m :]
    _, gain, _ = params_of(prm, layer, 1)
    e = da[...] + (f32(dx) + f32(dx_other))
    unit, r = get_unit(full)
    feed_back(e, unit, r, gain, ws, slope, outs)


def k_attend_back(m, layer, ins, outs, scr):
    dh, dh_other, df, unit_ref = ins[:4]
    qkv, p, prm = ins[4 + m :]
    da_ref, low_ref, dx_ref, grads_ref, sums = outs
    _, gain, _ = params_of(prm, layer, 0)
    e = df[...] + (f32(dh) + f32(dh_other))
    unit, r = get_unit(unit_ref)
    da = norm_back(e, unit, r, gain)
    low = da.astype(BF16)
    da_ref[...] = da
    low_ref[...] = low
    put_sums(sums, e, unit, low)
    w = rows_of(ins[4 : 4 + m])
    grads = attend_back(low, w, qkv, p)
    grads_ref[...] = grads
    dx_ref[...] = heads_back(grads, w).astype(BF16)


def k_attend_back_last(n, m, ins, outs, scr):
    sc, dh, dh_other, df, unit_ref = ins[:5]
    qkv, p, prm = ins[5 + m :]
    low_ref, grads_ref, sums = outs[n:]
    _, gain, _ = params_of(prm, 0, 0)
    e = df[...] + (f32(dh) + f32(dh_other))
    unit, r = get_unit(unit_ref)
    da = norm_back(e, unit, r, gain)
    low = da.astype(BF16)
    low_ref[...] = low
    put_sums(sums, e, unit, low)
    w = rows_of(ins[5 : 5 + m])
    grads = attend_back(low, w, qkv, p)
    grads_ref[...] = grads
    dx = heads_back(grads, w)
    place = sc[0] ^ sc[1]
    pick_features(place, m, da + dx, outs[0])
    for k in range(1, n):
        pick_features(place ^ k, m, dx, outs[k])


def k_total(ins, outs, scr):
    outs[0][...] = ins[0][...] + ((f32(ins[1]) + f32(ins[2])) + f32(ins[3]))


def k_feed_weight(m, ins, outs, scr):
    low, g, h, du = ins
    keep, send, sums = outs
    split_blocks(t_dot(low[...], g[...]), m, 0, 2, keep, send)
    split_blocks(t_dot(h[...], du[...]), m, 1, 2, keep, send)
    sums[0:1, :] = jnp.sum(f32(du), axis=0, keepdims=True)
    sums[1:8, :] = jnp.zeros((7, sums.shape[1]), F32)


def k_attend_weight(m, ins, outs, scr):
    x, grads, low, o = ins[:4]
    keep, send, sums = outs
    first = t_dot(x[...], grads[...])
    second = t_dot(low[...], o[...])
    split_blocks(jnp.concatenate([first, second], axis=1), m, 0, 1, keep, send)
    sums[...] = jnp.zeros(sums.shape, F32)
    sums[0:1, : grads.shape[1]] = jnp.sum(f32(grads), axis=0, keepdims=True)


def k_attend_weight_last(m, ins, outs, scr):
    x, grads, low, o = ins[:4]
    hidden_sums, head_sums, norm_sums = ins[4:6], ins[6], ins[7:]
    keep, send = outs
    first = t_dot(x[...], grads[...])
    second = t_dot(low[...], o[...])
    split_blocks(jnp.concatenate([first, second], axis=1), m, 0, 1, keep, send)
    model = x.shape[1]
    piece = model // m
    width = grads.shape[1]
    own = jnp.sum(f32(grads), axis=0, keepdims=True)
    own = jnp.concatenate([own, jnp.zeros((1, model - width), F32)], axis=1)
    common = [r[0:1, :] for r in hidden_sums] + [own, head_sums[0:1, :]]
    common = jnp.concatenate(common, axis=0)
    each = jnp.concatenate([r[0:3, :] for r in norm_sums], axis=0)
    rows = keep.shape[0] // 2
    for k in range(m):
        target = send if k % 2 else keep
        start = (k // 2) * rows + piece
        block = jnp.concatenate(
            [each[:, k * piece : (k + 1) * piece], jnp.zeros((each.shape[0], model - piece), F32)],
            axis=1,
        )
        target[start : start + 16, :] = jnp.concatenate([common, block], axis=0).astype(BF16)


def k_middle(ins, outs, scr):
    keep, got = ins
    total = f32(keep) + f32(got)
    rows = outs[0].shape[0]
    for i, out in enumerate(outs):
        out[...] = total[i * rows : (i + 1) * rows].astype(BF16)


def k_add(ins, outs, scr):
    outs[0][...] = (f32(ins[0]) + f32(ins[1])).astype(outs[0].dtype)


def k_feed_outputs(ins, outs, scr):
    for i, out in enumerate(outs):
        for layer in range(2):
            at = 4 * layer + 2 * i
            out[layer] = f32(ins[at]) + f32(ins[at + 1])


def k_attend_outputs(ins, outs, scr):
    grad_w, qv, b_out, gains, shifts, b_up, b_down = outs
    piece = grad_w.shape[1]
    total = f32(ins[0]) + f32(ins[1])
    grad_w[0] = total[:piece]
    grad_w[1] = f32(ins[2]) + f32(ins[3])
    small = total[piece:]
    b_up[...] = small[0:2]
    for layer in range(2):
        heads = small[2 + layer : 3 + layer]
        qv[layer, 0:1, :] = heads[:, :piece]
        qv[layer, 1:2, :] = heads[:, 2 * piece : 3 * piece]
        at = 4 + 6 * layer
        b_out[layer : layer + 1, :] = small[at + 2 : at + 3, :piece]
        b_down[layer : layer + 1, :] = small[at + 5 : at + 6, :piece]
        for which in range(2):
            start = at + 3 * which
            gains[layer, which : which + 1, :] = small[start : start + 1, :piece]
            shifts[layer, which : which + 1, :] = small[start + 1 : start + 2, :piece]


def per_device(
    hidden_in, lengths, w_attn, b_qv, b_out, ln_gain, ln_bias, w_up, b_up, w_down, b_down, cotangent
):
    layers = w_attn.shape[0]
    n, m = lax.axis_size("row"), lax.axis_size("col")
    row, col = lax.axis_index("row"), lax.axis_index("col")
    tokens, piece = hidden_in.shape
    model = piece * m
    hidden = w_up.shape[2]
    width = w_attn.shape[2] // 4
    heads = width // HEAD_DIM
    length = lax.dynamic_index_in_dim(lengths, col, 0, keepdims=False)
    sc = jnp.stack([row, col, length]).astype(jnp.int32)

    tile = (tokens, model)

    def layer_of(array, layer):
        return (array, (1,) + array.shape[1:], (layer, 0, 0))

    def pack(rows, arrays, after=()):
        return call(k_pack, [sds((rows, hidden), BF16)], arrays, after=after, final=True)[0]

    def held(array, after):
        return pack(array.shape[0], [whole(array)], after)

    def blocks(own, along, near, rows=piece):
        views = [(own, 0), (near, 0), (along, 0), (near, 1)]
        return [(a, (rows, hidden), (i, 0)) for a, i in views]

    def near_of(own, along, after=()):
        both = pack(2 * own.shape[0], [whole(own), whole(along)], after)
        return exchange(both, "col", 1)

    def sent(array, layer, after):
        own = pack(piece, [layer_of(array, layer)], after)
        return own, exchange(own, "col", 2)

    def pair_sum(value, after=()):
        return call(k_sum, [low_tile], [value, exchange(value, "row", 1)], after=after)[0]

    def both(value):
        return [value, exchange(value, "row", 2)]

    block, rowwise, pair = call(
        k_start,
        [sds((piece + 16, hidden), BF16), sds((16, hidden), BF16), sds((2 * tokens, piece), BF16)],
        [
            layer_of(w_attn, 0),
            *map(whole, (b_out, b_down, ln_gain, ln_bias, b_up, b_qv, hidden_in, cotangent)),
        ],
    )
    along = exchange(block, "col", 2)
    x_in = [turned(pair, k) for k in range(n)]
    x, cotan = call(k_prep, [sds(tile, BF16)] * 2, [sc, *x_in])
    near = near_of(block, along, [x])
    up0, up0_along = sent(w_up, 0, [x])

    low_tile = sds(tile, BF16)
    low_block, low_tail = sds((piece, hidden), BF16), sds((piece + 16, hidden), BF16)
    unit_out = sds((tokens, model + 128), F32)
    qkv_out, p_out, o_out = (
        sds((tokens, 3 * width), BF16),
        sds((heads, tokens, tokens), F32),
        sds((tokens, width), BF16),
    )
    g_out, slope_out = sds((tokens, hidden), BF16), sds((tokens, hidden), F32)
    feed_out = [low_tile, unit_out, low_tile, g_out, slope_out]

    attn0 = blocks(block, along, near, piece + 16)
    z, prm, o0, qkv0, p0 = call(
        partial(k_attend_first, m),
        [low_tile, sds((16, model), F32), o_out, qkv_out, p_out],
        [sc, x, *attn0, rowwise],
        after=[up0_along],
    )
    down0, down0_along = sent(w_down, 0, [z])
    up0_near = near_of(up0, up0_along, [z])
    z = pair_sum(z, [down0_along, up0_near])
    down0_near = near_of(down0, down0_along, [z])
    attn1, attn1_along = sent(w_attn, 1, [z])
    up0 = blocks(up0, up0_along, up0_near)
    down0 = blocks(down0, down0_along, down0_near)
    f, unit_a0, h0, g0, slope0 = call(
        partial(k_feed, m, 0),
        feed_out,
        [*both(z), x, *up0, *down0, rowwise, prm],
        after=[attn1_along],
    )
    attn1_near = near_of(attn1, attn1_along, [f])
    attn1 = blocks(attn1, attn1_along, attn1_near)
    f = pair_sum(f, [attn1_near])
    up1, up1_along = sent(w_up, 1, [f])
    z, unit_b0, x1, o1, qkv1, p1 = call(
        partial(k_attend, m, 1),
        [low_tile, unit_out, low_tile, o_out, qkv_out, p_out],
        [sc, *both(f), unit_a0, *attn1, rowwise, prm],
        after=[up1_along],
    )
    down1, down1_along = sent(w_down, 1, [z])
    up1_near = near_of(up1, up1_along, [z])
    z = pair_sum(z, [down1_along, up1_near])
    down1_near = near_of(down1, down1_along, [z])
    up1 = blocks(up1, up1_along, up1_near)
    down1 = blocks(down1, down1_along, down1_near)
    f, unit_a1, h1, g1, slope1 = call(
        partial(k_feed, m, 1),
        feed_out,
        [*both(z), unit_b0, *up1, *down1, rowwise, prm],
    )

    sums_out = sds((8, model), F32)
    feed_back_out = [sds(tile, F32), low_tile, low_tile, sds((tokens, hidden), BF16), sums_out]
    out, df, df_low, dh, du, sums_b1 = call(
        partial(k_turn, m, 1),
        [sds((tokens, piece), BF16)] + feed_back_out,
        [sc, *both(pair_sum(f)), unit_a1, cotan, *up1, *down1, slope1, prm],
    )
    out_hidden = turned(out, 0)
    weight_out = [sds((4 * piece, hidden), BF16)] * 2 + [sds((8, hidden), F32)]
    keep, send, hidden_sums1 = call(
        partial(k_feed_weight, m), weight_out, [df_low, g1, h1, du]
    )
    got = exchange(send, "col", 1)
    dh = pair_sum(dh, [got])
    down1_stay, up1_stay, down1_go, up1_go = call(k_middle, [low_block] * 4, [keep, got], after=[dh])
    down1_more = exchange(down1_go, "col", 2)
    da, da_low, dx, grads1, sums_a1 = call(
        partial(k_attend_back, m, 1),
        [sds(tile, F32), low_tile, low_tile, qkv_out, sums_out],
        [*both(dh), df, unit_a1, *attn1, qkv1, p1, prm],
        after=[down1_more, out_hidden],
    )
    keep, send, head_sums1 = call(
        partial(k_attend_weight, m),
        [sds((2 * piece, 4 * width), BF16)] * 2 + [sums_out],
        [x1, grads1, da_low, o1],
    )
    got = exchange(send, "col", 1)
    up1_more = exchange(held(up1_go, [dx]), "col", 2)
    dx = pair_sum(dx, [got, up1_more])
    attn1_stay, attn1_go = call(k_middle, [low_block] * 2, [keep, got], after=[dx])
    attn1_more = exchange(attn1_go, "col", 2)
    (down1_low,) = call(k_add, [low_block], [down1_stay, down1_more], after=[dx])
    down1_terms = last_of_dp(down1_low)

    df, df_low, dh, du, sums_b0 = call(
        partial(k_feed_back, m, 0),
        feed_back_out,
        [*both(dx), da, unit_b0, *up0, *down0, slope0, prm],
        after=[attn1_more, down1_terms[1]],
    )
    keep, send, hidden_sums0 = call(
        partial(k_feed_weight, m), weight_out, [df_low, g0, h0, du]
    )
    got = exchange(send, "col", 1)
    (up1_low,) = call(k_add, [low_block], [up1_stay, up1_more], after=[dh])
    up1_terms = last_of_dp(up1_low)
    dh = pair_sum(dh, [got, up1_terms[1]])
    down0_stay, up0_stay, down0_go, up0_go = call(k_middle, [low_block] * 4, [keep, got], after=[dh])
    down0_more = exchange(down0_go, "col", 2)
    (attn1_low,) = call(k_add, [low_block], [attn1_stay, attn1_more], after=[dh])
    attn1_terms = last_of_dp(attn1_low)
    *dx, low_last, grads0, sums_a0 = call(
        partial(k_attend_back_last, n, m),
        [sds((tokens, piece), F32)]
        + [sds((tokens, piece), BF16)] * (n - 1)
        + [low_tile, qkv_out, sums_out],
        [sc, *both(dh), df, unit_a0, *attn0, qkv0, p0, prm],
        after=[down0_more, attn1_terms[1]],
    )
    up0_more = exchange(held(up0_go, [dx[0]]), "col", 2)
    (grad_input,) = call(
        k_total,
        [sds((tokens, piece), F32)],
        [dx[0]] + [exchange(dx[k], "row", k) for k in range(1, n)],
        after=[up0_more],
    )
    grad_input = turned(grad_input, 0)

    keep, send = call(
        partial(k_attend_weight_last, m),
        [sds((2 * (piece + 16), 4 * width), BF16)] * 2,
        [
            x,
            grads0,
            low_last,
            o0,
            hidden_sums0,
            hidden_sums1,
            head_sums1,
            sums_a0,
            sums_b0,
            sums_a1,
            sums_b1,
        ],
    )
    got = exchange(send, "col", 1)
    attn0_stay, attn0_go = call(k_middle, [low_tail] * 2, [keep, got])
    (down0_low,) = call(k_add, [low_block], [down0_stay, down0_more])
    down0_terms = last_of_dp(down0_low)
    (up0_low,) = call(k_add, [low_block], [up0_stay, up0_more])
    up0_terms = last_of_dp(up0_low)
    (attn0_low,) = call(k_add, [low_tail], [attn0_stay, exchange(attn0_go, "col", 2)])
    attn0_terms = last_of_dp(attn0_low)
    grad_down, grad_up = call(
        k_feed_outputs,
        [sds((layers, piece, hidden), F32)] * 2,
        [*down0_terms, *up0_terms, *down1_terms, *up1_terms],
        final=True,
    )
    grad_attn, grad_qv, grad_out, grad_gain, grad_shift, grad_b_up, grad_b_down = call(
        k_attend_outputs,
        [
            sds(w_attn.shape, F32),
            sds(b_qv.shape, F32),
            sds(b_out.shape, F32),
            sds(ln_gain.shape, F32),
            sds(ln_bias.shape, F32),
            sds(b_up.shape, F32),
            sds(b_down.shape, F32),
        ],
        [*attn0_terms, *attn1_terms],
        final=True,
    )
    return (
        out_hidden,
        grad_input,
        grad_attn,
        grad_qv,
        grad_out,
        grad_gain,
        grad_shift,
        grad_up,
        grad_b_up,
        grad_down,
        grad_b_down,
    )


def solution(mesh):
    in_specs = (
        P(("dp", "row"), "col"),
        P("dp"),
        P(None, "col", "row"),
        P(None, None, "row"),
        P(None, "col"),
        P(None, None, "col"),
        P(None, None, "col"),
        P(None, "col", "row"),
        P(None, "row"),
        P(None, "col", "row"),
        P(None, "col"),
        P(("dp", "row"), "col"),
    )
    out_specs = (
        P(("dp", "row"), "col"),
        P(("dp", "row"), "col"),
        P(None, "col", "row"),
        P(None, None, "row"),
        P(None, "col"),
        P(None, None, "col"),
        P(None, None, "col"),
        P(None, "col", "row"),
        P(None, "row"),
        P(None, "col", "row"),
        P(None, "col"),
    )
    return jax.shard_map(
        per_device, mesh=mesh, in_specs=in_specs, out_specs=out_specs, check_vma=False
    )
```

time: 659 us -> 248 us (0.38)
  blocking collectives: 283 us -> 0 us
  waiting for transfers between devices: 248 us -> 172 us
  matrix products: 32.6 us -> 0 us
  other arithmetic: 25.9 us -> 0.72 us
  Pallas kernels: 0 us -> 22.3 us
  starting transfers between devices: 17.9 us -> 40.1 us
  local copies, waits for them, and re-layouts: 30.6 us -> 11.5 us
  between operations: 16.5 us -> 1.13 us
    all_gather x18 -> x0, blocking collectives: 183 us -> none  [the longest x4 51 us: back_out(): grad_all = lax.all_gather(grad_low, 'row', axis=0, tiled=True)]
    ppermute x0 -> x51, waiting for transfers between devices: none -> 172 us  [the longest x45 148 us: exchange(): return lax.ppermute(x, axis, [(i, i ^ bit) for i in range(n)])]
    unnamed x25 -> x0, waiting for transfers between devices: 161 us -> none
    psum x14 -> x0, blocking collectives: 100 us -> none  [the longest x12 70.1 us: feature_total(): return lax.psum(members, 'col')]
    psum x1 -> x0, waiting for transfers between devices: 41.2 us -> none  [per_device(): lax.psum(attn_w.astype(jnp.bfloat16), 'dp').astype(jnp.float32)]
    ppermute x0 -> x51, starting transfers between devices: none -> 40.1 us  [the longest x45 23.1 us: exchange(): return lax.ppermute(x, axis, [(i, i ^ bit) for i in range(n)])]
    reduce_scatter x2 -> x0, waiting for transfers between devices: 39.1 us -> none  [back_out(): lax.psum_scatter(partial_term(jnp.int32(0), lax.axis_size('col') * grad_l...]
    dot_general x36 -> x0, matrix products: 32.6 us -> none  [the longest x8 10.8 us: inner_rows(): lax.dot_general(left_side, right_side, (((0,), (0,)), ((), ())), preferre...]
  transfers between devices with their start and end apart: 19 -> 51, of which waited for: 14 -> 28; matrix products, arithmetic and copies ran while one was open for 4% -> 2% of each run, Pallas kernels for 0% -> 2%
where the time goes in v2:
time: 248 us; the launch traced here: 247 us
  waiting for transfers between devices  172 us (69%)
  starting transfers between devices  40.1 us (16%)
  Pallas kernels  22.3 us (9%)
  local copies, waits for them, and re-layouts  11.5 us (5%)
    ppermute x45, waiting for transfers between devices, exchange(): return lax.ppermute(x, axis, [(i, i ^ bit) for i in range(n)])  148 us
    ppermute x6, waiting for transfers between devices, turned(): return lax.ppermute(x, ('row', 'col'), pairs)  23.2 us
    ppermute x45, starting transfers between devices, exchange(): return lax.ppermute(x, axis, [(i, i ^ bit) for i in range(n)])  23.1 us
    pallas_call x47, Pallas kernels, call(): pl.pallas_call(body, grid=(1,), out_shape=outs, in_specs=specs + [pl.Bloc...  22.3 us
    ppermute x6, starting transfers between devices, turned(): return lax.ppermute(x, ('row', 'col'), pairs)  17 us
    unnamed x24, local copies, waits for them, and re-layouts  10.2 us
  transfers between devices with their start and end apart: 51, of which 28 were waited for; matrix products, arithmetic and copies ran while one was open for 2% of the time, Pallas kernels for 2%

profile of v2, /device:TPU:2, one launch (start us, length us, event | category | flops | bytes accessed | tf_op | source)
XLA Modules:
  0.0 247.3 jit_solution(3067511707023183957)
XLA Ops:
  7.8 3.0 %collective-permute-start.3 = (bf16[256,192]{1,0:T(8,128)(2,1)S(1)}, bf16[256,192]{1,0:T(8,128)(2,1)S(1)}, u32[]{:S(2)}, u32[]{:S(2)}) collective-permute-start(bf16[256,192]{1,0:T(8,128)(2,1)S(1)} %get-tuple-element.92), channel_id=1, source_target_pairs={{0,12},{1,8},{2,4},{3,0},{4,13},{5,9},{6,5},{7,1},{8,14},{9,10},{1... | collective-permute-start | bytes 294920 | tf_op jit(solution)/shard_map/ppermute | solution.py:27
  13.4 4.4 %collective-permute-start = (bf16[256,192]{1,0:T(8,128)(2,1)S(1)}, bf16[256,192]{1,0:T(8,128)(2,1)S(1)}, u32[]{:S(2)}, u32[]{:S(2)}) collective-permute-start(bf16[256,192]{1,0:T(8,128)(2,1)S(1)} %get-tuple-element.92), channel_id=1, source_target_pairs={{0,0},{1,4},{2,8},{3,12},{4,1},{5,5},{6,9},{7,13},{8,2},{9,6},{10,... | collective-permute-start | bytes 294920 | tf_op jit(solution)/shard_map/ppermute | solution.py:27
  19.8 3.2 %collective-permute-done.2.refs_3_ = bf16[256,192]{1,0:T(8,128)(2,1)S(1)} collective-permute-done((bf16[256,192]{1,0:T(8,128)(2,1)S(1)}, bf16[256,192]{1,0:T(8,128)(2,1)S(1)}, u32[]{:S(2)}, u32[]{:S(2)}) %collective-permute-start.2) | collective-permute-done | bytes 98336 | tf_op jit(solution)/shard_map/ppermute | solution.py:27
  28.7 9.4 %collective-permute-done.6.refs_7_.refs_1_.refs_5_.refs_6_ = bf16[192,768]{1,0:T(8,128)(2,1)S(1)} collective-permute-done((bf16[192,768]{1,0:T(8,128)(2,1)S(1)}, bf16[192,768]{1,0:T(8,128)(2,1)S(1)}, u32[]{:S(2)}, u32[]{:S(2)}) %collective-permute-start.6) | collective-permute-done | bytes 294944 | tf_op jit(solution)/shard_map/ppermute | solution.py:21
  41.9 5.7 %collective-permute-done.7.refs_1_ = bf16[128,768]{1,0:T(8,128)(2,1)S(1)} collective-permute-done((bf16[128,768]{1,0:T(8,128)(2,1)S(1)}, bf16[128,768]{1,0:T(8,128)(2,1)S(1)}, u32[]{:S(2)}, u32[]{:S(2)}) %collective-permute-start.7) | collective-permute-done | bytes 196640 | tf_op jit(solution)/shard_map/ppermute | solution.py:21
  50.4 12.1 %collective-permute-done.10.refs_1_ = bf16[128,768]{1,0:T(8,128)(2,1)S(1)} collective-permute-done((bf16[128,768]{1,0:T(8,128)(2,1)S(1)}, bf16[128,768]{1,0:T(8,128)(2,1)S(1)}, u32[]{:S(2)}, u32[]{:S(2)}) %collective-permute-start.10) | collective-permute-done | bytes 196640 | tf_op jit(solution)/shard_map/ppermute | solution.py:21
  63.6 7.2 %collective-permute-done.13.refs_1_ = bf16[128,768]{1,0:T(8,128)(2,1)S(1)} collective-permute-done((bf16[128,768]{1,0:T(8,128)(2,1)S(1)}, bf16[128,768]{1,0:T(8,128)(2,1)S(1)}, u32[]{:S(2)}, u32[]{:S(2)}) %collective-permute-start.13) | collective-permute-done | bytes 196640 | tf_op jit(solution)/shard_map/ppermute | solution.py:21
  72.6 11.2 %collective-permute-done.15.refs_2_ = bf16[128,768]{1,0:T(8,128)(2,1)S(1)} collective-permute-done((bf16[128,768]{1,0:T(8,128)(2,1)S(1)}, bf16[128,768]{1,0:T(8,128)(2,1)S(1)}, u32[]{:S(2)}, u32[]{:S(2)}) %collective-permute-start.15) | collective-permute-done | bytes 196640 | tf_op jit(solution)/shard_map/ppermute | solution.py:21
  86.4 7.0 %collective-permute-done.17.refs_1_ = bf16[128,768]{1,0:T(8,128)(2,1)S(1)} collective-permute-done((bf16[128,768]{1,0:T(8,128)(2,1)S(1)}, bf16[128,768]{1,0:T(8,128)(2,1)S(1)}, u32[]{:S(2)}, u32[]{:S(2)}) %collective-permute-start.17) | collective-permute-done | bytes 196640 | tf_op jit(solution)/shard_map/ppermute | solution.py:21
  95.6 10.3 %collective-permute-done.20.refs_1_ = bf16[128,768]{1,0:T(8,128)(2,1)S(1)} collective-permute-done((bf16[128,768]{1,0:T(8,128)(2,1)S(1)}, bf16[128,768]{1,0:T(8,128)(2,1)S(1)}, u32[]{:S(2)}, u32[]{:S(2)}) %collective-permute-start.20) | collective-permute-done | bytes 196640 | tf_op jit(solution)/shard_map/ppermute | solution.py:21
  106.9 6.9 %collective-permute-done.22.refs_1_ = bf16[128,768]{1,0:T(8,128)(2,1)S(1)} collective-permute-done((bf16[128,768]{1,0:T(8,128)(2,1)S(1)}, bf16[128,768]{1,0:T(8,128)(2,1)S(1)}, u32[]{:S(2)}, u32[]{:S(2)}) %collective-permute-start.22) | collective-permute-done | bytes 196640 | tf_op jit(solution)/shard_map/ppermute | solution.py:21
  115.0 10.1 %collective-permute-done.23.refs_2_ = bf16[128,768]{1,0:T(8,128)(2,1)S(1)} collective-permute-done((bf16[128,768]{1,0:T(8,128)(2,1)S(1)}, bf16[128,768]{1,0:T(8,128)(2,1)S(1)}, u32[]{:S(2)}, u32[]{:S(2)}) %collective-permute-start.23) | collective-permute-done | bytes 196640 | tf_op jit(solution)/shard_map/ppermute | solution.py:21
  127.8 7.2 %collective-permute-done.25.refs_1_ = bf16[128,768]{1,0:T(8,128)(2,1)S(1)} collective-permute-done((bf16[128,768]{1,0:T(8,128)(2,1)S(1)}, bf16[128,768]{1,0:T(8,128)(2,1)S(1)}, u32[]{:S(2)}, u32[]{:S(2)}) %collective-permute-start.25) | collective-permute-done | bytes 196640 | tf_op jit(solution)/shard_map/ppermute | solution.py:21
  136.9 5.0 %collective-permute-start.24 = (bf16[128,192]{1,0:T(8,128)(2,1)S(1)}, bf16[128,192]{1,0:T(8,128)(2,1)S(1)}, u32[]{:S(2)}, u32[]{:S(2)}) collective-permute-start(bf16[128,192]{1,0:T(8,128)(2,1)S(1)} %get-tuple-element.106), channel_id=1, source_target_pairs={{0,0},{1,4},{2,8},{3,12},{4,1},{5,5},{6,9},{7,13},{8,2},{9,6},{10,... | collective-permute-start | bytes 147464 | tf_op jit(solution)/shard_map/ppermute | solution.py:27
  141.9 9.0 %collective-permute-done.24.refs_12_ = bf16[128,192]{1,0:T(8,128)(2,1)S(1)} collective-permute-done((bf16[128,192]{1,0:T(8,128)(2,1)S(1)}, bf16[128,192]{1,0:T(8,128)(2,1)S(1)}, u32[]{:S(2)}, u32[]{:S(2)}) %collective-permute-start.24) | collective-permute-done | bytes 49184 | tf_op jit(solution)/shard_map/ppermute | solution.py:27
  154.1 6.8 %collective-permute-done.29.refs_1_ = bf16[128,768]{1,0:T(8,128)(2,1)S(1)} collective-permute-done((bf16[128,768]{1,0:T(8,128)(2,1)S(1)}, bf16[128,768]{1,0:T(8,128)(2,1)S(1)}, u32[]{:S(2)}, u32[]{:S(2)}) %collective-permute-start.29) | collective-permute-done | bytes 196640 | tf_op jit(solution)/shard_map/ppermute | solution.py:21
  165.9 10.4 %collective-permute-done.32.refs_1_ = bf16[128,768]{1,0:T(8,128)(2,1)S(1)} collective-permute-done((bf16[128,768]{1,0:T(8,128)(2,1)S(1)}, bf16[128,768]{1,0:T(8,128)(2,1)S(1)}, u32[]{:S(2)}, u32[]{:S(2)}) %collective-permute-start.32) | collective-permute-done | bytes 196640 | tf_op jit(solution)/shard_map/ppermute | solution.py:21
  178.9 7.0 %collective-permute-done.35.refs_1_ = bf16[128,768]{1,0:T(8,128)(2,1)S(1)} collective-permute-done((bf16[128,768]{1,0:T(8,128)(2,1)S(1)}, bf16[128,768]{1,0:T(8,128)(2,1)S(1)}, u32[]{:S(2)}, u32[]{:S(2)}) %collective-permute-start.35) | collective-permute-done | bytes 196640 | tf_op jit(solution)/shard_map/ppermute | solution.py:21
  190.3 9.9 %collective-permute-done.38.refs_2_ = bf16[128,768]{1,0:T(8,128)(2,1)S(1)} collective-permute-done((bf16[128,768]{1,0:T(8,128)(2,1)S(1)}, bf16[128,768]{1,0:T(8,128)(2,1)S(1)}, u32[]{:S(2)}, u32[]{:S(2)}) %collective-permute-start.38) | collective-permute-done | bytes 196640 | tf_op jit(solution)/shard_map/ppermute | solution.py:21
  208.6 7.6 %collective-permute-done.47.refs_1_ = bf16[208,768]{1,0:T(8,128)(2,1)S(1)} collective-permute-done((bf16[208,768]{1,0:T(8,128)(2,1)S(1)}, bf16[208,768]{1,0:T(8,128)(2,1)S(1)}, u32[]{:S(2)}, u32[]{:S(2)}) %collective-permute-start.47) | collective-permute-done | bytes 319520 | tf_op jit(solution)/shard_map/ppermute | solution.py:21
  216.9 4.9 %collective-permute-done.44.refs_4_.refs_1_ = bf16[192,768]{1,0:T(8,128)(2,1)S(1)} collective-permute-done((bf16[192,768]{1,0:T(8,128)(2,1)S(1)}, bf16[192,768]{1,0:T(8,128)(2,1)S(1)}, u32[]{:S(2)}, u32[]{:S(2)}) %collective-permute-start.44) | collective-permute-done | bytes 294944 | tf_op jit(solution)/shard_map/ppermute | solution.py:21
  222.4 3.0 %collective-permute-start.42 = (bf16[128,192]{1,0:T(8,128)(2,1)S(1)}, bf16[128,192]{1,0:T(8,128)(2,1)S(1)}, u32[]{:S(2)}, u32[]{:S(2)}) collective-permute-start(bf16[128,192]{1,0:T(8,128)(2,1)S(1)} %get-tuple-element.145), channel_id=1, source_target_pairs={{0,8},{4,12},{8,0},{12,4},{1,9},{5,13},{9,1},{13,5},{2,10},{6,14},... | collective-permute-start | bytes 147464 | tf_op jit(solution)/shard_map/ppermute | solution.py:21
  229.1 3.6 %collective-permute-done.43.refs_3_ = bf16[128,192]{1,0:T(8,128)(2,1)S(1)} collective-permute-done((bf16[128,192]{1,0:T(8,128)(2,1)S(1)}, bf16[128,192]{1,0:T(8,128)(2,1)S(1)}, u32[]{:S(2)}, u32[]{:S(2)}) %collective-permute-start.43) | collective-permute-done | bytes 49184 | tf_op jit(solution)/shard_map/ppermute | solution.py:21
  235.4 6.6 %collective-permute-done.45 = f32[128,192]{1,0:T(8,128)} collective-permute-done((f32[128,192]{1,0:T(8,128)S(1)}, f32[128,192]{1,0:T(8,128)}, u32[]{:S(2)}, u32[]{:S(2)}) %collective-permute-start.45) | collective-permute-done | bytes 98336 | tf_op jit(solution)/shard_map/ppermute | solution.py:27
  (151 shorter events, 74.6 us)
Async XLA Ops:
  7.7 20.8 %collective-permute-start.4 = (bf16[208,768]{1,0:T(8,128)(2,1)S(1)}, bf16[208,768]{1,0:T(8,128)(2,1)S(1)}, u32[]{:S(2)}, u32[]{:S(2)}) collective-permute-start(bf16[208,768]{1,0:T(8,128)(2,1)S(1)} %get-tuple-element.94.refs_0_.refs_2_.refs_5_), channel_id=1, source_target_pairs={{0,2},{1,3},{2,0},{3,1},{4,6},{5,7},{6,4},{7,5},{8,10},{9,11},{10,... | collective-permute-start | bytes 958472 | tf_op jit(solution)/shard_map/ppermute | solution.py:21
  7.8 12.0 %collective-permute-start.3 = (bf16[256,192]{1,0:T(8,128)(2,1)S(1)}, bf16[256,192]{1,0:T(8,128)(2,1)S(1)}, u32[]{:S(2)}, u32[]{:S(2)}) collective-permute-start(bf16[256,192]{1,0:T(8,128)(2,1)S(1)} %get-tuple-element.92), channel_id=1, source_target_pairs={{0,12},{1,8},{2,4},{3,0},{4,13},{5,9},{6,5},{7,1},{8,14},{9,10},{1... | collective-permute-start | bytes 294920 | tf_op jit(solution)/shard_map/ppermute | solution.py:27
  10.8 12.2 %collective-permute-start.2 = (bf16[256,192]{1,0:T(8,128)(2,1)S(1)}, bf16[256,192]{1,0:T(8,128)(2,1)S(1)}, u32[]{:S(2)}, u32[]{:S(2)}) collective-permute-start(bf16[256,192]{1,0:T(8,128)(2,1)S(1)} %get-tuple-element.92), channel_id=1, source_target_pairs={{0,8},{1,12},{2,0},{3,4},{4,9},{5,13},{6,1},{7,5},{8,10},{9,14},{1... | collective-permute-start | bytes 294920 | tf_op jit(solution)/shard_map/ppermute | solution.py:27
  13.4 11.6 %collective-permute-start.1 = (bf16[256,192]{1,0:T(8,128)(2,1)S(1)}, bf16[256,192]{1,0:T(8,128)(2,1)S(1)}, u32[]{:S(2)}, u32[]{:S(2)}) collective-permute-start(bf16[256,192]{1,0:T(8,128)(2,1)S(1)} %get-tuple-element.92), channel_id=1, source_target_pairs={{0,4},{1,0},{2,12},{3,8},{4,5},{5,1},{6,13},{7,9},{8,6},{9,2},{10,... | collective-permute-start | bytes 294920 | tf_op jit(solution)/shard_map/ppermute | solution.py:27
  13.4 14.1 %collective-permute-start = (bf16[256,192]{1,0:T(8,128)(2,1)S(1)}, bf16[256,192]{1,0:T(8,128)(2,1)S(1)}, u32[]{:S(2)}, u32[]{:S(2)}) collective-permute-start(bf16[256,192]{1,0:T(8,128)(2,1)S(1)} %get-tuple-element.92), channel_id=1, source_target_pairs={{0,0},{1,4},{2,8},{3,12},{4,1},{5,5},{6,9},{7,13},{8,2},{9,6},{10,... | collective-permute-start | bytes 294920 | tf_op jit(solution)/shard_map/ppermute | solution.py:27
  49.6 12.8 %collective-permute-start.11 = (bf16[384,768]{1,0:T(8,128)(2,1)S(1)}, bf16[384,768]{1,0:T(8,128)(2,1)S(1)}, u32[]{:S(2)}, u32[]{:S(2)}) collective-permute-start(bf16[384,768]{1,0:T(8,128)(2,1)S(1)} %shard_map.211), channel_id=1, source_target_pairs={{0,1},{1,0},{2,3},{3,2},{4,5},{5,4},{6,7},{7,6},{8,9},{9,8},{10,11... | collective-permute-start | bytes 1769480 | tf_op jit(solution)/shard_map/ppermute | solution.py:21
  49.8 12.7 %collective-permute-start.12 = (bf16[192,768]{1,0:T(8,128)(2,1)S(1)}, bf16[192,768]{1,0:T(8,128)(2,1)S(1)}, u32[]{:S(2)}, u32[]{:S(2)}) collective-permute-start(bf16[192,768]{1,0:T(8,128)(2,1)S(1)} %shard_map.212.refs_0_.refs_4_), channel_id=1, source_target_pairs={{0,2},{1,3},{2,0},{3,1},{4,6},{5,7},{6,4},{7,5},{8,10},{9,11},{10,... | collective-permute-start | bytes 884744 | tf_op jit(solution)/shard_map/ppermute | solution.py:21
  50.3 12.1 %collective-permute-start.10 = (bf16[128,768]{1,0:T(8,128)(2,1)S(1)}, bf16[128,768]{1,0:T(8,128)(2,1)S(1)}, u32[]{:S(2)}, u32[]{:S(2)}) collective-permute-start(bf16[128,768]{1,0:T(8,128)(2,1)S(1)} %shard_map.210.refs_2_.refs_1_.refs_0_), channel_id=1, source_target_pairs={{0,8},{4,12},{8,0},{12,4},{1,9},{5,13},{9,1},{13,5},{2,10},{6,14},... | collective-permute-start | bytes 589832 | tf_op jit(solution)/shard_map/ppermute | solution.py:21
  71.0 12.8 %collective-permute-start.16 = (bf16[192,768]{1,0:T(8,128)(2,1)S(1)}, bf16[192,768]{1,0:T(8,128)(2,1)S(1)}, u32[]{:S(2)}, u32[]{:S(2)}) collective-permute-start(bf16[192,768]{1,0:T(8,128)(2,1)S(1)} %shard_map.216.refs_0_.refs_3_.refs_5_), channel_id=1, source_target_pairs={{0,2},{1,3},{2,0},{3,1},{4,6},{5,7},{6,4},{7,5},{8,10},{9,11},{10,... | collective-permute-start | bytes 884744 | tf_op jit(solution)/shard_map/ppermute | solution.py:21
  72.6 11.2 %collective-permute-start.15 = (bf16[128,768]{1,0:T(8,128)(2,1)S(1)}, bf16[128,768]{1,0:T(8,128)(2,1)S(1)}, u32[]{:S(2)}, u32[]{:S(2)}) collective-permute-start(bf16[128,768]{1,0:T(8,128)(2,1)S(1)} %shard_map.215.refs_1_), channel_id=1, source_target_pairs={{0,8},{4,12},{8,0},{12,4},{1,9},{5,13},{9,1},{13,5},{2,10},{6,14},... | collective-permute-start | bytes 589832 | tf_op jit(solution)/shard_map/ppermute | solution.py:21
  113.8 11.2 %collective-permute-start.23 = (bf16[128,768]{1,0:T(8,128)(2,1)S(1)}, bf16[128,768]{1,0:T(8,128)(2,1)S(1)}, u32[]{:S(2)}, u32[]{:S(2)}) collective-permute-start(bf16[128,768]{1,0:T(8,128)(2,1)S(1)} %shard_map.223.refs_1_), channel_id=1, source_target_pairs={{0,8},{4,12},{8,0},{12,4},{1,9},{5,13},{9,1},{13,5},{2,10},{6,14},... | collective-permute-start | bytes 589832 | tf_op jit(solution)/shard_map/ppermute | solution.py:21
  135.3 15.5 %collective-permute-start.28 = (bf16[192,768]{1,0:T(8,128)(2,1)S(1)}, bf16[192,768]{1,0:T(8,128)(2,1)S(1)}, u32[]{:S(2)}, u32[]{:S(2)}) collective-permute-start(bf16[192,768]{1,0:T(8,128)(2,1)S(1)} %get-tuple-element.117), channel_id=1, source_target_pairs={{0,2},{1,3},{2,0},{3,1},{4,6},{5,7},{6,4},{7,5},{8,10},{9,11},{10,... | collective-permute-start | bytes 884744 | tf_op jit(solution)/shard_map/ppermute | solution.py:21
  136.9 14.0 %collective-permute-start.27 = (bf16[128,768]{1,0:T(8,128)(2,1)S(1)}, bf16[128,768]{1,0:T(8,128)(2,1)S(1)}, u32[]{:S(2)}, u32[]{:S(2)}) collective-permute-start(bf16[128,768]{1,0:T(8,128)(2,1)S(1)} %shard_map.226.refs_2_.refs_0_), channel_id=1, source_target_pairs={{0,8},{4,12},{8,0},{12,4},{1,9},{5,13},{9,1},{13,5},{2,10},{6,14},... | collective-permute-start | bytes 589832 | tf_op jit(solution)/shard_map/ppermute | solution.py:21
  136.9 14.0 %collective-permute-start.24 = (bf16[128,192]{1,0:T(8,128)(2,1)S(1)}, bf16[128,192]{1,0:T(8,128)(2,1)S(1)}, u32[]{:S(2)}, u32[]{:S(2)}) collective-permute-start(bf16[128,192]{1,0:T(8,128)(2,1)S(1)} %get-tuple-element.106), channel_id=1, source_target_pairs={{0,0},{1,4},{2,8},{3,12},{4,1},{5,5},{6,9},{7,13},{8,2},{9,6},{10,... | collective-permute-start | bytes 147464 | tf_op jit(solution)/shard_map/ppermute | solution.py:27
  163.1 13.2 %collective-permute-start.33 = (bf16[192,768]{1,0:T(8,128)(2,1)S(1)}, bf16[192,768]{1,0:T(8,128)(2,1)S(1)}, u32[]{:S(2)}, u32[]{:S(2)}) collective-permute-start(bf16[192,768]{1,0:T(8,128)(2,1)S(1)} %get-tuple-element.128), channel_id=1, source_target_pairs={{0,2},{1,3},{2,0},{3,1},{4,6},{5,7},{6,4},{7,5},{8,10},{9,11},{10,... | collective-permute-start | bytes 884744 | tf_op jit(solution)/shard_map/ppermute | solution.py:21
  163.5 12.8 %collective-permute-start.34 = (bf16[192,768]{1,0:T(8,128)(2,1)S(1)}, bf16[192,768]{1,0:T(8,128)(2,1)S(1)}, u32[]{:S(2)}, u32[]{:S(2)}) collective-permute-start(bf16[192,768]{1,0:T(8,128)(2,1)S(1)} %shard_map.233.refs_4_), channel_id=1, source_target_pairs={{0,16},{16,0},{1,17},{17,1},{2,18},{18,2},{3,19},{19,3},{4,20},{20... | collective-permute-start | bytes 884744 | tf_op jit(solution)/shard_map/ppermute | solution.py:21
  165.1 11.2 %collective-permute-start.32 = (bf16[128,768]{1,0:T(8,128)(2,1)S(1)}, bf16[128,768]{1,0:T(8,128)(2,1)S(1)}, u32[]{:S(2)}, u32[]{:S(2)}) collective-permute-start(bf16[128,768]{1,0:T(8,128)(2,1)S(1)} %shard_map.231.refs_2_.refs_0_), channel_id=1, source_target_pairs={{0,8},{4,12},{8,0},{12,4},{1,9},{5,13},{9,1},{13,5},{2,10},{6,14},... | collective-permute-start | bytes 589832 | tf_op jit(solution)/shard_map/ppermute | solution.py:21
  188.1 12.2 %collective-permute-start.39 = (bf16[192,768]{1,0:T(8,128)(2,1)S(1)}, bf16[192,768]{1,0:T(8,128)(2,1)S(1)}, u32[]{:S(2)}, u32[]{:S(2)}) collective-permute-start(bf16[192,768]{1,0:T(8,128)(2,1)S(1)} %get-tuple-element.141), channel_id=1, source_target_pairs={{0,2},{1,3},{2,0},{3,1},{4,6},{5,7},{6,4},{7,5},{8,10},{9,11},{10,... | collective-permute-start | bytes 884744 | tf_op jit(solution)/shard_map/ppermute | solution.py:21
  189.8 10.5 %collective-permute-start.40 = (bf16[192,768]{1,0:T(8,128)(2,1)S(1)}, bf16[192,768]{1,0:T(8,128)(2,1)S(1)}, u32[]{:S(2)}, u32[]{:S(2)}) collective-permute-start(bf16[192,768]{1,0:T(8,128)(2,1)S(1)} %shard_map.239.refs_2_), channel_id=1, source_target_pairs={{0,16},{16,0},{1,17},{17,1},{2,18},{18,2},{3,19},{19,3},{4,20},{20... | collective-permute-start | bytes 884744 | tf_op jit(solution)/shard_map/ppermute | solution.py:21
  205.8 10.4 %collective-permute-start.47 = (bf16[208,768]{1,0:T(8,128)(2,1)S(1)}, bf16[208,768]{1,0:T(8,128)(2,1)S(1)}, u32[]{:S(2)}, u32[]{:S(2)}) collective-permute-start(bf16[208,768]{1,0:T(8,128)(2,1)S(1)} %get-tuple-element.161), channel_id=1, source_target_pairs={{0,2},{1,3},{2,0},{3,1},{4,6},{5,7},{6,4},{7,5},{8,10},{9,11},{10,... | collective-permute-start | bytes 958472 | tf_op jit(solution)/shard_map/ppermute | solution.py:21
  206.4 15.4 %collective-permute-start.44 = (bf16[192,768]{1,0:T(8,128)(2,1)S(1)}, bf16[192,768]{1,0:T(8,128)(2,1)S(1)}, u32[]{:S(2)}, u32[]{:S(2)}) collective-permute-start(bf16[192,768]{1,0:T(8,128)(2,1)S(1)} %shard_map.241), channel_id=1, source_target_pairs={{0,2},{1,3},{2,0},{3,1},{4,6},{5,7},{6,4},{7,5},{8,10},{9,11},{10,... | collective-permute-start | bytes 884744 | tf_op jit(solution)/shard_map/ppermute | solution.py:21
  208.1 35.6 %collective-permute-start.49 = (bf16[192,768]{1,0:T(8,128)(2,1)S(1)}, bf16[192,768]{1,0:T(8,128)(2,1)S(1)}, u32[]{:S(2)}, u32[]{:S(2)}) collective-permute-start(bf16[192,768]{1,0:T(8,128)(2,1)S(1)} %shard_map.247.refs_0_), channel_id=1, source_target_pairs={{0,16},{16,0},{1,17},{17,1},{2,18},{18,2},{3,19},{19,3},{4,20},{20... | collective-permute-start | bytes 884744 | tf_op jit(solution)/shard_map/ppermute | solution.py:21
  216.3 29.8 %collective-permute-start.48 = (bf16[208,768]{1,0:T(8,128)(2,1)S(1)}, bf16[208,768]{1,0:T(8,128)(2,1)S(1)}, u32[]{:S(2)}, u32[]{:S(2)}) collective-permute-start(bf16[208,768]{1,0:T(8,128)(2,1)S(1)} %shard_map.245.refs_0_), channel_id=1, source_target_pairs={{0,16},{16,0},{1,17},{17,1},{2,18},{18,2},{3,19},{19,3},{4,20},{20... | collective-permute-start | bytes 958472 | tf_op jit(solution)/shard_map/ppermute | solution.py:21
  221.8 21.8 %collective-permute-start.50 = (bf16[192,768]{1,0:T(8,128)(2,1)S(1)}, bf16[192,768]{1,0:T(8,128)(2,1)}, u32[]{:S(2)}, u32[]{:S(2)}) collective-permute-start(bf16[192,768]{1,0:T(8,128)(2,1)S(1)} %shard_map.248.refs_2_), channel_id=1, source_target_pairs={{0,16},{16,0},{1,17},{17,1},{2,18},{18,2},{3,19},{19,3},{4,20},{20... | collective-permute-start | bytes 884744 | tf_op jit(solution)/shard_map/ppermute | solution.py:21
  (37 other events, 253.9 us)

commit v3 on v2

--- a/solution.py
+++ b/solution.py
@@ -21,9 +21,9 @@
     return lax.ppermute(x, axis, [(i, i ^ bit) for i in range(n)])
 
 
-def turned(x, bit):
+def turned(x):
     n = lax.axis_size("row")
-    pairs = [(a * n + b, (b ^ bit) * n + a) for a in range(n) for b in range(n)]
+    pairs = [(a * n + b, b * n + a) for a in range(n) for b in range(n)]
     return lax.ppermute(x, ("row", "col"), pairs)
 
 
@@ -43,7 +43,7 @@
     return (array, array.shape, (0,) * array.ndim)
 
 
-def call(kernel, outs, ins, scratch=(), after=(), final=False):
+def call(kernel, outs, ins, scratch=(), after=(), final=False, vmem_mib=32):
     vmem = pl.BlockSpec(memory_space=pltpu.VMEM)
     specs, args = [], []
     moved = 0
@@ -54,6 +54,10 @@
             moved += math.prod(shape) * array.dtype.itemsize
             args.append(array)
             continue
+        if isinstance(item, list):
+            args.append(item[0])
+            specs.append(pl.BlockSpec(memory_space=pltpu.HBM))
+            continue
         args.append(item)
         if item.dtype == jnp.int32:
             specs.append(pl.BlockSpec(memory_space=pltpu.SMEM))
@@ -76,11 +80,13 @@
         out_shape=outs,
         in_specs=specs + [pl.BlockSpec(memory_space=pl.ANY)] * n_after,
         out_specs=[
-            pl.BlockSpec(o.shape, lambda i, d=len(o.shape): (0,) * d) if final else vmem
+            pl.BlockSpec(o.shape, lambda i, d=len(o.shape): (0,) * d)
+            if final
+            else vmem
             for o in outs
         ],
         scratch_shapes=list(scratch),
-        compiler_params=pltpu.CompilerParams(vmem_limit_bytes=32 * 1024 * 1024),
+        compiler_params=pltpu.CompilerParams(vmem_limit_bytes=vmem_mib * 1024 * 1024),
         cost_estimate=pl.CostEstimate(
             flops=200_000_000, bytes_accessed=moved, transcendentals=0
         ),
@@ -239,10 +245,20 @@
 
 
 def k_start(ins, outs, scr):
-    w, b_out, b_down, gain, shift, b_up, b_qv, hidden_in, cotangent = ins
-    block, rowwise, pair = outs
-    rows, piece = w.shape[1], b_out.shape[1]
-    block[:rows, :] = w[0]
+    attn, hidden_in, small = ins[0], ins[1], scr[:-1]
+    block, rowwise, x = outs
+    fetched = [
+        pltpu.make_async_copy(a, b, scr[-1].at[i]) for i, (a, b) in enumerate(zip(ins[2:], small))
+    ]
+    for copy in fetched:
+        copy.start()
+    rows = attn.shape[1]
+    block[:rows, :] = attn[0]
+    x[...] = hidden_in[...].astype(F32).T.astype(BF16)
+    for copy in fetched:
+        copy.wait()
+    b_out, b_down, gain, shift, b_up, b_qv = small
+    piece = b_out.shape[1]
     norms = [b_out[...], b_down[...], gain[0], gain[1], shift[0], shift[1]]
     norms = jnp.concatenate([x.astype(F32) for x in norms] + [jnp.zeros((4, piece), F32)], axis=0)
     block[rows:, :piece] = norms.astype(BF16)
@@ -253,9 +269,6 @@
     qv = jnp.concatenate([jnp.concatenate(qv, axis=0), jnp.zeros((2, rest), F32)], axis=1)
     low = jnp.concatenate([b_up[...].astype(F32), qv, jnp.zeros((12, b_up.shape[1]), F32)], axis=0)
     rowwise[...] = low.astype(BF16)
-    tokens = hidden_in.shape[0]
-    pair[:tokens, :] = hidden_in[...]
-    pair[tokens:, :] = cotangent[...]
 
 
 def k_pack(ins, outs, scr):
@@ -266,11 +279,13 @@
         at += value.shape[0]
 
 
+def k_turned(ins, outs, scr):
+    outs[0][...] = ins[0][...].astype(F32).T.astype(BF16)
+
+
 def k_prep(ins, outs, scr):
     sc, *pieces = ins
-    tokens = outs[0].shape[0]
-    place_features(sc, [p.at[:tokens] for p in pieces], outs[0])
-    place_features(sc, [p.at[tokens:] for p in pieces], outs[1])
+    place_features(sc, pieces, outs[0])
 
 
 def k_sum(ins, outs, scr):
@@ -349,7 +364,8 @@
     h = get_unit(unit_ref)[0] * gain + shift
     bias, gain, shift = params_of(prm, layer, 1)
     unit, r = norm_of(h + (f32(f) + f32(f_other) + bias))
-    pick_features(sc[0] ^ sc[1], m, unit * gain + shift, outs[0])
+    pick_features(sc[0] ^ sc[1], m, unit * gain + shift, scr[0])
+    outs[0][...] = scr[0][...].T.astype(BF16)
     feed_back(f32(cotan), unit, r, gain, ws, slope, outs[1:])
 
 
@@ -403,7 +419,7 @@
 
 
 def k_total(ins, outs, scr):
-    outs[0][...] = ins[0][...] + ((f32(ins[1]) + f32(ins[2])) + f32(ins[3]))
+    outs[0][...] = (ins[0][...] + ((f32(ins[1]) + f32(ins[2])) + f32(ins[3]))).T
 
 
 def k_feed_weight(m, ins, outs, scr):
@@ -454,20 +470,28 @@
 def k_middle(ins, outs, scr):
     keep, got = ins
     total = f32(keep) + f32(got)
-    rows = outs[0].shape[0]
-    for i, out in enumerate(outs):
-        out[...] = total[i * rows : (i + 1) * rows].astype(BF16)
+    at = 0
+    for out in outs:
+        out[...] = total[at : at + out.shape[0]].astype(BF16)
+        at += out.shape[0]
 
 
 def k_add(ins, outs, scr):
-    outs[0][...] = (f32(ins[0]) + f32(ins[1])).astype(outs[0].dtype)
+    count = len(ins) // 2
+    at = 0
+    for first, second in zip(ins[:count], ins[count:]):
+        rows = first.shape[0]
+        outs[0][at : at + rows, :] = (f32(first) + f32(second)).astype(BF16)
+        at += rows
 
 
 def k_feed_outputs(ins, outs, scr):
-    for i, out in enumerate(outs):
-        for layer in range(2):
-            at = 4 * layer + 2 * i
-            out[layer] = f32(ins[at]) + f32(ins[at + 1])
+    half = ins[0].shape[0]
+    for layer in range(2):
+        for i, out in enumerate(outs):
+            for j in range(2):
+                at = 4 * layer + 2 * i + j
+                out[layer, j * half : (j + 1) * half, :] = f32(ins[at]) + f32(ins[8 + at])
 
 
 def k_attend_outputs(ins, outs, scr):
@@ -475,7 +499,9 @@
     piece = grad_w.shape[1]
     total = f32(ins[0]) + f32(ins[1])
     grad_w[0] = total[:piece]
-    grad_w[1] = f32(ins[2]) + f32(ins[3])
+    half = piece // 2
+    grad_w[1, :half, :] = f32(ins[2]) + f32(ins[4])
+    grad_w[1, half:, :] = f32(ins[3]) + f32(ins[5])
     small = total[piece:]
     b_up[...] = small[0:2]
     for layer in range(2):
@@ -510,23 +536,29 @@
     def layer_of(array, layer):
         return (array, (1,) + array.shape[1:], (layer, 0, 0))
 
+    half_block = sds((piece // 2, hidden), BF16)
+
     def pack(rows, arrays, after=()):
         return call(k_pack, [sds((rows, hidden), BF16)], arrays, after=after, final=True)[0]
 
-    def held(array, after):
-        return pack(array.shape[0], [whole(array)], after)
-
-    def blocks(own, along, near, rows=piece):
-        views = [(own, 0), (near, 0), (along, 0), (near, 1)]
+    def held(arrays, after):
+        return [
+            call(k_pack, [sds(a.shape, a.dtype)], [whole(a)], after=after, final=True)[0]
+            for a in arrays
+        ]
+
+    def along_of(arrays):
+        return [exchange(a, "col", 2) for a in arrays]
+
+    def half_of(array, layer, which, after):
+        view = (array, (1, piece // 2, hidden), (layer, which, 0))
+        return pack(piece // 2, [view], after)
+
+    def gathered(own, along, rows=piece, after=()):
+        both = pack(2 * rows, [whole(a) for a in [*own, *along]], after)
+        near = exchange(both, "col", 1)
+        views = [(both, 0), (near, 0), (both, 1), (near, 1)]
         return [(a, (rows, hidden), (i, 0)) for a, i in views]
-
-    def near_of(own, along, after=()):
-        both = pack(2 * own.shape[0], [whole(own), whole(along)], after)
-        return exchange(both, "col", 1)
-
-    def sent(array, layer, after):
-        own = pack(piece, [layer_of(array, layer)], after)
-        return own, exchange(own, "col", 2)
 
     def pair_sum(value, after=()):
         return call(k_sum, [low_tile], [value, exchange(value, "row", 1)], after=after)[0]
@@ -534,22 +566,24 @@
     def both(value):
         return [value, exchange(value, "row", 2)]
 
-    block, rowwise, pair = call(
+    smalls = [b_out, b_down, ln_gain, ln_bias, b_up, b_qv]
+    block, rowwise, mine = call(
         k_start,
-        [sds((piece + 16, hidden), BF16), sds((16, hidden), BF16), sds((2 * tokens, piece), BF16)],
-        [
-            layer_of(w_attn, 0),
-            *map(whole, (b_out, b_down, ln_gain, ln_bias, b_up, b_qv, hidden_in, cotangent)),
-        ],
+        [sds((piece + 16, hidden), BF16), sds((16, hidden), BF16), sds((tokens, piece), BF16)],
+        [layer_of(w_attn, 0), whole(hidden_in.T), *[[a] for a in smalls]],
+        [pltpu.VMEM(a.shape, a.dtype) for a in smalls] + [pltpu.SemaphoreType.DMA((6,))],
+        final=True,
+        vmem_mib=60,
     )
     along = exchange(block, "col", 2)
-    x_in = [turned(pair, k) for k in range(n)]
-    x, cotan = call(k_prep, [sds(tile, BF16)] * 2, [sc, *x_in])
-    near = near_of(block, along, [x])
-    up0, up0_along = sent(w_up, 0, [x])
+    mine = turned(mine)
+    x_in = [mine] + [exchange(mine, "row", k) for k in range(1, n)]
+    (x,) = call(k_prep, [sds(tile, BF16)], [sc, *x_in])
+    up0 = pack(piece, [layer_of(w_up, 0)], [mine])
+    (up0_along,) = along_of([up0])
+    attn0 = gathered([block], [along], piece + 16, [*x_in[1:], up0_along])
 
     low_tile = sds(tile, BF16)
-    low_block, low_tail = sds((piece, hidden), BF16), sds((piece + 16, hidden), BF16)
     unit_out = sds((tokens, model + 128), F32)
     qkv_out, p_out, o_out = (
         sds((tokens, 3 * width), BF16),
@@ -559,69 +593,78 @@
     g_out, slope_out = sds((tokens, hidden), BF16), sds((tokens, hidden), F32)
     feed_out = [low_tile, unit_out, low_tile, g_out, slope_out]
 
-    attn0 = blocks(block, along, near, piece + 16)
     z, prm, o0, qkv0, p0 = call(
         partial(k_attend_first, m),
         [low_tile, sds((16, model), F32), o_out, qkv_out, p_out],
         [sc, x, *attn0, rowwise],
-        after=[up0_along],
-    )
-    down0, down0_along = sent(w_down, 0, [z])
-    up0_near = near_of(up0, up0_along, [z])
-    z = pair_sum(z, [down0_along, up0_near])
-    down0_near = near_of(down0, down0_along, [z])
-    attn1, attn1_along = sent(w_attn, 1, [z])
-    up0 = blocks(up0, up0_along, up0_near)
-    down0 = blocks(down0, down0_along, down0_near)
+    )
+    down0 = [half_of(w_down, 0, i, [z]) for i in range(2)]
+    down0_along = along_of(down0)
+    z = pair_sum(z, down0_along)
+    up0 = gathered([up0], [up0_along], after=[z])
+    down0 = gathered(down0, down0_along, after=[z])
+    attn1 = [half_of(w_attn, 1, i, [z]) for i in range(2)]
+    attn1_along = along_of(attn1)
     f, unit_a0, h0, g0, slope0 = call(
         partial(k_feed, m, 0),
         feed_out,
         [*both(z), x, *up0, *down0, rowwise, prm],
-        after=[attn1_along],
-    )
-    attn1_near = near_of(attn1, attn1_along, [f])
-    attn1 = blocks(attn1, attn1_along, attn1_near)
-    f = pair_sum(f, [attn1_near])
-    up1, up1_along = sent(w_up, 1, [f])
+        after=attn1_along,
+    )
+    attn1 = gathered(attn1, attn1_along, after=[f])
+    up1 = [half_of(w_up, 1, 0, [f])]
+    up1_along = along_of(up1)
+    f = pair_sum(f, [attn1[1][0], *up1_along])
+    up1 += [half_of(w_up, 1, 1, [f])]
+    up1_along += along_of(up1[1:])
+    down1 = [half_of(w_down, 1, 0, [f])]
+    down1_along = along_of(down1)
     z, unit_b0, x1, o1, qkv1, p1 = call(
         partial(k_attend, m, 1),
         [low_tile, unit_out, low_tile, o_out, qkv_out, p_out],
         [sc, *both(f), unit_a0, *attn1, rowwise, prm],
-        after=[up1_along],
-    )
-    down1, down1_along = sent(w_down, 1, [z])
-    up1_near = near_of(up1, up1_along, [z])
-    z = pair_sum(z, [down1_along, up1_near])
-    down1_near = near_of(down1, down1_along, [z])
-    up1 = blocks(up1, up1_along, up1_near)
-    down1 = blocks(down1, down1_along, down1_near)
+        after=[up1_along[1], *down1_along],
+    )
+    down1 += [half_of(w_down, 1, 1, [z])]
+    down1_along += along_of(down1[1:])
+    up1 = gathered(up1, up1_along, after=[z])
+    z = pair_sum(z, [down1_along[1], up1[1][0]])
+    down1 = gathered(down1, down1_along, after=[z])
+    (low,) = call(k_turned, [sds((tokens, piece), BF16)], [whole(cotangent.T)], after=[z], final=True)
+    cotan = turned(low)
     f, unit_a1, h1, g1, slope1 = call(
         partial(k_feed, m, 1),
         feed_out,
         [*both(z), unit_b0, *up1, *down1, rowwise, prm],
-    )
+        after=[cotan],
+    )
+    cotan = [cotan, *held([cotan], [f])]
+    cotan = [cotan[0]] + [exchange(cotan[1], "row", k) for k in range(1, n)]
+    f = pair_sum(f, cotan[1:])
+    (cotan,) = call(k_prep, [sds(tile, BF16)], [sc, *cotan], after=[f])
 
     sums_out = sds((8, model), F32)
     feed_back_out = [sds(tile, F32), low_tile, low_tile, sds((tokens, hidden), BF16), sums_out]
     out, df, df_low, dh, du, sums_b1 = call(
         partial(k_turn, m, 1),
-        [sds((tokens, piece), BF16)] + feed_back_out,
-        [sc, *both(pair_sum(f)), unit_a1, cotan, *up1, *down1, slope1, prm],
-    )
-    out_hidden = turned(out, 0)
+        [sds((piece, tokens), BF16)] + feed_back_out,
+        [sc, *both(f), unit_a1, cotan, *up1, *down1, slope1, prm],
+        [pltpu.VMEM((tokens, piece), F32)],
+    )
+    out_hidden = turned(out)
     weight_out = [sds((4 * piece, hidden), BF16)] * 2 + [sds((8, hidden), F32)]
     keep, send, hidden_sums1 = call(
         partial(k_feed_weight, m), weight_out, [df_low, g1, h1, du]
     )
     got = exchange(send, "col", 1)
     dh = pair_sum(dh, [got])
-    down1_stay, up1_stay, down1_go, up1_go = call(k_middle, [low_block] * 4, [keep, got], after=[dh])
-    down1_more = exchange(down1_go, "col", 2)
+    stay1 = call(k_middle, [half_block] * 8, [keep, got], after=[dh])
+    more1 = along_of(stay1[4:6])
     da, da_low, dx, grads1, sums_a1 = call(
         partial(k_attend_back, m, 1),
         [sds(tile, F32), low_tile, low_tile, qkv_out, sums_out],
         [*both(dh), df, unit_a1, *attn1, qkv1, p1, prm],
-        after=[down1_more, out_hidden],
+        after=more1,
     )
     keep, send, head_sums1 = call(
         partial(k_attend_weight, m),
@@ -629,46 +672,56 @@
         [x1, grads1, da_low, o1],
     )
     got = exchange(send, "col", 1)
-    up1_more = exchange(held(up1_go, [dx]), "col", 2)
-    dx = pair_sum(dx, [got, up1_more])
-    attn1_stay, attn1_go = call(k_middle, [low_block] * 2, [keep, got], after=[dx])
-    attn1_more = exchange(attn1_go, "col", 2)
-    (down1_low,) = call(k_add, [low_block], [down1_stay, down1_more], after=[dx])
-    down1_terms = last_of_dp(down1_low)
+    more1 += along_of(held(stay1[6:7], [dx]))
+    (low,) = call(k_add, [half_block], [stay1[0], more1[0]], after=[dx])
+    terms1 = [last_of_dp(low)]
+    dx = pair_sum(dx, [got, more1[2], terms1[0][1]])
+    (out_hidden,) = held([out_hidden], [dx])
+    attn1_stay = call(k_middle, [half_block] * 4, [keep, got], after=[dx])
+    more1 += along_of(held(stay1[7:], [dx]))
+    attn1_more = along_of(attn1_stay[2:3])
+    for i in (1, 2):
+        (low,) = call(k_add, [half_block], [stay1[i], more1[i]], after=[dx])
+        terms1 += [last_of_dp(low)]
 
     df, df_low, dh, du, sums_b0 = call(
         partial(k_feed_back, m, 0),
         feed_back_out,
         [*both(dx), da, unit_b0, *up0, *down0, slope0, prm],
-        after=[attn1_more, down1_terms[1]],
+        after=[more1[3], *attn1_more, terms1[1][1], terms1[2][1], out_hidden],
     )
     keep, send, hidden_sums0 = call(
         partial(k_feed_weight, m), weight_out, [df_low, g0, h0, du]
     )
     got = exchange(send, "col", 1)
-    (up1_low,) = call(k_add, [low_block], [up1_stay, up1_more], after=[dh])
-    up1_terms = last_of_dp(up1_low)
-    dh = pair_sum(dh, [got, up1_terms[1]])
-    down0_stay, up0_stay, down0_go, up0_go = call(k_middle, [low_block] * 4, [keep, got], after=[dh])
-    down0_more = exchange(down0_go, "col", 2)
-    (attn1_low,) = call(k_add, [low_block], [attn1_stay, attn1_more], after=[dh])
-    attn1_terms = last_of_dp(attn1_low)
+    attn1_more += along_of(held(attn1_stay[3:], [dh]))
+    (low,) = call(k_add, [half_block], [stay1[3], more1[3]], after=[dh])
+    terms1 += [last_of_dp(low)]
+    (low,) = call(k_add, [half_block], [attn1_stay[0], attn1_more[0]], after=[dh])
+    attn1_terms = [last_of_dp(low)]
+    dh = pair_sum(dh, [got, attn1_more[1], terms1[3][1], attn1_terms[0][1]])
+    stay0 = call(k_middle, [half_block] * 8, [keep, got], after=[dh])
+    more0 = along_of(stay0[4:7])
+    (low,) = call(k_add, [half_block], [attn1_stay[1], attn1_more[1]], after=[dh])
+    attn1_terms += [last_of_dp(low)]
     *dx, low_last, grads0, sums_a0 = call(
         partial(k_attend_back_last, n, m),
         [sds((tokens, piece), F32)]
         + [sds((tokens, piece), BF16)] * (n - 1)
         + [low_tile, qkv_out, sums_out],
         [sc, *both(dh), df, unit_a0, *attn0, qkv0, p0, prm],
-        after=[down0_more, attn1_terms[1]],
-    )
-    up0_more = exchange(held(up0_go, [dx[0]]), "col", 2)
-    (grad_input,) = call(
+        after=[*more0, attn1_terms[1][1]],
+    )
+    more0 += along_of(held(stay0[7:], [dx[0]]))
+    most = [sds((3 * piece // 2, hidden), BF16)]
+    (low,) = call(k_add, most, [*stay0[:3], *more0[:3]])
+    most0_terms = last_of_dp(low)
+    (grad_total,) = call(
         k_total,
-        [sds((tokens, piece), F32)],
+        [sds((piece, tokens), F32)],
         [dx[0]] + [exchange(dx[k], "row", k) for k in range(1, n)],
-        after=[up0_more],
-    )
-    grad_input = turned(grad_input, 0)
+    )
+    grad_input = turned(grad_total)
 
     keep, send = call(
         partial(k_attend_weight_last, m),
@@ -688,17 +741,23 @@
         ],
     )
     got = exchange(send, "col", 1)
+    low_tail = sds((piece + 16, hidden), BF16)
     attn0_stay, attn0_go = call(k_middle, [low_tail] * 2, [keep, got])
-    (down0_low,) = call(k_add, [low_block], [down0_stay, down0_more])
-    down0_terms = last_of_dp(down0_low)
-    (up0_low,) = call(k_add, [low_block], [up0_stay, up0_more])
-    up0_terms = last_of_dp(up0_low)
-    (attn0_low,) = call(k_add, [low_tail], [attn0_stay, exchange(attn0_go, "col", 2)])
-    attn0_terms = last_of_dp(attn0_low)
+    (attn0_more,) = along_of([attn0_go])
+    (low,) = call(k_add, [half_block], [stay0[3], more0[3]], after=[grad_total])
+    rest0_terms = last_of_dp(low)
+    (low,) = call(k_add, [low_tail], [attn0_stay, attn0_more])
+    attn0_terms = [last_of_dp(low)]
+    def halves_of(array):
+        return [(array, (piece // 2, hidden), (i, 0)) for i in range(3)]
+
+    first = [halves_of(a) + [b] for a, b in zip(most0_terms, rest0_terms)]
+    second = [[t[side] for t in terms1] for side in range(2)]
     grad_down, grad_up = call(
         k_feed_outputs,
         [sds((layers, piece, hidden), F32)] * 2,
-        [*down0_terms, *up0_terms, *down1_terms, *up1_terms],
+        [*first[0], *second[0], *first[1], *second[1]],
+        after=[grad_input],
         final=True,
     )
     grad_attn, grad_qv, grad_out, grad_gain, grad_shift, grad_b_up, grad_b_down = call(
@@ -712,12 +771,12 @@
             sds(b_up.shape, F32),
             sds(b_down.shape, F32),
         ],
-        [*attn0_terms, *attn1_terms],
+        [t[side] for terms in (attn0_terms, attn1_terms) for side in range(2) for t in terms],
         final=True,
     )
     return (
-        out_hidden,
-        grad_input,
+        out_hidden.T,
+        grad_input.T,
         grad_attn,
         grad_qv,
         grad_out,

time: 248 us -> 231 us (0.931)
  waiting for transfers between devices: 172 us -> 128 us
  starting transfers between devices: 40.1 us -> 71.1 us
  local copies, waits for them, and re-layouts: 11.5 us -> 5.02 us
  Pallas kernels: 22.3 us -> 25.3 us
    ppermute x45 -> x63, waiting for transfers between devices: 148 us -> 104 us  [exchange(): return lax.ppermute(x, axis, [(i, i ^ bit) for i in range(n)])]
    ppermute x45 -> x63, starting transfers between devices: 23.1 us -> 54.9 us  [exchange(): return lax.ppermute(x, axis, [(i, i ^ bit) for i in range(n)])]
    unnamed x24 -> x19, local copies, waits for them, and re-layouts: 10.2 us -> 4.43 us
    pallas_call x47 -> x60, Pallas kernels: 22.3 us -> 25.3 us  [call(): pl.pallas_call(body, grid=(1,), out_shape=outs, in_specs=specs + [pl.Bloc...]
    ppermute x6 -> x4, starting transfers between devices: 17 us -> 16.2 us  [turned(): return lax.ppermute(x, ('row', 'col'), pairs)]
    ppermute x6 -> x4, waiting for transfers between devices: 23.2 us -> 24 us  [turned(): return lax.ppermute(x, ('row', 'col'), pairs)]
  transfers between devices with their start and end apart: 51 -> 67, of which waited for: 28 -> 40; matrix products, arithmetic and copies ran while one was open for 2% -> 1% of each run, Pallas kernels for 2% -> 2%
where the time goes in v3:
time: 231 us
  waiting for transfers between devices  128 us (55%)
  starting transfers between devices  71.1 us (31%)
  Pallas kernels  25.3 us (11%)
  local copies, waits for them, and re-layouts  5.02 us (2%)
    ppermute x63, waiting for transfers between devices, exchange(): return lax.ppermute(x, axis, [(i, i ^ bit) for i in range(n)])  104 us
    ppermute x63, starting transfers between devices, exchange(): return lax.ppermute(x, axis, [(i, i ^ bit) for i in range(n)])  54.9 us
    pallas_call x60, Pallas kernels, call(): pl.pallas_call(body, grid=(1,), out_shape=outs, in_specs=specs + [pl.Bloc...  25.3 us
    ppermute x4, waiting for transfers between devices, turned(): return lax.ppermute(x, ('row', 'col'), pairs)  24 us
    ppermute x4, starting transfers between devices, turned(): return lax.ppermute(x, ('row', 'col'), pairs)  16.2 us
  transfers between devices with their start and end apart: 67, of which 40 were waited for; matrix products, arithmetic and copies ran while one was open for 1% of the time, Pallas kernels for 2%

profile of v3, /device:TPU:2, one launch (start us, length us, event | category | flops | bytes accessed | tf_op | source)
XLA Modules:
  0.0 230.9 jit_solution(8165177685542954995)
XLA Ops:
  3.2 4.5 %collective-permute-start = (bf16[128,192]{1,0:T(8,128)(2,1)}, bf16[128,192]{1,0:T(8,128)(2,1)S(1)}, u32[]{:S(2)}, u32[]{:S(2)}) collective-permute-start(bf16[128,192]{1,0:T(8,128)(2,1)} %get-tuple-element.100), channel_id=1, source_target_pairs={{0,0},{1,4},{2,8},{3,12},{4,1},{5,5},{6,9},{7,13},{8,2},{9,6},{10,... | collective-permute-start | bytes 147464 | tf_op jit(solution)/shard_map/ppermute | solution.py:27
  7.8 5.3 %collective-permute-done.refs_1_ = bf16[128,192]{1,0:T(8,128)(2,1)S(1)} collective-permute-done((bf16[128,192]{1,0:T(8,128)(2,1)}, bf16[128,192]{1,0:T(8,128)(2,1)S(1)}, u32[]{:S(2)}, u32[]{:S(2)}) %collective-permute-start) | collective-permute-done | bytes 49184 | tf_op jit(solution)/shard_map/ppermute | solution.py:27
  14.2 3.1 %collective-permute-start.3 = (bf16[128,192]{1,0:T(8,128)(2,1)S(1)}, bf16[128,192]{1,0:T(8,128)(2,1)S(1)}, u32[]{:S(2)}, u32[]{:S(2)}) collective-permute-start(bf16[128,192]{1,0:T(8,128)(2,1)S(1)} %collective-permute-done.refs_1_), channel_id=1, source_target_pairs={{0,12},{4,8},{8,4},{12,0},{1,13},{5,9},{9,5},{13,1},{2,14},{6,10},... | collective-permute-start | bytes 147464 | tf_op jit(solution)/shard_map/ppermute | solution.py:21
  22.5 3.3 %collective-permute-done.5.refs_5_.refs_1_ = bf16[192,768]{1,0:T(8,128)(2,1)S(1)} collective-permute-done((bf16[192,768]{1,0:T(8,128)(2,1)S(1)}, bf16[192,768]{1,0:T(8,128)(2,1)S(1)}, u32[]{:S(2)}, u32[]{:S(2)}) %collective-permute-start.5) | collective-permute-done | bytes 294944 | tf_op jit(solution)/shard_map/ppermute | solution.py:21
  33.0 4.6 %collective-permute-done.8.refs_2_ = bf16[96,768]{1,0:T(8,128)(2,1)S(1)} collective-permute-done((bf16[96,768]{1,0:T(8,128)(2,1)S(1)}, bf16[96,768]{1,0:T(8,128)(2,1)S(1)}, u32[]{:S(2)}, u32[]{:S(2)}) %collective-permute-start.8) | collective-permute-done | bytes 147488 | tf_op jit(solution)/shard_map/ppermute | solution.py:21
  43.5 4.7 %collective-permute-done.13.refs_13_.refs_2_ = bf16[96,768]{1,0:T(8,128)(2,1)S(1)} collective-permute-done((bf16[96,768]{1,0:T(8,128)(2,1)S(1)}, bf16[96,768]{1,0:T(8,128)(2,1)S(1)}, u32[]{:S(2)}, u32[]{:S(2)}) %collective-permute-start.13) | collective-permute-done | bytes 147488 | tf_op jit(solution)/shard_map/ppermute | solution.py:21
  55.5 5.1 %collective-permute-done.17.refs_3_.refs_2_ = bf16[96,768]{1,0:T(8,128)(2,1)S(1)} collective-permute-done((bf16[96,768]{1,0:T(8,128)(2,1)S(1)}, bf16[96,768]{1,0:T(8,128)(2,1)S(1)}, u32[]{:S(2)}, u32[]{:S(2)}) %collective-permute-start.17) | collective-permute-done | bytes 147488 | tf_op jit(solution)/shard_map/ppermute | solution.py:21
  64.3 4.5 %collective-permute-done.19.refs_10_.refs_3_ = bf16[96,768]{1,0:T(8,128)(2,1)S(1)} collective-permute-done((bf16[96,768]{1,0:T(8,128)(2,1)S(1)}, bf16[96,768]{1,0:T(8,128)(2,1)S(1)}, u32[]{:S(2)}, u32[]{:S(2)}) %collective-permute-start.19) | collective-permute-done | bytes 147488 | tf_op jit(solution)/shard_map/ppermute | solution.py:21
  75.7 5.9 %collective-permute-done.22.refs_2_.refs_3_ = bf16[96,768]{1,0:T(8,128)(2,1)S(1)} collective-permute-done((bf16[96,768]{1,0:T(8,128)(2,1)S(1)}, bf16[96,768]{1,0:T(8,128)(2,1)S(1)}, u32[]{:S(2)}, u32[]{:S(2)}) %collective-permute-start.22) | collective-permute-done | bytes 147488 | tf_op jit(solution)/shard_map/ppermute | solution.py:21
  83.5 4.0 %collective-permute-start.26 = (bf16[128,192]{1,0:T(8,128)(2,1)S(1)}, bf16[128,192]{1,0:T(8,128)(2,1)S(1)}, u32[]{:S(2)}, u32[]{:S(2)}) collective-permute-start(bf16[128,192]{1,0:T(8,128)(2,1)S(1)} %shard_map.226), channel_id=1, source_target_pairs={{0,0},{1,4},{2,8},{3,12},{4,1},{5,5},{6,9},{7,13},{8,2},{9,6},{10,... | collective-permute-start | bytes 147464 | tf_op jit(solution)/shard_map/ppermute | solution.py:27
  87.4 10.2 %collective-permute-done.26.refs_13_.refs_0_.refs_1_ = bf16[128,192]{1,0:T(8,128)(2,1)S(1)} collective-permute-done((bf16[128,192]{1,0:T(8,128)(2,1)S(1)}, bf16[128,192]{1,0:T(8,128)(2,1)S(1)}, u32[]{:S(2)}, u32[]{:S(2)}) %collective-permute-start.26) | collective-permute-done | bytes 49184 | tf_op jit(solution)/shard_map/ppermute | solution.py:27
  99.3 3.0 %collective-permute-start.29 = (bf16[128,192]{1,0:T(8,128)(2,1)S(1)}, bf16[128,192]{1,0:T(8,128)(2,1)S(1)}, u32[]{:S(2)}, u32[]{:S(2)}) collective-permute-start(bf16[128,192]{1,0:T(8,128)(2,1)S(1)} %shard_map.228), channel_id=1, source_target_pairs={{0,8},{4,12},{8,0},{12,4},{1,9},{5,13},{9,1},{13,5},{2,10},{6,14},... | collective-permute-start | bytes 147464 | tf_op jit(solution)/shard_map/ppermute | solution.py:21
  103.4 3.1 %collective-permute-done.30.refs_4_ = bf16[128,192]{1,0:T(8,128)(2,1)S(1)} collective-permute-done((bf16[128,192]{1,0:T(8,128)(2,1)S(1)}, bf16[128,192]{1,0:T(8,128)(2,1)S(1)}, u32[]{:S(2)}, u32[]{:S(2)}) %collective-permute-start.30) | collective-permute-done | bytes 49184 | tf_op jit(solution)/shard_map/ppermute | solution.py:21
  109.5 7.1 %collective-permute-done.31.refs_2_ = bf16[128,768]{1,0:T(8,128)(2,1)S(1)} collective-permute-done((bf16[128,768]{1,0:T(8,128)(2,1)S(1)}, bf16[128,768]{1,0:T(8,128)(2,1)S(1)}, u32[]{:S(2)}, u32[]{:S(2)}) %collective-permute-start.31) | collective-permute-done | bytes 196640 | tf_op jit(solution)/shard_map/ppermute | solution.py:21
  119.2 7.2 %collective-permute-done.33.refs_1_ = bf16[128,768]{1,0:T(8,128)(2,1)S(1)} collective-permute-done((bf16[128,768]{1,0:T(8,128)(2,1)S(1)}, bf16[128,768]{1,0:T(8,128)(2,1)S(1)}, u32[]{:S(2)}, u32[]{:S(2)}) %collective-permute-start.33) | collective-permute-done | bytes 196640 | tf_op jit(solution)/shard_map/ppermute | solution.py:21
  128.1 3.5 %collective-permute-start.36 = (bf16[96,768]{1,0:T(8,128)(2,1)S(1)}, bf16[96,768]{1,0:T(8,128)(2,1)S(1)}, u32[]{:S(2)}, u32[]{:S(2)}) collective-permute-start(bf16[96,768]{1,0:T(8,128)(2,1)S(1)} %get-tuple-element.123), channel_id=1, source_target_pairs={{0,2},{1,3},{2,0},{3,1},{4,6},{5,7},{6,4},{7,5},{8,10},{9,11},{10,... | collective-permute-start | bytes 442376 | tf_op jit(solution)/shard_map/ppermute | solution.py:21
  131.7 4.6 %collective-permute-done.36.refs_11_.refs_1_ = bf16[96,768]{1,0:T(8,128)(2,1)S(1)} collective-permute-done((bf16[96,768]{1,0:T(8,128)(2,1)S(1)}, bf16[96,768]{1,0:T(8,128)(2,1)S(1)}, u32[]{:S(2)}, u32[]{:S(2)}) %collective-permute-start.36) | collective-permute-done | bytes 147488 | tf_op jit(solution)/shard_map/ppermute | solution.py:21
  146.1 4.2 %collective-permute-start.32 = (bf16[192,128]{1,0:T(8,128)(2,1)S(1)}, bf16[192,128]{1,0:T(8,128)(2,1)S(1)}, u32[]{:S(2)}, u32[]{:S(2)}) collective-permute-start(bf16[192,128]{1,0:T(8,128)(2,1)S(1)} %get-tuple-element.112), channel_id=1, source_target_pairs={{0,0},{1,4},{2,8},{3,12},{4,1},{5,5},{6,9},{7,13},{8,2},{9,6},{10,... | collective-permute-start | bytes 147464 | tf_op jit(solution)/shard_map/ppermute | solution.py:27
  161.4 3.5 %collective-permute-done.46.refs_17_.refs_14_ = bf16[96,768]{1,0:T(8,128)(2,1)S(1)} collective-permute-done((bf16[96,768]{1,0:T(8,128)(2,1)S(1)}, bf16[96,768]{1,0:T(8,128)(2,1)S(1)}, u32[]{:S(2)}, u32[]{:S(2)}) %collective-permute-start.46) | collective-permute-done | bytes 147488 | tf_op jit(solution)/shard_map/ppermute | solution.py:21
  170.5 3.7 %collective-permute-done.49.refs_3_.refs_1_ = bf16[96,768]{1,0:T(8,128)(2,1)S(1)} collective-permute-done((bf16[96,768]{1,0:T(8,128)(2,1)S(1)}, bf16[96,768]{1,0:T(8,128)(2,1)S(1)}, u32[]{:S(2)}, u32[]{:S(2)}) %collective-permute-start.49) | collective-permute-done | bytes 147488 | tf_op jit(solution)/shard_map/ppermute | solution.py:21
  198.5 6.8 %collective-permute-done.62.refs_1_ = bf16[208,768]{1,0:T(8,128)(2,1)S(1)} collective-permute-done((bf16[208,768]{1,0:T(8,128)(2,1)S(1)}, bf16[208,768]{1,0:T(8,128)(2,1)S(1)}, u32[]{:S(2)}, u32[]{:S(2)}) %collective-permute-start.62) | collective-permute-done | bytes 319520 | tf_op jit(solution)/shard_map/ppermute | solution.py:21
  214.7 2.9 %collective-permute-done.59.refs_3_ = bf16[128,192]{1,0:T(8,128)(2,1)S(1)} collective-permute-done((bf16[128,192]{1,0:T(8,128)(2,1)S(1)}, bf16[128,192]{1,0:T(8,128)(2,1)S(1)}, u32[]{:S(2)}, u32[]{:S(2)}) %collective-permute-start.59) | collective-permute-done | bytes 49184 | tf_op jit(solution)/shard_map/ppermute | solution.py:21
  218.2 3.6 %collective-permute-start.60 = (f32[192,128]{1,0:T(8,128)S(1)}, f32[192,128]{1,0:T(8,128)S(1)}, u32[]{:S(2)}, u32[]{:S(2)}) collective-permute-start(f32[192,128]{1,0:T(8,128)S(1)} %shard_map.254.refs_2_), channel_id=1, source_target_pairs={{0,0},{1,4},{2,8},{3,12},{4,1},{5,5},{6,9},{7,13},{8,2},{9,6},{10,... | collective-permute-start | bytes 294920 | tf_op jit(solution)/shard_map/ppermute | solution.py:27
  221.8 5.8 %collective-permute-done.60.refs_16_ = f32[192,128]{1,0:T(8,128)S(1)} collective-permute-done((f32[192,128]{1,0:T(8,128)S(1)}, f32[192,128]{1,0:T(8,128)S(1)}, u32[]{:S(2)}, u32[]{:S(2)}) %collective-permute-start.60) | collective-permute-done | bytes 98336 | tf_op jit(solution)/shard_map/ppermute | solution.py:27
  (191 shorter events, 115.8 us)
Async XLA Ops:
  3.2 9.9 %collective-permute-start = (bf16[128,192]{1,0:T(8,128)(2,1)}, bf16[128,192]{1,0:T(8,128)(2,1)S(1)}, u32[]{:S(2)}, u32[]{:S(2)}) collective-permute-start(bf16[128,192]{1,0:T(8,128)(2,1)} %get-tuple-element.100), channel_id=1, source_target_pairs={{0,0},{1,4},{2,8},{3,12},{4,1},{5,5},{6,9},{7,13},{8,2},{9,6},{10,... | collective-permute-start | bytes 147464 | tf_op jit(solution)/shard_map/ppermute | solution.py:27
  7.7 14.8 %collective-permute-start.4 = (bf16[208,768]{1,0:T(8,128)(2,1)}, bf16[208,768]{1,0:T(8,128)(2,1)S(1)}, u32[]{:S(2)}, u32[]{:S(2)}) collective-permute-start(bf16[208,768]{1,0:T(8,128)(2,1)} %get-tuple-element.101.refs_0_), channel_id=1, source_target_pairs={{0,2},{1,3},{2,0},{3,1},{4,6},{5,7},{6,4},{7,5},{8,10},{9,11},{10,... | collective-permute-start | bytes 958472 | tf_op jit(solution)/shard_map/ppermute | solution.py:21
  14.1 11.6 %collective-permute-start.5 = (bf16[192,768]{1,0:T(8,128)(2,1)S(1)}, bf16[192,768]{1,0:T(8,128)(2,1)S(1)}, u32[]{:S(2)}, u32[]{:S(2)}) collective-permute-start(bf16[192,768]{1,0:T(8,128)(2,1)S(1)} %shard_map.205.refs_0_), channel_id=1, source_target_pairs={{0,2},{1,3},{2,0},{3,1},{4,6},{5,7},{6,4},{7,5},{8,10},{9,11},{10,... | collective-permute-start | bytes 884744 | tf_op jit(solution)/shard_map/ppermute | solution.py:21
  30.7 9.5 %collective-permute-start.7 = (bf16[128,768]{1,0:T(8,128)(2,1)S(1)}, bf16[128,768]{1,0:T(8,128)(2,1)S(1)}, u32[]{:S(2)}, u32[]{:S(2)}) collective-permute-start(bf16[128,768]{1,0:T(8,128)(2,1)S(1)} %get-tuple-element.103.refs_1_.refs_0_), channel_id=1, source_target_pairs={{0,4},{4,0},{8,12},{12,8},{1,5},{5,1},{9,13},{13,9},{2,6},{6,2},{1... | collective-permute-start | bytes 589832 | tf_op jit(solution)/shard_map/ppermute | solution.py:21
  40.4 12.7 %collective-permute-start.11 = (bf16[384,768]{1,0:T(8,128)(2,1)S(1)}, bf16[384,768]{1,0:T(8,128)(2,1)S(1)}, u32[]{:S(2)}, u32[]{:S(2)}) collective-permute-start(bf16[384,768]{1,0:T(8,128)(2,1)S(1)} %shard_map.211.refs_3_.refs_5_.refs_4_.refs_6_), channel_id=1, source_target_pairs={{0,1},{1,0},{2,3},{3,2},{4,5},{5,4},{6,7},{7,6},{8,9},{9,8},{10,11... | collective-permute-start | bytes 1769480 | tf_op jit(solution)/shard_map/ppermute | solution.py:21
  40.5 12.6 %collective-permute-start.12 = (bf16[384,768]{1,0:T(8,128)(2,1)S(1)}, bf16[384,768]{1,0:T(8,128)(2,1)S(1)}, u32[]{:S(2)}, u32[]{:S(2)}) collective-permute-start(bf16[384,768]{1,0:T(8,128)(2,1)S(1)} %shard_map.212.refs_7_.refs_9_.refs_8_.refs_10_), channel_id=1, source_target_pairs={{0,1},{1,0},{2,3},{3,2},{4,5},{5,4},{6,7},{7,6},{8,9},{9,8},{10,11... | collective-permute-start | bytes 1769480 | tf_op jit(solution)/shard_map/ppermute | solution.py:21
  41.1 12.0 %collective-permute-start.10 = (bf16[128,768]{1,0:T(8,128)(2,1)S(1)}, bf16[128,768]{1,0:T(8,128)(2,1)S(1)}, u32[]{:S(2)}, u32[]{:S(2)}) collective-permute-start(bf16[128,768]{1,0:T(8,128)(2,1)S(1)} %shard_map.210.refs_2_.refs_4_.refs_1_.refs_0_), channel_id=1, source_target_pairs={{0,8},{4,12},{8,0},{12,4},{1,9},{5,13},{9,1},{13,5},{2,10},{6,14},... | collective-permute-start | bytes 589832 | tf_op jit(solution)/shard_map/ppermute | solution.py:21
  61.6 11.5 %collective-permute-start.18 = (bf16[128,768]{1,0:T(8,128)(2,1)S(1)}, bf16[128,768]{1,0:T(8,128)(2,1)S(1)}, u32[]{:S(2)}, u32[]{:S(2)}) collective-permute-start(bf16[128,768]{1,0:T(8,128)(2,1)S(1)} %shard_map.218.refs_1_), channel_id=1, source_target_pairs={{0,8},{4,12},{8,0},{12,4},{1,9},{5,13},{9,1},{13,5},{2,10},{6,14},... | collective-permute-start | bytes 589832 | tf_op jit(solution)/shard_map/ppermute | solution.py:21
  82.6 15.1 %collective-permute-start.25 = (bf16[384,768]{1,0:T(8,128)(2,1)S(1)}, bf16[384,768]{1,0:T(8,128)(2,1)S(1)}, u32[]{:S(2)}, u32[]{:S(2)}) collective-permute-start(bf16[384,768]{1,0:T(8,128)(2,1)S(1)} %shard_map.225.refs_7_.refs_9_.refs_11_), channel_id=1, source_target_pairs={{0,1},{1,0},{2,3},{3,2},{4,5},{5,4},{6,7},{7,6},{8,9},{9,8},{10,11... | collective-permute-start | bytes 1769480 | tf_op jit(solution)/shard_map/ppermute | solution.py:21
  82.7 15.0 %collective-permute-start.24 = (bf16[128,768]{1,0:T(8,128)(2,1)S(1)}, bf16[128,768]{1,0:T(8,128)(2,1)S(1)}, u32[]{:S(2)}, u32[]{:S(2)}) collective-permute-start(bf16[128,768]{1,0:T(8,128)(2,1)S(1)} %shard_map.224.refs_4_.refs_1_.refs_0_), channel_id=1, source_target_pairs={{0,8},{4,12},{8,0},{12,4},{1,9},{5,13},{9,1},{13,5},{2,10},{6,14},... | collective-permute-start | bytes 589832 | tf_op jit(solution)/shard_map/ppermute | solution.py:21
  83.5 14.2 %collective-permute-start.26 = (bf16[128,192]{1,0:T(8,128)(2,1)S(1)}, bf16[128,192]{1,0:T(8,128)(2,1)S(1)}, u32[]{:S(2)}, u32[]{:S(2)}) collective-permute-start(bf16[128,192]{1,0:T(8,128)(2,1)S(1)} %shard_map.226), channel_id=1, source_target_pairs={{0,0},{1,4},{2,8},{3,12},{4,1},{5,5},{6,9},{7,13},{8,2},{9,6},{10,... | collective-permute-start | bytes 147464 | tf_op jit(solution)/shard_map/ppermute | solution.py:27
  126.5 11.8 %collective-permute-start.35 = (bf16[128,768]{1,0:T(8,128)(2,1)S(1)}, bf16[128,768]{1,0:T(8,128)(2,1)S(1)}, u32[]{:S(2)}, u32[]{:S(2)}) collective-permute-start(bf16[128,768]{1,0:T(8,128)(2,1)S(1)} %shard_map.233.refs_2_.refs_0_), channel_id=1, source_target_pairs={{0,8},{4,12},{8,0},{12,4},{1,9},{5,13},{9,1},{13,5},{2,10},{6,14},... | collective-permute-start | bytes 589832 | tf_op jit(solution)/shard_map/ppermute | solution.py:21
  140.8 9.7 %collective-permute-start.39 = (bf16[384,768]{1,0:T(8,128)(2,1)S(1)}, bf16[384,768]{1,0:T(8,128)(2,1)S(1)}, u32[]{:S(2)}, u32[]{:S(2)}) collective-permute-start(bf16[384,768]{1,0:T(8,128)(2,1)S(1)} %get-tuple-element.130), channel_id=1, source_target_pairs={{0,1},{1,0},{2,3},{3,2},{4,5},{5,4},{6,7},{7,6},{8,9},{9,8},{10,11... | collective-permute-start | bytes 1769480 | tf_op jit(solution)/shard_map/ppermute | solution.py:21
  140.9 9.6 %collective-permute-start.38 = (bf16[128,768]{1,0:T(8,128)(2,1)S(1)}, bf16[128,768]{1,0:T(8,128)(2,1)S(1)}, u32[]{:S(2)}, u32[]{:S(2)}) collective-permute-start(bf16[128,768]{1,0:T(8,128)(2,1)S(1)} %get-tuple-element.125.refs_1_.refs_2_.refs_0_), channel_id=1, source_target_pairs={{0,4},{4,0},{8,12},{12,8},{1,5},{5,1},{9,13},{13,9},{2,6},{6,2},{1... | collective-permute-start | bytes 589832 | tf_op jit(solution)/shard_map/ppermute | solution.py:21
  146.1 13.6 %collective-permute-start.32 = (bf16[192,128]{1,0:T(8,128)(2,1)S(1)}, bf16[192,128]{1,0:T(8,128)(2,1)S(1)}, u32[]{:S(2)}, u32[]{:S(2)}) collective-permute-start(bf16[192,128]{1,0:T(8,128)(2,1)S(1)} %get-tuple-element.112), channel_id=1, source_target_pairs={{0,0},{1,4},{2,8},{3,12},{4,1},{5,5},{6,9},{7,13},{8,2},{9,6},{10,... | collective-permute-start | bytes 147464 | tf_op jit(solution)/shard_map/ppermute | solution.py:27
  150.6 14.3 %collective-permute-start.42 = (bf16[128,768]{1,0:T(8,128)(2,1)S(1)}, bf16[128,768]{1,0:T(8,128)(2,1)S(1)}, u32[]{:S(2)}, u32[]{:S(2)}) collective-permute-start(bf16[128,768]{1,0:T(8,128)(2,1)S(1)} %shard_map.239.refs_1_.refs_2_.refs_0_), channel_id=1, source_target_pairs={{0,8},{4,12},{8,0},{12,4},{1,9},{5,13},{9,1},{13,5},{2,10},{6,14},... | collective-permute-start | bytes 589832 | tf_op jit(solution)/shard_map/ppermute | solution.py:21
  167.5 9.9 %collective-permute-start.48 = (bf16[768,768]{1,0:T(8,128)(2,1)S(1)}, bf16[768,768]{1,0:T(8,128)(2,1)S(1)}, u32[]{:S(2)}, u32[]{:S(2)}) collective-permute-start(bf16[768,768]{1,0:T(8,128)(2,1)S(1)} %get-tuple-element.145), channel_id=1, source_target_pairs={{0,1},{1,0},{2,3},{3,2},{4,5},{5,4},{6,7},{7,6},{8,9},{9,8},{10,11... | collective-permute-start | bytes 3538952 | tf_op jit(solution)/shard_map/ppermute | solution.py:21
  167.6 9.9 %collective-permute-start.47 = (bf16[128,768]{1,0:T(8,128)(2,1)S(1)}, bf16[128,768]{1,0:T(8,128)(2,1)S(1)}, u32[]{:S(2)}, u32[]{:S(2)}) collective-permute-start(bf16[128,768]{1,0:T(8,128)(2,1)S(1)} %get-tuple-element.140.refs_1_.refs_2_.refs_0_), channel_id=1, source_target_pairs={{0,4},{4,0},{8,12},{12,8},{1,5},{5,1},{9,13},{13,9},{2,6},{6,2},{1... | collective-permute-start | bytes 589832 | tf_op jit(solution)/shard_map/ppermute | solution.py:21
  177.5 11.8 %collective-permute-start.52 = (bf16[128,768]{1,0:T(8,128)(2,1)S(1)}, bf16[128,768]{1,0:T(8,128)(2,1)S(1)}, u32[]{:S(2)}, u32[]{:S(2)}) collective-permute-start(bf16[128,768]{1,0:T(8,128)(2,1)S(1)} %shard_map.250.refs_2_.refs_1_), channel_id=1, source_target_pairs={{0,8},{4,12},{8,0},{12,4},{1,9},{5,13},{9,1},{13,5},{2,10},{6,14},... | collective-permute-start | bytes 589832 | tf_op jit(solution)/shard_map/ppermute | solution.py:21
  194.9 10.4 %collective-permute-start.62 = (bf16[208,768]{1,0:T(8,128)(2,1)S(1)}, bf16[208,768]{1,0:T(8,128)(2,1)S(1)}, u32[]{:S(2)}, u32[]{:S(2)}) collective-permute-start(bf16[208,768]{1,0:T(8,128)(2,1)S(1)} %get-tuple-element.174), channel_id=1, source_target_pairs={{0,2},{1,3},{2,0},{3,1},{4,6},{5,7},{6,4},{7,5},{8,10},{9,11},{10,... | collective-permute-start | bytes 958472 | tf_op jit(solution)/shard_map/ppermute | solution.py:21
  196.4 31.1 %collective-permute-start.65 = (bf16[288,768]{1,0:T(8,128)(2,1)S(1)}, bf16[288,768]{1,0:T(8,128)(2,1)S(1)}, u32[]{:S(2)}, u32[]{:S(2)}) collective-permute-start(bf16[288,768]{1,0:T(8,128)(2,1)S(1)} %shard_map.259.refs_0_.refs_1_.refs_2_), channel_id=1, source_target_pairs={{0,16},{16,0},{1,17},{17,1},{2,18},{18,2},{3,19},{19,3},{4,20},{20... | collective-permute-start | bytes 1327112 | tf_op jit(solution)/shard_map/ppermute | solution.py:21
  197.2 20.5 %collective-permute-start.64 = (bf16[96,768]{1,0:T(8,128)(2,1)S(1)}, bf16[96,768]{1,0:T(8,128)(2,1)S(1)}, u32[]{:S(2)}, u32[]{:S(2)}) collective-permute-start(bf16[96,768]{1,0:T(8,128)(2,1)S(1)} %shard_map.260), channel_id=1, source_target_pairs={{0,2},{1,3},{2,0},{3,1},{4,6},{5,7},{6,4},{7,5},{8,10},{9,11},{10,... | collective-permute-start | bytes 442376 | tf_op jit(solution)/shard_map/ppermute | solution.py:21
  205.4 23.8 %collective-permute-start.63 = (bf16[208,768]{1,0:T(8,128)(2,1)S(1)}, bf16[208,768]{1,0:T(8,128)(2,1)S(1)}, u32[]{:S(2)}, u32[]{:S(2)}) collective-permute-start(bf16[208,768]{1,0:T(8,128)(2,1)S(1)} %shard_map.257.refs_0_), channel_id=1, source_target_pairs={{0,16},{16,0},{1,17},{17,1},{2,18},{18,2},{3,19},{19,3},{4,20},{20... | collective-permute-start | bytes 958472 | tf_op jit(solution)/shard_map/ppermute | solution.py:21
  217.8 9.8 %collective-permute-start.66 = (bf16[96,768]{1,0:T(8,128)(2,1)S(1)}, bf16[96,768]{1,0:T(8,128)(2,1)S(1)}, u32[]{:S(2)}, u32[]{:S(2)}) collective-permute-start(bf16[96,768]{1,0:T(8,128)(2,1)S(1)} %shard_map.261.refs_3_), channel_id=1, source_target_pairs={{0,16},{16,0},{1,17},{17,1},{2,18},{18,2},{3,19},{19,3},{4,20},{20... | collective-permute-start | bytes 442376 | tf_op jit(solution)/shard_map/ppermute | solution.py:21
  (52 other events, 343.2 us)

commit v4 on v3

--- a/solution.py
+++ b/solution.py
@@ -68,8 +68,12 @@
     n_in, n_after, n_out = len(ins), len(after), len(outs)
 
     def body(*refs):
+        inputs = list(refs[:n_in])
+        if args[0].dtype == jnp.int32:
+            col = lax.axis_index("col")
+            inputs[0] = (lax.axis_index("row"), col, refs[0][col])
         kernel(
-            refs[:n_in],
+            inputs,
             refs[n_in + n_after : n_in + n_after + n_out],
             refs[n_in + n_after + n_out :],
         )
@@ -271,6 +275,14 @@
     rowwise[...] = low.astype(BF16)
 
 
+def k_split(ins, outs, scr):
+    attn, up, down = ins
+    half = outs[0].shape[0]
+    for i, (ref, layer) in enumerate(((down, 0), (attn, 1), (up, 1), (down, 1))):
+        for j in range(2):
+            outs[2 * i + j][...] = ref[layer, j * half : (j + 1) * half, :]
+
+
 def k_pack(ins, outs, scr):
     at = 0
     for ref in ins:
@@ -485,6 +497,19 @@
         at += rows
 
 
+def k_add_whole(ins, outs, scr):
+    at = 0
+    for ref in ins[:3]:
+        outs[0][at : at + ref.shape[0], :] = ref[...]
+        at += ref.shape[0]
+    at = 0
+    for ref in ins[3:]:
+        rows = ref.shape[0]
+        total = f32(outs[0].at[at : at + rows]) + f32(ref)
+        outs[0][at : at + rows, :] = total.astype(BF16)
+        at += rows
+
+
 def k_feed_outputs(ins, outs, scr):
     half = ins[0].shape[0]
     for layer in range(2):
@@ -522,21 +547,19 @@
 ):
     layers = w_attn.shape[0]
     n, m = lax.axis_size("row"), lax.axis_size("col")
-    row, col = lax.axis_index("row"), lax.axis_index("col")
     tokens, piece = hidden_in.shape
     model = piece * m
     hidden = w_up.shape[2]
     width = w_attn.shape[2] // 4
     heads = width // HEAD_DIM
-    length = lax.dynamic_index_in_dim(lengths, col, 0, keepdims=False)
-    sc = jnp.stack([row, col, length]).astype(jnp.int32)
+    sc = lengths
 
     tile = (tokens, model)
 
     def layer_of(array, layer):
         return (array, (1,) + array.shape[1:], (layer, 0, 0))
 
-    half_block = sds((piece // 2, hidden), BF16)
+    half_block, low_block = sds((piece // 2, hidden), BF16), sds((piece, hidden), BF16)
 
     def pack(rows, arrays, after=()):
         return call(k_pack, [sds((rows, hidden), BF16)], arrays, after=after, final=True)[0]
@@ -549,10 +572,6 @@
 
     def along_of(arrays):
         return [exchange(a, "col", 2) for a in arrays]
-
-    def half_of(array, layer, which, after):
-        view = (array, (1, piece // 2, hidden), (layer, which, 0))
-        return pack(piece // 2, [view], after)
 
     def gathered(own, along, rows=piece, after=()):
         both = pack(2 * rows, [whole(a) for a in [*own, *along]], after)
@@ -579,6 +598,9 @@
     mine = turned(mine)
     x_in = [mine] + [exchange(mine, "row", k) for k in range(1, n)]
     (x,) = call(k_prep, [sds(tile, BF16)], [sc, *x_in])
+    weights = [whole(a) for a in (w_attn, w_up, w_down)]
+    halves = call(k_split, [half_block] * 8, weights, after=x_in[1:], final=True)
+    down0, attn1, up1, down1 = [halves[2 * i : 2 * i + 2] for i in range(4)]
     up0 = pack(piece, [layer_of(w_up, 0)], [mine])
     (up0_along,) = along_of([up0])
     attn0 = gathered([block], [along], piece + 16, [*x_in[1:], up0_along])
@@ -597,13 +619,12 @@
         partial(k_attend_first, m),
         [low_tile, sds((16, model), F32), o_out, qkv_out, p_out],
         [sc, x, *attn0, rowwise],
-    )
-    down0 = [half_of(w_down, 0, i, [z]) for i in range(2)]
+        after=[down0[0]],
+    )
     down0_along = along_of(down0)
     z = pair_sum(z, down0_along)
     up0 = gathered([up0], [up0_along], after=[z])
     down0 = gathered(down0, down0_along, after=[z])
-    attn1 = [half_of(w_attn, 1, i, [z]) for i in range(2)]
     attn1_along = along_of(attn1)
     f, unit_a0, h0, g0, slope0 = call(
         partial(k_feed, m, 0),
@@ -612,34 +633,29 @@
         after=attn1_along,
     )
     attn1 = gathered(attn1, attn1_along, after=[f])
-    up1 = [half_of(w_up, 1, 0, [f])]
-    up1_along = along_of(up1)
-    f = pair_sum(f, [attn1[1][0], *up1_along])
-    up1 += [half_of(w_up, 1, 1, [f])]
+    up1_along = along_of(up1[:1])
+    (low,) = call(k_turned, [sds((tokens, piece), BF16)], [whole(cotangent.T)], after=[f], final=True)
+    cotan = turned(low)
+    f = pair_sum(f, [attn1[1][0], *up1_along, cotan])
     up1_along += along_of(up1[1:])
-    down1 = [half_of(w_down, 1, 0, [f])]
-    down1_along = along_of(down1)
+    down1_along = along_of(down1[:1])
     z, unit_b0, x1, o1, qkv1, p1 = call(
         partial(k_attend, m, 1),
         [low_tile, unit_out, low_tile, o_out, qkv_out, p_out],
         [sc, *both(f), unit_a0, *attn1, rowwise, prm],
         after=[up1_along[1], *down1_along],
     )
-    down1 += [half_of(w_down, 1, 1, [z])]
     down1_along += along_of(down1[1:])
     up1 = gathered(up1, up1_along, after=[z])
     z = pair_sum(z, [down1_along[1], up1[1][0]])
     down1 = gathered(down1, down1_along, after=[z])
-    (low,) = call(k_turned, [sds((tokens, piece), BF16)], [whole(cotangent.T)], after=[z], final=True)
-    cotan = turned(low)
     f, unit_a1, h1, g1, slope1 = call(
         partial(k_feed, m, 1),
         feed_out,
         [*both(z), unit_b0, *up1, *down1, rowwise, prm],
-        after=[cotan],
-    )
-    cotan = [cotan, *held([cotan], [f])]
-    cotan = [cotan[0]] + [exchange(cotan[1], "row", k) for k in range(1, n)]
+    )
+    (again,) = held([cotan], [f])
+    cotan = [cotan] + [exchange(again, "row", k) for k in range(1, n)]
     f = pair_sum(f, cotan[1:])
     (cotan,) = call(k_prep, [sds(tile, BF16)], [sc, *cotan], after=[f])
 
@@ -697,31 +713,33 @@
     attn1_more += along_of(held(attn1_stay[3:], [dh]))
     (low,) = call(k_add, [half_block], [stay1[3], more1[3]], after=[dh])
     terms1 += [last_of_dp(low)]
-    (low,) = call(k_add, [half_block], [attn1_stay[0], attn1_more[0]], after=[dh])
-    attn1_terms = [last_of_dp(low)]
-    dh = pair_sum(dh, [got, attn1_more[1], terms1[3][1], attn1_terms[0][1]])
-    stay0 = call(k_middle, [half_block] * 8, [keep, got], after=[dh])
-    more0 = along_of(stay0[4:7])
-    (low,) = call(k_add, [half_block], [attn1_stay[1], attn1_more[1]], after=[dh])
-    attn1_terms += [last_of_dp(low)]
+    dh = pair_sum(dh, [got, attn1_more[1], terms1[3][1]])
+    stay0 = call(
+        k_middle, [half_block] * 4 + [low_block] + [half_block] * 2, [keep, got], after=[dh]
+    )
+    more0 = along_of(stay0[4:6])
+    attn1_terms = []
+    for i in range(2):
+        (low,) = call(k_add, [half_block], [attn1_stay[i], attn1_more[i]], after=[dh])
+        attn1_terms.append(last_of_dp(low))
     *dx, low_last, grads0, sums_a0 = call(
         partial(k_attend_back_last, n, m),
         [sds((tokens, piece), F32)]
         + [sds((tokens, piece), BF16)] * (n - 1)
         + [low_tile, qkv_out, sums_out],
         [sc, *both(dh), df, unit_a0, *attn0, qkv0, p0, prm],
-        after=[*more0, attn1_terms[1][1]],
-    )
-    more0 += along_of(held(stay0[7:], [dx[0]]))
+        after=[*more0, attn1_terms[0][1], attn1_terms[1][1]],
+    )
+    more0 += along_of(held(stay0[6:], [dx[0]]))
     most = [sds((3 * piece // 2, hidden), BF16)]
-    (low,) = call(k_add, most, [*stay0[:3], *more0[:3]])
+    (low,) = call(k_add_whole, most, [*stay0[:3], *more0[:2]])
     most0_terms = last_of_dp(low)
     (grad_total,) = call(
         k_total,
         [sds((piece, tokens), F32)],
         [dx[0]] + [exchange(dx[k], "row", k) for k in range(1, n)],
     )
-    grad_input = turned(grad_total)
+    (grad_input,) = held([turned(grad_total)], [])
 
     keep, send = call(
         partial(k_attend_weight_last, m),
@@ -744,9 +762,9 @@
     low_tail = sds((piece + 16, hidden), BF16)
     attn0_stay, attn0_go = call(k_middle, [low_tail] * 2, [keep, got])
     (attn0_more,) = along_of([attn0_go])
-    (low,) = call(k_add, [half_block], [stay0[3], more0[3]], after=[grad_total])
+    (low,) = call(k_add, [half_block], [stay0[3], more0[2]])
     rest0_terms = last_of_dp(low)
-    (low,) = call(k_add, [low_tail], [attn0_stay, attn0_more])
+    (low,) = call(k_add, [low_tail], [attn0_stay, attn0_more], after=[grad_total])
     attn0_terms = [last_of_dp(low)]
     def halves_of(array):
         return [(array, (piece // 2, hidden), (i, 0)) for i in range(3)]

time: 231 us -> 220 us (0.952)
  starting transfers between devices: 71.1 us -> 63.1 us
  waiting for transfers between devices: 128 us -> 124 us
    ppermute x63 -> x62, starting transfers between devices: 54.9 us -> 45.6 us  [exchange(): return lax.ppermute(x, axis, [(i, i ^ bit) for i in range(n)])]
    ppermute x4, waiting for transfers between devices: 24 us -> 15.2 us  [turned(): return lax.ppermute(x, ('row', 'col'), pairs)]
    ppermute x63 -> x62, waiting for transfers between devices: 104 us -> 109 us  [exchange(): return lax.ppermute(x, axis, [(i, i ^ bit) for i in range(n)])]
    pallas_call x60 -> x54, Pallas kernels: 25.3 us -> 26 us  [call(): pl.pallas_call(body, grid=(1,), out_shape=outs, in_specs=specs + [pl.Bloc...]
  transfers between devices with their start and end apart: 67 -> 66, of which waited for: 40 -> 41; matrix products, arithmetic and copies ran while one was open for 1% -> 0% of each run, Pallas kernels for 2% -> 3%
where the time goes in v4:
time: 220 us; the launch traced here: 219 us
  waiting for transfers between devices  124 us (56%)
  starting transfers between devices  63.1 us (29%)
  Pallas kernels  26 us (12%)
  local copies, waits for them, and re-layouts  3.99 us (2%)
    ppermute x62, waiting for transfers between devices, exchange(): return lax.ppermute(x, axis, [(i, i ^ bit) for i in range(n)])  109 us
    ppermute x62, starting transfers between devices, exchange(): return lax.ppermute(x, axis, [(i, i ^ bit) for i in range(n)])  45.6 us
    pallas_call x54, Pallas kernels, call(): pl.pallas_call(body, grid=(1,), out_shape=outs, in_specs=specs + [pl.Bloc...  26 us
    ppermute x4, starting transfers between devices, turned(): return lax.ppermute(x, ('row', 'col'), pairs)  17.5 us
    ppermute x4, waiting for transfers between devices, turned(): return lax.ppermute(x, ('row', 'col'), pairs)  15.2 us
  transfers between devices with their start and end apart: 66, of which 41 were waited for; matrix products, arithmetic and copies ran while one was open for 0% of the time, Pallas kernels for 3%

profile of v4, /device:TPU:2, one launch (start us, length us, event | category | flops | bytes accessed | tf_op | source)
XLA Modules:
  0.0 218.5 jit_solution(2994977509336213852)
XLA Ops:
  0.6 2.5 %shard_map.203 = (bf16[208,768]{1,0:T(8,128)(2,1)}, bf16[16,768]{1,0:T(8,128)(2,1)}, bf16[128,192]{1,0:T(8,128)(2,1)}) custom-call(bf16[2,192,768]{2,1,0:T(8,128)(2,1)} %refs_0_.12, bf16[192,128]{1,0:T(8,128)(2,1)} %bitcast.7, bf16[2,192]{1,0:T(2,128)(2,1)} %refs_2_.2, bf16[2,192]{1,0:T(2,128)(2,1)} %refs_3_.1, bf16[2,2,192]{2,1,0:T(2,128)(2,1)} %refs_4_.1, ...), custom_call_target="tpu_custom_call" | custom-call | flops 200000000 | bytes 737280 | tf_op jit(solution)/shard_map/pallas_call | solution.py:81
  3.2 4.5 %collective-permute-start = (bf16[128,192]{1,0:T(8,128)(2,1)}, bf16[128,192]{1,0:T(8,128)(2,1)S(1)}, u32[]{:S(2)}, u32[]{:S(2)}) collective-permute-start(bf16[128,192]{1,0:T(8,128)(2,1)} %get-tuple-element.107), channel_id=1, source_target_pairs={{0,0},{1,4},{2,8},{3,12},{4,1},{5,5},{6,9},{7,13},{8,2},{9,6},{10,... | collective-permute-start | bytes 147464 | tf_op jit(solution)/shard_map/ppermute | solution.py:27
  7.8 5.3 %collective-permute-done.refs_1_ = bf16[128,192]{1,0:T(8,128)(2,1)S(1)} collective-permute-done((bf16[128,192]{1,0:T(8,128)(2,1)}, bf16[128,192]{1,0:T(8,128)(2,1)S(1)}, u32[]{:S(2)}, u32[]{:S(2)}) %collective-permute-start) | collective-permute-done | bytes 49184 | tf_op jit(solution)/shard_map/ppermute | solution.py:27
  14.2 3.1 %collective-permute-start.3 = (bf16[128,192]{1,0:T(8,128)(2,1)S(1)}, bf16[128,192]{1,0:T(8,128)(2,1)S(1)}, u32[]{:S(2)}, u32[]{:S(2)}) collective-permute-start(bf16[128,192]{1,0:T(8,128)(2,1)S(1)} %collective-permute-done.refs_1_), channel_id=1, source_target_pairs={{0,12},{4,8},{8,4},{12,0},{1,13},{5,9},{9,5},{13,1},{2,14},{6,10},... | collective-permute-start | bytes 147464 | tf_op jit(solution)/shard_map/ppermute | solution.py:21
  22.5 3.3 %collective-permute-done.5.refs_5_.refs_1_ = bf16[192,768]{1,0:T(8,128)(2,1)S(1)} collective-permute-done((bf16[192,768]{1,0:T(8,128)(2,1)S(1)}, bf16[192,768]{1,0:T(8,128)(2,1)S(1)}, u32[]{:S(2)}, u32[]{:S(2)}) %collective-permute-start.5) | collective-permute-done | bytes 294944 | tf_op jit(solution)/shard_map/ppermute | solution.py:21
  32.8 4.7 %collective-permute-done.9.refs_3_ = bf16[96,768]{1,0:T(8,128)(2,1)S(1)} collective-permute-done((bf16[96,768]{1,0:T(8,128)(2,1)S(1)}, bf16[96,768]{1,0:T(8,128)(2,1)S(1)}, u32[]{:S(2)}, u32[]{:S(2)}) %collective-permute-start.9) | collective-permute-done | bytes 147488 | tf_op jit(solution)/shard_map/ppermute | solution.py:21
  42.8 4.7 %collective-permute-done.13.refs_13_.refs_2_ = bf16[96,768]{1,0:T(8,128)(2,1)S(1)} collective-permute-done((bf16[96,768]{1,0:T(8,128)(2,1)S(1)}, bf16[96,768]{1,0:T(8,128)(2,1)S(1)}, u32[]{:S(2)}, u32[]{:S(2)}) %collective-permute-start.13) | collective-permute-done | bytes 147488 | tf_op jit(solution)/shard_map/ppermute | solution.py:21
  49.6 2.9 %collective-permute-done.10.refs_1_ = bf16[128,768]{1,0:T(8,128)(2,1)S(1)} collective-permute-done((bf16[128,768]{1,0:T(8,128)(2,1)S(1)}, bf16[128,768]{1,0:T(8,128)(2,1)S(1)}, u32[]{:S(2)}, u32[]{:S(2)}) %collective-permute-start.10) | collective-permute-done | bytes 196640 | tf_op jit(solution)/shard_map/ppermute | solution.py:21
  54.5 4.5 %collective-permute-start.18 = (bf16[128,192]{1,0:T(8,128)(2,1)S(1)}, bf16[128,192]{1,0:T(8,128)(2,1)S(1)}, u32[]{:S(2)}, u32[]{:S(2)}) collective-permute-start(bf16[128,192]{1,0:T(8,128)(2,1)S(1)} %shard_map.214), channel_id=1, source_target_pairs={{0,0},{1,4},{2,8},{3,12},{4,1},{5,5},{6,9},{7,13},{8,2},{9,6},{10,... | collective-permute-start | bytes 147464 | tf_op jit(solution)/shard_map/ppermute | solution.py:27
  60.0 4.3 %collective-permute-done.18.refs_4_.refs_0_.refs_1_ = bf16[128,192]{1,0:T(8,128)(2,1)S(1)} collective-permute-done((bf16[128,192]{1,0:T(8,128)(2,1)S(1)}, bf16[128,192]{1,0:T(8,128)(2,1)S(1)}, u32[]{:S(2)}, u32[]{:S(2)}) %collective-permute-start.18) | collective-permute-done | bytes 49184 | tf_op jit(solution)/shard_map/ppermute | solution.py:27
  66.5 4.2 %collective-permute-done.20.refs_10_.refs_3_ = bf16[96,768]{1,0:T(8,128)(2,1)S(1)} collective-permute-done((bf16[96,768]{1,0:T(8,128)(2,1)S(1)}, bf16[96,768]{1,0:T(8,128)(2,1)S(1)}, u32[]{:S(2)}, u32[]{:S(2)}) %collective-permute-start.20) | collective-permute-done | bytes 147488 | tf_op jit(solution)/shard_map/ppermute | solution.py:21
  72.2 2.6 %collective-permute-done.19.refs_2_ = bf16[128,768]{1,0:T(8,128)(2,1)S(1)} collective-permute-done((bf16[128,768]{1,0:T(8,128)(2,1)S(1)}, bf16[128,768]{1,0:T(8,128)(2,1)S(1)}, u32[]{:S(2)}, u32[]{:S(2)}) %collective-permute-start.19) | collective-permute-done | bytes 196640 | tf_op jit(solution)/shard_map/ppermute | solution.py:21
  77.1 6.1 %collective-permute-done.23.refs_2_.refs_3_ = bf16[96,768]{1,0:T(8,128)(2,1)S(1)} collective-permute-done((bf16[96,768]{1,0:T(8,128)(2,1)S(1)}, bf16[96,768]{1,0:T(8,128)(2,1)S(1)}, u32[]{:S(2)}, u32[]{:S(2)}) %collective-permute-start.23) | collective-permute-done | bytes 147488 | tf_op jit(solution)/shard_map/ppermute | solution.py:21
  84.5 12.4 %collective-permute-done.25.refs_1_ = bf16[128,768]{1,0:T(8,128)(2,1)S(1)} collective-permute-done((bf16[128,768]{1,0:T(8,128)(2,1)S(1)}, bf16[128,768]{1,0:T(8,128)(2,1)S(1)}, u32[]{:S(2)}, u32[]{:S(2)}) %collective-permute-start.25) | collective-permute-done | bytes 196640 | tf_op jit(solution)/shard_map/ppermute | solution.py:21
  102.4 3.8 %collective-permute-done.30.refs_4_ = bf16[128,192]{1,0:T(8,128)(2,1)S(1)} collective-permute-done((bf16[128,192]{1,0:T(8,128)(2,1)S(1)}, bf16[128,192]{1,0:T(8,128)(2,1)S(1)}, u32[]{:S(2)}, u32[]{:S(2)}) %collective-permute-start.30) | collective-permute-done | bytes 49184 | tf_op jit(solution)/shard_map/ppermute | solution.py:21
  110.3 9.4 %collective-permute-done.31.refs_2_ = bf16[128,768]{1,0:T(8,128)(2,1)S(1)} collective-permute-done((bf16[128,768]{1,0:T(8,128)(2,1)S(1)}, bf16[128,768]{1,0:T(8,128)(2,1)S(1)}, u32[]{:S(2)}, u32[]{:S(2)}) %collective-permute-start.31) | collective-permute-done | bytes 196640 | tf_op jit(solution)/shard_map/ppermute | solution.py:21
  122.4 7.2 %collective-permute-done.33.refs_1_ = bf16[128,768]{1,0:T(8,128)(2,1)S(1)} collective-permute-done((bf16[128,768]{1,0:T(8,128)(2,1)S(1)}, bf16[128,768]{1,0:T(8,128)(2,1)S(1)}, u32[]{:S(2)}, u32[]{:S(2)}) %collective-permute-start.33) | collective-permute-done | bytes 196640 | tf_op jit(solution)/shard_map/ppermute | solution.py:21
  132.1 4.7 %collective-permute-done.36.refs_11_.refs_1_ = bf16[96,768]{1,0:T(8,128)(2,1)S(1)} collective-permute-done((bf16[96,768]{1,0:T(8,128)(2,1)S(1)}, bf16[96,768]{1,0:T(8,128)(2,1)S(1)}, u32[]{:S(2)}, u32[]{:S(2)}) %collective-permute-start.36) | collective-permute-done | bytes 147488 | tf_op jit(solution)/shard_map/ppermute | solution.py:21
  145.6 4.9 %collective-permute-start.32 = (bf16[192,128]{1,0:T(8,128)(2,1)S(1)}, bf16[192,128]{1,0:T(8,128)(2,1)S(1)}, u32[]{:S(2)}, u32[]{:S(2)}) collective-permute-start(bf16[192,128]{1,0:T(8,128)(2,1)S(1)} %get-tuple-element.127), channel_id=1, source_target_pairs={{0,0},{1,4},{2,8},{3,12},{4,1},{5,5},{6,9},{7,13},{8,2},{9,6},{10,... | collective-permute-start | bytes 147464 | tf_op jit(solution)/shard_map/ppermute | solution.py:27
  168.1 3.7 %collective-permute-done.49.refs_3_.refs_1_ = bf16[96,768]{1,0:T(8,128)(2,1)S(1)} collective-permute-done((bf16[96,768]{1,0:T(8,128)(2,1)S(1)}, bf16[96,768]{1,0:T(8,128)(2,1)S(1)}, u32[]{:S(2)}, u32[]{:S(2)}) %collective-permute-start.49) | collective-permute-done | bytes 147488 | tf_op jit(solution)/shard_map/ppermute | solution.py:21
  179.5 5.4 %collective-permute-done.53.refs_13_.refs_4_ = bf16[96,768]{1,0:T(8,128)(2,1)S(1)} collective-permute-done((bf16[96,768]{1,0:T(8,128)(2,1)S(1)}, bf16[96,768]{1,0:T(8,128)(2,1)S(1)}, u32[]{:S(2)}, u32[]{:S(2)}) %collective-permute-start.53) | collective-permute-done | bytes 147488 | tf_op jit(solution)/shard_map/ppermute | solution.py:21
  185.6 2.6 %shard_map.246 = (f32[128,192]{1,0:T(8,128)S(1)}, bf16[128,192]{1,0:T(8,128)(2,1)S(1)}, bf16[128,192]{1,0:T(8,128)(2,1)S(1)}, bf16[128,192]{1,0:T(8,128)(2,1)S(1...) custom-call(s32[4]{0:T(128)S(1)} %copy-done.8, ...), custom_call_target="tpu_custom_call" | custom-call | flops 200000000 | bytes 3530752 | tf_op jit(solution)/shard_map/pallas_call | solution.py:81
  205.0 3.6 %collective-permute-start.59 = (f32[192,128]{1,0:T(8,128)S(1)}, f32[192,128]{1,0:T(8,128)S(1)}, u32[]{:S(2)}, u32[]{:S(2)}) collective-permute-start(f32[192,128]{1,0:T(8,128)S(1)} %shard_map.247.refs_2_), channel_id=1, source_target_pairs={{0,0},{1,4},{2,8},{3,12},{4,1},{5,5},{6,9},{7,13},{8,2},{9,6},{10,... | collective-permute-start | bytes 294920 | tf_op jit(solution)/shard_map/ppermute | solution.py:27
  208.6 5.7 %collective-permute-done.59.refs_0_ = f32[192,128]{1,0:T(8,128)S(1)} collective-permute-done((f32[192,128]{1,0:T(8,128)S(1)}, f32[192,128]{1,0:T(8,128)S(1)}, u32[]{:S(2)}, u32[]{:S(2)}) %collective-permute-start.59) | collective-permute-done | bytes 98336 | tf_op jit(solution)/shard_map/ppermute | solution.py:27
  (182 shorter events, 101.2 us)
Async XLA Ops:
  3.2 9.9 %collective-permute-start = (bf16[128,192]{1,0:T(8,128)(2,1)}, bf16[128,192]{1,0:T(8,128)(2,1)S(1)}, u32[]{:S(2)}, u32[]{:S(2)}) collective-permute-start(bf16[128,192]{1,0:T(8,128)(2,1)} %get-tuple-element.107), channel_id=1, source_target_pairs={{0,0},{1,4},{2,8},{3,12},{4,1},{5,5},{6,9},{7,13},{8,2},{9,6},{10,... | collective-permute-start | bytes 147464 | tf_op jit(solution)/shard_map/ppermute | solution.py:27
  7.7 14.8 %collective-permute-start.4 = (bf16[208,768]{1,0:T(8,128)(2,1)}, bf16[208,768]{1,0:T(8,128)(2,1)S(1)}, u32[]{:S(2)}, u32[]{:S(2)}) collective-permute-start(bf16[208,768]{1,0:T(8,128)(2,1)} %get-tuple-element.108.refs_0_), channel_id=1, source_target_pairs={{0,2},{1,3},{2,0},{3,1},{4,6},{5,7},{6,4},{7,5},{8,10},{9,11},{10,... | collective-permute-start | bytes 958472 | tf_op jit(solution)/shard_map/ppermute | solution.py:21
  14.2 11.6 %collective-permute-start.5 = (bf16[192,768]{1,0:T(8,128)(2,1)S(1)}, bf16[192,768]{1,0:T(8,128)(2,1)S(1)}, u32[]{:S(2)}, u32[]{:S(2)}) collective-permute-start(bf16[192,768]{1,0:T(8,128)(2,1)S(1)} %shard_map.205.refs_0_), channel_id=1, source_target_pairs={{0,2},{1,3},{2,0},{3,1},{4,6},{5,7},{6,4},{7,5},{8,10},{9,11},{10,... | collective-permute-start | bytes 884744 | tf_op jit(solution)/shard_map/ppermute | solution.py:21
  39.9 12.7 %collective-permute-start.11 = (bf16[384,768]{1,0:T(8,128)(2,1)S(1)}, bf16[384,768]{1,0:T(8,128)(2,1)S(1)}, u32[]{:S(2)}, u32[]{:S(2)}) collective-permute-start(bf16[384,768]{1,0:T(8,128)(2,1)S(1)} %shard_map.210.refs_3_.refs_5_.refs_4_.refs_6_), channel_id=1, source_target_pairs={{0,1},{1,0},{2,3},{3,2},{4,5},{5,4},{6,7},{7,6},{8,9},{9,8},{10,11... | collective-permute-start | bytes 1769480 | tf_op jit(solution)/shard_map/ppermute | solution.py:21
  40.0 12.6 %collective-permute-start.12 = (bf16[384,768]{1,0:T(8,128)(2,1)S(1)}, bf16[384,768]{1,0:T(8,128)(2,1)S(1)}, u32[]{:S(2)}, u32[]{:S(2)}) collective-permute-start(bf16[384,768]{1,0:T(8,128)(2,1)S(1)} %shard_map.211.refs_7_.refs_9_.refs_8_.refs_10_), channel_id=1, source_target_pairs={{0,1},{1,0},{2,3},{3,2},{4,5},{5,4},{6,7},{7,6},{8,9},{9,8},{10,11... | collective-permute-start | bytes 1769480 | tf_op jit(solution)/shard_map/ppermute | solution.py:21
  40.6 12.0 %collective-permute-start.10 = (bf16[128,768]{1,0:T(8,128)(2,1)S(1)}, bf16[128,768]{1,0:T(8,128)(2,1)S(1)}, u32[]{:S(2)}, u32[]{:S(2)}) collective-permute-start(bf16[128,768]{1,0:T(8,128)(2,1)S(1)} %shard_map.209.refs_2_.refs_4_.refs_0_), channel_id=1, source_target_pairs={{0,8},{4,12},{8,0},{12,4},{1,9},{5,13},{9,1},{13,5},{2,10},{6,14},... | collective-permute-start | bytes 589832 | tf_op jit(solution)/shard_map/ppermute | solution.py:21
  53.6 10.6 %collective-permute-start.16 = (bf16[384,768]{1,0:T(8,128)(2,1)S(1)}, bf16[384,768]{1,0:T(8,128)(2,1)S(1)}, u32[]{:S(2)}, u32[]{:S(2)}) collective-permute-start(bf16[384,768]{1,0:T(8,128)(2,1)S(1)} %shard_map.213.refs_4_.refs_6_), channel_id=1, source_target_pairs={{0,1},{1,0},{2,3},{3,2},{4,5},{5,4},{6,7},{7,6},{8,9},{9,8},{10,11... | collective-permute-start | bytes 1769480 | tf_op jit(solution)/shard_map/ppermute | solution.py:21
  53.7 10.5 %collective-permute-start.15 = (bf16[128,768]{1,0:T(8,128)(2,1)S(1)}, bf16[128,768]{1,0:T(8,128)(2,1)S(1)}, u32[]{:S(2)}, u32[]{:S(2)}) collective-permute-start(bf16[128,768]{1,0:T(8,128)(2,1)S(1)} %get-tuple-element.116.refs_4_.refs_1_.refs_0_), channel_id=1, source_target_pairs={{0,4},{4,0},{8,12},{12,8},{1,5},{5,1},{9,13},{13,9},{2,6},{6,2},{1... | collective-permute-start | bytes 589832 | tf_op jit(solution)/shard_map/ppermute | solution.py:21
  54.5 9.7 %collective-permute-start.18 = (bf16[128,192]{1,0:T(8,128)(2,1)S(1)}, bf16[128,192]{1,0:T(8,128)(2,1)S(1)}, u32[]{:S(2)}, u32[]{:S(2)}) collective-permute-start(bf16[128,192]{1,0:T(8,128)(2,1)S(1)} %shard_map.214), channel_id=1, source_target_pairs={{0,0},{1,4},{2,8},{3,12},{4,1},{5,5},{6,9},{7,13},{8,2},{9,6},{10,... | collective-permute-start | bytes 147464 | tf_op jit(solution)/shard_map/ppermute | solution.py:27
  64.3 10.6 %collective-permute-start.19 = (bf16[128,768]{1,0:T(8,128)(2,1)S(1)}, bf16[128,768]{1,0:T(8,128)(2,1)S(1)}, u32[]{:S(2)}, u32[]{:S(2)}) collective-permute-start(bf16[128,768]{1,0:T(8,128)(2,1)S(1)} %shard_map.215.refs_1_), channel_id=1, source_target_pairs={{0,8},{4,12},{8,0},{12,4},{1,9},{5,13},{9,1},{13,5},{2,10},{6,14},... | collective-permute-start | bytes 589832 | tf_op jit(solution)/shard_map/ppermute | solution.py:21
  84.4 12.5 %collective-permute-start.26 = (bf16[384,768]{1,0:T(8,128)(2,1)S(1)}, bf16[384,768]{1,0:T(8,128)(2,1)S(1)}, u32[]{:S(2)}, u32[]{:S(2)}) collective-permute-start(bf16[384,768]{1,0:T(8,128)(2,1)S(1)} %shard_map.219.refs_7_.refs_9_.refs_11_), channel_id=1, source_target_pairs={{0,1},{1,0},{2,3},{3,2},{4,5},{5,4},{6,7},{7,6},{8,9},{9,8},{10,11... | collective-permute-start | bytes 1769480 | tf_op jit(solution)/shard_map/ppermute | solution.py:21
  84.4 12.4 %collective-permute-start.25 = (bf16[128,768]{1,0:T(8,128)(2,1)S(1)}, bf16[128,768]{1,0:T(8,128)(2,1)S(1)}, u32[]{:S(2)}, u32[]{:S(2)}) collective-permute-start(bf16[128,768]{1,0:T(8,128)(2,1)S(1)} %shard_map.218.refs_4_.refs_0_), channel_id=1, source_target_pairs={{0,8},{4,12},{8,0},{12,4},{1,9},{5,13},{9,1},{13,5},{2,10},{6,14},... | collective-permute-start | bytes 589832 | tf_op jit(solution)/shard_map/ppermute | solution.py:21
  97.9 11.0 %collective-permute-start.27 = (bf16[128,768]{1,0:T(8,128)(2,1)S(1)}, bf16[128,768]{1,0:T(8,128)(2,1)S(1)}, u32[]{:S(2)}, u32[]{:S(2)}) collective-permute-start(bf16[128,768]{1,0:T(8,128)(2,1)S(1)} %get-tuple-element.124.refs_1_.refs_0_), channel_id=1, source_target_pairs={{0,4},{4,0},{8,12},{12,8},{1,5},{5,1},{9,13},{13,9},{2,6},{6,2},{1... | collective-permute-start | bytes 589832 | tf_op jit(solution)/shard_map/ppermute | solution.py:21
  108.9 10.8 %collective-permute-start.31 = (bf16[128,768]{1,0:T(8,128)(2,1)S(1)}, bf16[128,768]{1,0:T(8,128)(2,1)S(1)}, u32[]{:S(2)}, u32[]{:S(2)}) collective-permute-start(bf16[128,768]{1,0:T(8,128)(2,1)S(1)} %shard_map.222.refs_5_.refs_1_), channel_id=1, source_target_pairs={{0,8},{4,12},{8,0},{12,4},{1,9},{5,13},{9,1},{13,5},{2,10},{6,14},... | collective-permute-start | bytes 589832 | tf_op jit(solution)/shard_map/ppermute | solution.py:21
  129.7 11.5 %collective-permute-start.35 = (bf16[128,768]{1,0:T(8,128)(2,1)S(1)}, bf16[128,768]{1,0:T(8,128)(2,1)S(1)}, u32[]{:S(2)}, u32[]{:S(2)}) collective-permute-start(bf16[128,768]{1,0:T(8,128)(2,1)S(1)} %shard_map.226.refs_2_.refs_0_), channel_id=1, source_target_pairs={{0,8},{4,12},{8,0},{12,4},{1,9},{5,13},{9,1},{13,5},{2,10},{6,14},... | collective-permute-start | bytes 589832 | tf_op jit(solution)/shard_map/ppermute | solution.py:21
  145.6 10.4 %collective-permute-start.32 = (bf16[192,128]{1,0:T(8,128)(2,1)S(1)}, bf16[192,128]{1,0:T(8,128)(2,1)S(1)}, u32[]{:S(2)}, u32[]{:S(2)}) collective-permute-start(bf16[192,128]{1,0:T(8,128)(2,1)S(1)} %get-tuple-element.127), channel_id=1, source_target_pairs={{0,0},{1,4},{2,8},{3,12},{4,1},{5,5},{6,9},{7,13},{8,2},{9,6},{10,... | collective-permute-start | bytes 147464 | tf_op jit(solution)/shard_map/ppermute | solution.py:27
  151.1 11.7 %collective-permute-start.42 = (bf16[128,768]{1,0:T(8,128)(2,1)S(1)}, bf16[128,768]{1,0:T(8,128)(2,1)S(1)}, u32[]{:S(2)}, u32[]{:S(2)}) collective-permute-start(bf16[128,768]{1,0:T(8,128)(2,1)S(1)} %shard_map.232.refs_1_.refs_2_.refs_0_), channel_id=1, source_target_pairs={{0,8},{4,12},{8,0},{12,4},{1,9},{5,13},{9,1},{13,5},{2,10},{6,14},... | collective-permute-start | bytes 589832 | tf_op jit(solution)/shard_map/ppermute | solution.py:21
  173.2 12.4 %collective-permute-start.52 = (bf16[192,768]{1,0:T(8,128)(2,1)S(1)}, bf16[192,768]{1,0:T(8,128)(2,1)S(1)}, u32[]{:S(2)}, u32[]{:S(2)}) collective-permute-start(bf16[192,768]{1,0:T(8,128)(2,1)S(1)} %get-tuple-element.167), channel_id=1, source_target_pairs={{0,2},{1,3},{2,0},{3,1},{4,6},{5,7},{6,4},{7,5},{8,10},{9,11},{10,... | collective-permute-start | bytes 884744 | tf_op jit(solution)/shard_map/ppermute | solution.py:21
  174.3 11.3 %collective-permute-start.51 = (bf16[128,768]{1,0:T(8,128)(2,1)S(1)}, bf16[128,768]{1,0:T(8,128)(2,1)S(1)}, u32[]{:S(2)}, u32[]{:S(2)}) collective-permute-start(bf16[128,768]{1,0:T(8,128)(2,1)S(1)} %shard_map.242.refs_2_.refs_1_), channel_id=1, source_target_pairs={{0,8},{4,12},{8,0},{12,4},{1,9},{5,13},{9,1},{13,5},{2,10},{6,14},... | collective-permute-start | bytes 589832 | tf_op jit(solution)/shard_map/ppermute | solution.py:21
  191.1 11.1 %collective-permute-start.61 = (bf16[208,768]{1,0:T(8,128)(2,1)S(1)}, bf16[208,768]{1,0:T(8,128)(2,1)S(1)}, u32[]{:S(2)}, u32[]{:S(2)}) collective-permute-start(bf16[208,768]{1,0:T(8,128)(2,1)S(1)} %get-tuple-element.188), channel_id=1, source_target_pairs={{0,2},{1,3},{2,0},{3,1},{4,6},{5,7},{6,4},{7,5},{8,10},{9,11},{10,... | collective-permute-start | bytes 958472 | tf_op jit(solution)/shard_map/ppermute | solution.py:21
  192.3 22.6 %collective-permute-start.64 = (bf16[288,768]{1,0:T(8,128)(2,1)S(1)}, bf16[288,768]{1,0:T(8,128)(2,1)S(1)}, u32[]{:S(2)}, u32[]{:S(2)}) collective-permute-start(bf16[288,768]{1,0:T(8,128)(2,1)S(1)} %shard_map.253.refs_0_.refs_1_.refs_2_), channel_id=1, source_target_pairs={{0,16},{16,0},{1,17},{17,1},{2,18},{18,2},{3,19},{19,3},{4,20},{20... | collective-permute-start | bytes 1327112 | tf_op jit(solution)/shard_map/ppermute | solution.py:21
  202.4 15.0 %collective-permute-start.62 = (bf16[208,768]{1,0:T(8,128)(2,1)S(1)}, bf16[208,768]{1,0:T(8,128)(2,1)S(1)}, u32[]{:S(2)}, u32[]{:S(2)}) collective-permute-start(bf16[208,768]{1,0:T(8,128)(2,1)S(1)} %shard_map.251.refs_0_), channel_id=1, source_target_pairs={{0,16},{16,0},{1,17},{17,1},{2,18},{18,2},{3,19},{19,3},{4,20},{20... | collective-permute-start | bytes 958472 | tf_op jit(solution)/shard_map/ppermute | solution.py:21
  204.0 10.9 %collective-permute-start.65 = (bf16[96,768]{1,0:T(8,128)(2,1)S(1)}, bf16[96,768]{1,0:T(8,128)(2,1)S(1)}, u32[]{:S(2)}, u32[]{:S(2)}) collective-permute-start(bf16[96,768]{1,0:T(8,128)(2,1)S(1)} %shard_map.255.refs_3_), channel_id=1, source_target_pairs={{0,16},{16,0},{1,17},{17,1},{2,18},{18,2},{3,19},{19,3},{4,20},{20... | collective-permute-start | bytes 442376 | tf_op jit(solution)/shard_map/ppermute | solution.py:21
  205.0 9.3 %collective-permute-start.59 = (f32[192,128]{1,0:T(8,128)S(1)}, f32[192,128]{1,0:T(8,128)S(1)}, u32[]{:S(2)}, u32[]{:S(2)}) collective-permute-start(f32[192,128]{1,0:T(8,128)S(1)} %shard_map.247.refs_2_), channel_id=1, source_target_pairs={{0,0},{1,4},{2,8},{3,12},{4,1},{5,5},{6,9},{7,13},{8,2},{9,6},{10,... | collective-permute-start | bytes 294920 | tf_op jit(solution)/shard_map/ppermute | solution.py:27
  (52 other events, 347.0 us)

commit v5 on v4

--- a/solution.py
+++ b/solution.py
@@ -66,6 +66,7 @@
             moved += item.size * item.dtype.itemsize
     moved += sum(o.size * o.dtype.itemsize for o in outs)
     n_in, n_after, n_out = len(ins), len(after), len(outs)
+    final = n_out if final is True else final
 
     def body(*refs):
         inputs = list(refs[:n_in])
@@ -85,9 +86,9 @@
         in_specs=specs + [pl.BlockSpec(memory_space=pl.ANY)] * n_after,
         out_specs=[
             pl.BlockSpec(o.shape, lambda i, d=len(o.shape): (0,) * d)
-            if final
+            if final and i < final
             else vmem
-            for o in outs
+            for i, o in enumerate(outs)
         ],
         scratch_shapes=list(scratch),
         compiler_params=pltpu.CompilerParams(vmem_limit_bytes=vmem_mib * 1024 * 1024),
@@ -275,6 +276,13 @@
     rowwise[...] = low.astype(BF16)
 
 
+def k_results(ins, outs, scr):
+    piece = outs[0].shape[0]
+    outs[0][...] = ins[0][piece:, :]
+    outs[1][...] = ins[0][:piece, :].astype(F32)
+    outs[2][...] = jnp.zeros(outs[2].shape, F32)
+
+
 def k_split(ins, outs, scr):
     attn, up, down = ins
     half = outs[0].shape[0]
@@ -431,7 +439,10 @@
 
 
 def k_total(ins, outs, scr):
-    outs[0][...] = (ins[0][...] + ((f32(ins[1]) + f32(ins[2])) + f32(ins[3]))).T
+    piece = ins[0].shape[1]
+    total = ins[0][...] + ((f32(ins[1]) + f32(ins[2])) + f32(ins[3]))
+    outs[0][:piece, :] = total.T.astype(BF16)
+    outs[0][piece:, :] = ins[4][...]
 
 
 def k_feed_weight(m, ins, outs, scr):
@@ -603,7 +614,10 @@
     down0, attn1, up1, down1 = [halves[2 * i : 2 * i + 2] for i in range(4)]
     up0 = pack(piece, [layer_of(w_up, 0)], [mine])
     (up0_along,) = along_of([up0])
-    attn0 = gathered([block], [along], piece + 16, [*x_in[1:], up0_along])
+    near = exchange(block, "col", 1)
+    (low,) = held([along], [*x_in[1:], up0_along])
+    sources = (block, near, along, exchange(low, "col", 1))
+    attn0 = [(a, (piece + 16, hidden), (0, 0)) for a in sources]
 
     low_tile = sds(tile, BF16)
     unit_out = sds((tokens, model + 128), F32)
@@ -622,7 +636,9 @@
         after=[down0[0]],
     )
     down0_along = along_of(down0)
-    z = pair_sum(z, down0_along)
+    (low,) = call(k_turned, [sds((tokens, piece), BF16)], [whole(cotangent.T)], after=[z], final=True)
+    cotan = turned(low)
+    z = pair_sum(z, [*down0_along, cotan])
     up0 = gathered([up0], [up0_along], after=[z])
     down0 = gathered(down0, down0_along, after=[z])
     attn1_along = along_of(attn1)
@@ -634,9 +650,7 @@
     )
     attn1 = gathered(attn1, attn1_along, after=[f])
     up1_along = along_of(up1[:1])
-    (low,) = call(k_turned, [sds((tokens, piece), BF16)], [whole(cotangent.T)], after=[f], final=True)
-    cotan = turned(low)
-    f = pair_sum(f, [attn1[1][0], *up1_along, cotan])
+    f = pair_sum(f, [attn1[1][0], *up1_along])
     up1_along += along_of(up1[1:])
     down1_along = along_of(down1[:1])
     z, unit_b0, x1, o1, qkv1, p1 = call(
@@ -655,8 +669,9 @@
         [*both(z), unit_b0, *up1, *down1, rowwise, prm],
     )
     (again,) = held([cotan], [f])
-    cotan = [cotan] + [exchange(again, "row", k) for k in range(1, n)]
-    f = pair_sum(f, cotan[1:])
+    cotan = [cotan, None] + [exchange(again, "row", k) for k in range(2, n)]
+    f = pair_sum(f, cotan[2:])
+    cotan[1] = exchange(held([again], [f])[0], "row", 1)
     (cotan,) = call(k_prep, [sds(tile, BF16)], [sc, *cotan], after=[f])
 
     sums_out = sds((8, model), F32)
@@ -667,7 +682,6 @@
         [sc, *both(f), unit_a1, cotan, *up1, *down1, slope1, prm],
         [pltpu.VMEM((tokens, piece), F32)],
     )
-    out_hidden = turned(out)
     weight_out = [sds((4 * piece, hidden), BF16)] * 2 + [sds((8, hidden), F32)]
     keep, send, hidden_sums1 = call(
         partial(k_feed_weight, m), weight_out, [df_low, g1, h1, du]
@@ -692,7 +706,6 @@
     (low,) = call(k_add, [half_block], [stay1[0], more1[0]], after=[dx])
     terms1 = [last_of_dp(low)]
     dx = pair_sum(dx, [got, more1[2], terms1[0][1]])
-    (out_hidden,) = held([out_hidden], [dx])
     attn1_stay = call(k_middle, [half_block] * 4, [keep, got], after=[dx])
     more1 += along_of(held(stay1[7:], [dx]))
     attn1_more = along_of(attn1_stay[2:3])
@@ -704,7 +717,7 @@
         partial(k_feed_back, m, 0),
         feed_back_out,
         [*both(dx), da, unit_b0, *up0, *down0, slope0, prm],
-        after=[more1[3], *attn1_more, terms1[1][1], terms1[2][1], out_hidden],
+        after=[more1[3], *attn1_more, terms1[1][1], terms1[2][1]],
     )
     keep, send, hidden_sums0 = call(
         partial(k_feed_weight, m), weight_out, [df_low, g0, h0, du]
@@ -734,12 +747,17 @@
     most = [sds((3 * piece // 2, hidden), BF16)]
     (low,) = call(k_add_whole, most, [*stay0[:3], *more0[:2]])
     most0_terms = last_of_dp(low)
-    (grad_total,) = call(
+    (results,) = call(
         k_total,
-        [sds((piece, tokens), F32)],
-        [dx[0]] + [exchange(dx[k], "row", k) for k in range(1, n)],
-    )
-    (grad_input,) = held([turned(grad_total)], [])
+        [sds((2 * piece, tokens), BF16)],
+        [dx[0]] + [exchange(dx[k], "row", k) for k in range(1, n)] + [out],
+    )
+    out_hidden, grad_input, token = call(
+        k_results,
+        [sds((piece, tokens), BF16), sds((piece, tokens), F32), sds((8, 128), F32)],
+        [turned(results)],
+        final=2,
+    )
 
     keep, send = call(
         partial(k_attend_weight_last, m),
@@ -764,7 +782,7 @@
     (attn0_more,) = along_of([attn0_go])
     (low,) = call(k_add, [half_block], [stay0[3], more0[2]])
     rest0_terms = last_of_dp(low)
-    (low,) = call(k_add, [low_tail], [attn0_stay, attn0_more], after=[grad_total])
+    (low,) = call(k_add, [low_tail], [attn0_stay, attn0_more], after=[results])
     attn0_terms = [last_of_dp(low)]
     def halves_of(array):
         return [(array, (piece // 2, hidden), (i, 0)) for i in range(3)]
@@ -775,7 +793,7 @@
         k_feed_outputs,
         [sds((layers, piece, hidden), F32)] * 2,
         [*first[0], *second[0], *first[1], *second[1]],
-        after=[grad_input],
+        after=[token],
         final=True,
     )
     grad_attn, grad_qv, grad_out, grad_gain, grad_shift, grad_b_up, grad_b_down = call(

time: 220 us -> 216 us (0.982)
  local copies, waits for them, and re-layouts: 3.99 us -> 1.1 us
    ppermute x4 -> x3, starting transfers between devices: 17.5 us -> 11.3 us  [turned(): return lax.ppermute(x, ('row', 'col'), pairs)]
    ppermute x62 -> x63, starting transfers between devices: 45.6 us -> 49.7 us  [exchange(): return lax.ppermute(x, axis, [(i, i ^ bit) for i in range(n)])]
    unnamed x20 -> x16, local copies, waits for them, and re-layouts: 3.99 us -> 1.1 us
    ppermute x62 -> x63, waiting for transfers between devices: 109 us -> 111 us  [exchange(): return lax.ppermute(x, axis, [(i, i ^ bit) for i in range(n)])]
    ppermute x4 -> x3, waiting for transfers between devices: 15.2 us -> 14.4 us  [turned(): return lax.ppermute(x, ('row', 'col'), pairs)]
  transfers between devices with their start and end apart: 66 -> 66, of which waited for: 41 -> 46; matrix products, arithmetic and copies ran while one was open for 0% -> 0% of each run, Pallas kernels for 3% -> 2%
where the time goes in v5:
time: 216 us; the launch traced here: 215 us
  waiting for transfers between devices  126 us (58%)
  starting transfers between devices  61 us (28%)
  Pallas kernels  25.6 us (12%)
    ppermute x63, waiting for transfers between devices, exchange(): return lax.ppermute(x, axis, [(i, i ^ bit) for i in range(n)])  111 us
    ppermute x63, starting transfers between devices, exchange(): return lax.ppermute(x, axis, [(i, i ^ bit) for i in range(n)])  49.7 us
    pallas_call x54, Pallas kernels, call(): pl.pallas_call(body, grid=(1,), out_shape=outs, in_specs=specs + [pl.Bloc...  25.6 us
    ppermute x3, waiting for transfers between devices, turned(): return lax.ppermute(x, ('row', 'col'), pairs)  14.4 us
    ppermute x3, starting transfers between devices, turned(): return lax.ppermute(x, ('row', 'col'), pairs)  11.3 us
  transfers between devices with their start and end apart: 66, of which 46 were waited for; matrix products, arithmetic and copies ran while one was open for 0% of the time, Pallas kernels for 2%

profile of v5, /device:TPU:2, one launch (start us, length us, event | category | flops | bytes accessed | tf_op | source)
XLA Modules:
  0.0 214.7 jit_solution(4887061784875420528)
XLA Ops:
  3.2 4.5 %collective-permute-start = (bf16[128,192]{1,0:T(8,128)(2,1)}, bf16[128,192]{1,0:T(8,128)(2,1)S(1)}, u32[]{:S(2)}, u32[]{:S(2)}) collective-permute-start(bf16[128,192]{1,0:T(8,128)(2,1)} %get-tuple-element.110), channel_id=1, source_target_pairs={{0,0},{1,4},{2,8},{3,12},{4,1},{5,5},{6,9},{7,13},{8,2},{9,6},{10,... | collective-permute-start | bytes 147464 | tf_op jit(solution)/shard_map/ppermute | solution.py:27
  7.8 5.3 %collective-permute-done.refs_1_ = bf16[128,192]{1,0:T(8,128)(2,1)S(1)} collective-permute-done((bf16[128,192]{1,0:T(8,128)(2,1)}, bf16[128,192]{1,0:T(8,128)(2,1)S(1)}, u32[]{:S(2)}, u32[]{:S(2)}) %collective-permute-start) | collective-permute-done | bytes 49184 | tf_op jit(solution)/shard_map/ppermute | solution.py:27
  14.2 3.1 %collective-permute-start.3 = (bf16[128,192]{1,0:T(8,128)(2,1)S(1)}, bf16[128,192]{1,0:T(8,128)(2,1)S(1)}, u32[]{:S(2)}, u32[]{:S(2)}) collective-permute-start(bf16[128,192]{1,0:T(8,128)(2,1)S(1)} %collective-permute-done.refs_1_), channel_id=1, source_target_pairs={{0,12},{4,8},{8,4},{12,0},{1,13},{5,9},{9,5},{13,1},{2,14},{6,10},... | collective-permute-start | bytes 147464 | tf_op jit(solution)/shard_map/ppermute | solution.py:21
  22.5 3.3 %collective-permute-done.6.refs_4_.refs_1_ = bf16[192,768]{1,0:T(8,128)(2,1)S(1)} collective-permute-done((bf16[192,768]{1,0:T(8,128)(2,1)S(1)}, bf16[192,768]{1,0:T(8,128)(2,1)S(1)}, u32[]{:S(2)}, u32[]{:S(2)}) %collective-permute-start.6) | collective-permute-done | bytes 294944 | tf_op jit(solution)/shard_map/ppermute | solution.py:21
  31.5 3.6 %collective-permute-start.11 = (bf16[128,192]{1,0:T(8,128)(2,1)S(1)}, bf16[128,192]{1,0:T(8,128)(2,1)S(1)}, u32[]{:S(2)}, u32[]{:S(2)}) collective-permute-start(bf16[128,192]{1,0:T(8,128)(2,1)S(1)} %shard_map.209), channel_id=1, source_target_pairs={{0,0},{1,4},{2,8},{3,12},{4,1},{5,5},{6,9},{7,13},{8,2},{9,6},{10,... | collective-permute-start | bytes 147464 | tf_op jit(solution)/shard_map/ppermute | solution.py:27
  38.4 2.9 %collective-permute-done.11.refs_4_.refs_0_.refs_1_ = bf16[128,192]{1,0:T(8,128)(2,1)S(1)} collective-permute-done((bf16[128,192]{1,0:T(8,128)(2,1)S(1)}, bf16[128,192]{1,0:T(8,128)(2,1)S(1)}, u32[]{:S(2)}, u32[]{:S(2)}) %collective-permute-start.11) | collective-permute-done | bytes 49184 | tf_op jit(solution)/shard_map/ppermute | solution.py:27
  44.1 4.7 %collective-permute-done.15.refs_13_.refs_2_ = bf16[96,768]{1,0:T(8,128)(2,1)S(1)} collective-permute-done((bf16[96,768]{1,0:T(8,128)(2,1)S(1)}, bf16[96,768]{1,0:T(8,128)(2,1)S(1)}, u32[]{:S(2)}, u32[]{:S(2)}) %collective-permute-start.15) | collective-permute-done | bytes 147488 | tf_op jit(solution)/shard_map/ppermute | solution.py:21
  51.1 2.9 %collective-permute-done.12.refs_1_ = bf16[128,768]{1,0:T(8,128)(2,1)S(1)} collective-permute-done((bf16[128,768]{1,0:T(8,128)(2,1)S(1)}, bf16[128,768]{1,0:T(8,128)(2,1)S(1)}, u32[]{:S(2)}, u32[]{:S(2)}) %collective-permute-start.12) | collective-permute-done | bytes 196640 | tf_op jit(solution)/shard_map/ppermute | solution.py:21
  55.3 6.1 %collective-permute-done.19.refs_3_.refs_2_ = bf16[96,768]{1,0:T(8,128)(2,1)S(1)} collective-permute-done((bf16[96,768]{1,0:T(8,128)(2,1)S(1)}, bf16[96,768]{1,0:T(8,128)(2,1)S(1)}, u32[]{:S(2)}, u32[]{:S(2)}) %collective-permute-start.19) | collective-permute-done | bytes 147488 | tf_op jit(solution)/shard_map/ppermute | solution.py:21
  64.7 4.7 %collective-permute-done.21.refs_10_.refs_3_ = bf16[96,768]{1,0:T(8,128)(2,1)S(1)} collective-permute-done((bf16[96,768]{1,0:T(8,128)(2,1)S(1)}, bf16[96,768]{1,0:T(8,128)(2,1)S(1)}, u32[]{:S(2)}, u32[]{:S(2)}) %collective-permute-start.21) | collective-permute-done | bytes 147488 | tf_op jit(solution)/shard_map/ppermute | solution.py:21
  71.2 2.8 %collective-permute-done.20.refs_2_ = bf16[128,768]{1,0:T(8,128)(2,1)S(1)} collective-permute-done((bf16[128,768]{1,0:T(8,128)(2,1)S(1)}, bf16[128,768]{1,0:T(8,128)(2,1)S(1)}, u32[]{:S(2)}, u32[]{:S(2)}) %collective-permute-start.20) | collective-permute-done | bytes 196640 | tf_op jit(solution)/shard_map/ppermute | solution.py:21
  76.3 6.1 %collective-permute-done.24.refs_2_.refs_3_ = bf16[96,768]{1,0:T(8,128)(2,1)S(1)} collective-permute-done((bf16[96,768]{1,0:T(8,128)(2,1)S(1)}, bf16[96,768]{1,0:T(8,128)(2,1)S(1)}, u32[]{:S(2)}, u32[]{:S(2)}) %collective-permute-start.24) | collective-permute-done | bytes 147488 | tf_op jit(solution)/shard_map/ppermute | solution.py:21
  83.7 12.4 %collective-permute-done.26.refs_1_ = bf16[128,768]{1,0:T(8,128)(2,1)S(1)} collective-permute-done((bf16[128,768]{1,0:T(8,128)(2,1)S(1)}, bf16[128,768]{1,0:T(8,128)(2,1)S(1)}, u32[]{:S(2)}, u32[]{:S(2)}) %collective-permute-start.26) | collective-permute-done | bytes 196640 | tf_op jit(solution)/shard_map/ppermute | solution.py:21
  100.6 4.5 %collective-permute-done.30.refs_3_.refs_4_ = bf16[128,192]{1,0:T(8,128)(2,1)S(1)} collective-permute-done((bf16[128,192]{1,0:T(8,128)(2,1)S(1)}, bf16[128,192]{1,0:T(8,128)(2,1)S(1)}, u32[]{:S(2)}, u32[]{:S(2)}) %collective-permute-start.30) | collective-permute-done | bytes 49184 | tf_op jit(solution)/shard_map/ppermute | solution.py:21
  109.5 3.3 %collective-permute-done.32.refs_2_ = bf16[128,192]{1,0:T(8,128)(2,1)S(1)} collective-permute-done((bf16[128,192]{1,0:T(8,128)(2,1)S(1)}, bf16[128,192]{1,0:T(8,128)(2,1)S(1)}, u32[]{:S(2)}, u32[]{:S(2)}) %collective-permute-start.32) | collective-permute-done | bytes 49184 | tf_op jit(solution)/shard_map/ppermute | solution.py:21
  113.6 2.8 %collective-permute-done.31.refs_2_ = bf16[128,768]{1,0:T(8,128)(2,1)S(1)} collective-permute-done((bf16[128,768]{1,0:T(8,128)(2,1)S(1)}, bf16[128,768]{1,0:T(8,128)(2,1)S(1)}, u32[]{:S(2)}, u32[]{:S(2)}) %collective-permute-start.31) | collective-permute-done | bytes 196640 | tf_op jit(solution)/shard_map/ppermute | solution.py:21
  119.2 7.2 %collective-permute-done.33.refs_1_ = bf16[128,768]{1,0:T(8,128)(2,1)S(1)} collective-permute-done((bf16[128,768]{1,0:T(8,128)(2,1)S(1)}, bf16[128,768]{1,0:T(8,128)(2,1)S(1)}, u32[]{:S(2)}, u32[]{:S(2)}) %collective-permute-start.33) | collective-permute-done | bytes 196640 | tf_op jit(solution)/shard_map/ppermute | solution.py:21
  129.9 4.7 %collective-permute-done.36.refs_11_.refs_1_ = bf16[96,768]{1,0:T(8,128)(2,1)S(1)} collective-permute-done((bf16[96,768]{1,0:T(8,128)(2,1)S(1)}, bf16[96,768]{1,0:T(8,128)(2,1)S(1)}, u32[]{:S(2)}, u32[]{:S(2)}) %collective-permute-start.36) | collective-permute-done | bytes 147488 | tf_op jit(solution)/shard_map/ppermute | solution.py:21
  142.5 4.4 %collective-permute-done.40.refs_3_.refs_1_ = bf16[96,768]{1,0:T(8,128)(2,1)S(1)} collective-permute-done((bf16[96,768]{1,0:T(8,128)(2,1)S(1)}, bf16[96,768]{1,0:T(8,128)(2,1)S(1)}, u32[]{:S(2)}, u32[]{:S(2)}) %collective-permute-start.40) | collective-permute-done | bytes 147488 | tf_op jit(solution)/shard_map/ppermute | solution.py:21
  165.1 3.7 %collective-permute-done.49.refs_3_.refs_1_ = bf16[96,768]{1,0:T(8,128)(2,1)S(1)} collective-permute-done((bf16[96,768]{1,0:T(8,128)(2,1)S(1)}, bf16[96,768]{1,0:T(8,128)(2,1)S(1)}, u32[]{:S(2)}, u32[]{:S(2)}) %collective-permute-start.49) | collective-permute-done | bytes 147488 | tf_op jit(solution)/shard_map/ppermute | solution.py:21
  175.6 5.4 %collective-permute-done.53.refs_13_.refs_4_ = bf16[96,768]{1,0:T(8,128)(2,1)S(1)} collective-permute-done((bf16[96,768]{1,0:T(8,128)(2,1)S(1)}, bf16[96,768]{1,0:T(8,128)(2,1)S(1)}, u32[]{:S(2)}, u32[]{:S(2)}) %collective-permute-start.53) | collective-permute-done | bytes 147488 | tf_op jit(solution)/shard_map/ppermute | solution.py:21
  181.8 2.6 %shard_map.246 = (f32[128,192]{1,0:T(8,128)S(1)}, bf16[128,192]{1,0:T(8,128)(2,1)S(1)}, bf16[128,192]{1,0:T(8,128)(2,1)S(1)}, bf16[128,192]{1,0:T(8,128)(2,1)S(1...) custom-call(s32[4]{0:T(128)S(1)} %copy-done.6, ...), custom_call_target="tpu_custom_call" | custom-call | flops 200000000 | bytes 3530752 | tf_op jit(solution)/shard_map/pallas_call | solution.py:82
  201.8 3.2 %collective-permute-start.59 = (bf16[384,128]{1,0:T(8,128)(2,1)S(1)}, bf16[384,128]{1,0:T(8,128)(2,1)S(1)}, u32[]{:S(2)}, u32[]{:S(2)}) collective-permute-start(bf16[384,128]{1,0:T(8,128)(2,1)S(1)} %shard_map.247.refs_2_), channel_id=1, source_target_pairs={{0,0},{1,4},{2,8},{3,12},{4,1},{5,5},{6,9},{7,13},{8,2},{9,6},{10,... | collective-permute-start | bytes 294920 | tf_op jit(solution)/shard_map/ppermute | solution.py:27
  205.0 6.2 %collective-permute-done.59.refs_0_ = bf16[384,128]{1,0:T(8,128)(2,1)S(1)} collective-permute-done((bf16[384,128]{1,0:T(8,128)(2,1)S(1)}, bf16[384,128]{1,0:T(8,128)(2,1)S(1)}, u32[]{:S(2)}, u32[]{:S(2)}) %collective-permute-start.59) | collective-permute-done | bytes 98336 | tf_op jit(solution)/shard_map/ppermute | solution.py:27
  (178 shorter events, 103.0 us)
Async XLA Ops:
  3.2 9.9 %collective-permute-start = (bf16[128,192]{1,0:T(8,128)(2,1)}, bf16[128,192]{1,0:T(8,128)(2,1)S(1)}, u32[]{:S(2)}, u32[]{:S(2)}) collective-permute-start(bf16[128,192]{1,0:T(8,128)(2,1)} %get-tuple-element.110), channel_id=1, source_target_pairs={{0,0},{1,4},{2,8},{3,12},{4,1},{5,5},{6,9},{7,13},{8,2},{9,6},{10,... | collective-permute-start | bytes 147464 | tf_op jit(solution)/shard_map/ppermute | solution.py:27
  7.7 14.8 %collective-permute-start.5 = (bf16[208,768]{1,0:T(8,128)(2,1)}, bf16[208,768]{1,0:T(8,128)(2,1)S(1)}, u32[]{:S(2)}, u32[]{:S(2)}) collective-permute-start(bf16[208,768]{1,0:T(8,128)(2,1)} %get-tuple-element.111.refs_2_.refs_5_), channel_id=1, source_target_pairs={{0,2},{1,3},{2,0},{3,1},{4,6},{5,7},{6,4},{7,5},{8,10},{9,11},{10,... | collective-permute-start | bytes 958472 | tf_op jit(solution)/shard_map/ppermute | solution.py:21
  14.1 11.6 %collective-permute-start.6 = (bf16[192,768]{1,0:T(8,128)(2,1)S(1)}, bf16[192,768]{1,0:T(8,128)(2,1)S(1)}, u32[]{:S(2)}, u32[]{:S(2)}) collective-permute-start(bf16[192,768]{1,0:T(8,128)(2,1)S(1)} %shard_map.205.refs_0_), channel_id=1, source_target_pairs={{0,2},{1,3},{2,0},{3,1},{4,6},{5,7},{6,4},{7,5},{8,10},{9,11},{10,... | collective-permute-start | bytes 884744 | tf_op jit(solution)/shard_map/ppermute | solution.py:21
  29.2 12.1 %collective-permute-start.8 = (bf16[128,768]{1,0:T(8,128)(2,1)S(1)}, bf16[128,768]{1,0:T(8,128)(2,1)S(1)}, u32[]{:S(2)}, u32[]{:S(2)}) collective-permute-start(bf16[128,768]{1,0:T(8,128)(2,1)S(1)} %get-tuple-element.114.refs_1_.refs_0_), channel_id=1, source_target_pairs={{0,4},{4,0},{8,12},{12,8},{1,5},{5,1},{9,13},{13,9},{2,6},{6,2},{1... | collective-permute-start | bytes 589832 | tf_op jit(solution)/shard_map/ppermute | solution.py:21
  29.3 9.0 %collective-permute-start.9 = (bf16[96,768]{1,0:T(8,128)(2,1)S(1)}, bf16[96,768]{1,0:T(8,128)(2,1)S(1)}, u32[]{:S(2)}, u32[]{:S(2)}) collective-permute-start(bf16[96,768]{1,0:T(8,128)(2,1)S(1)} %get-tuple-element.113.refs_7_.refs_0_), channel_id=1, source_target_pairs={{0,2},{1,3},{2,0},{3,1},{4,6},{5,7},{6,4},{7,5},{8,10},{9,11},{10,... | collective-permute-start | bytes 442376 | tf_op jit(solution)/shard_map/ppermute | solution.py:21
  31.5 9.8 %collective-permute-start.11 = (bf16[128,192]{1,0:T(8,128)(2,1)S(1)}, bf16[128,192]{1,0:T(8,128)(2,1)S(1)}, u32[]{:S(2)}, u32[]{:S(2)}) collective-permute-start(bf16[128,192]{1,0:T(8,128)(2,1)S(1)} %shard_map.209), channel_id=1, source_target_pairs={{0,0},{1,4},{2,8},{3,12},{4,1},{5,5},{6,9},{7,13},{8,2},{9,6},{10,... | collective-permute-start | bytes 147464 | tf_op jit(solution)/shard_map/ppermute | solution.py:27
  41.3 12.7 %collective-permute-start.13 = (bf16[384,768]{1,0:T(8,128)(2,1)S(1)}, bf16[384,768]{1,0:T(8,128)(2,1)S(1)}, u32[]{:S(2)}, u32[]{:S(2)}) collective-permute-start(bf16[384,768]{1,0:T(8,128)(2,1)S(1)} %shard_map.211.refs_3_.refs_5_.refs_4_.refs_6_), channel_id=1, source_target_pairs={{0,1},{1,0},{2,3},{3,2},{4,5},{5,4},{6,7},{7,6},{8,9},{9,8},{10,11... | collective-permute-start | bytes 1769480 | tf_op jit(solution)/shard_map/ppermute | solution.py:21
  41.5 12.6 %collective-permute-start.14 = (bf16[384,768]{1,0:T(8,128)(2,1)S(1)}, bf16[384,768]{1,0:T(8,128)(2,1)S(1)}, u32[]{:S(2)}, u32[]{:S(2)}) collective-permute-start(bf16[384,768]{1,0:T(8,128)(2,1)S(1)} %shard_map.212.refs_7_.refs_9_.refs_8_.refs_10_), channel_id=1, source_target_pairs={{0,1},{1,0},{2,3},{3,2},{4,5},{5,4},{6,7},{7,6},{8,9},{9,8},{10,11... | collective-permute-start | bytes 1769480 | tf_op jit(solution)/shard_map/ppermute | solution.py:21
  42.0 12.0 %collective-permute-start.12 = (bf16[128,768]{1,0:T(8,128)(2,1)S(1)}, bf16[128,768]{1,0:T(8,128)(2,1)S(1)}, u32[]{:S(2)}, u32[]{:S(2)}) collective-permute-start(bf16[128,768]{1,0:T(8,128)(2,1)S(1)} %shard_map.210.refs_2_.refs_4_.refs_0_), channel_id=1, source_target_pairs={{0,8},{4,12},{8,0},{12,4},{1,9},{5,13},{9,1},{13,5},{2,10},{6,14},... | collective-permute-start | bytes 589832 | tf_op jit(solution)/shard_map/ppermute | solution.py:21
  62.5 11.5 %collective-permute-start.20 = (bf16[128,768]{1,0:T(8,128)(2,1)S(1)}, bf16[128,768]{1,0:T(8,128)(2,1)S(1)}, u32[]{:S(2)}, u32[]{:S(2)}) collective-permute-start(bf16[128,768]{1,0:T(8,128)(2,1)S(1)} %shard_map.215.refs_1_), channel_id=1, source_target_pairs={{0,8},{4,12},{8,0},{12,4},{1,9},{5,13},{9,1},{13,5},{2,10},{6,14},... | collective-permute-start | bytes 589832 | tf_op jit(solution)/shard_map/ppermute | solution.py:21
  83.5 12.5 %collective-permute-start.27 = (bf16[384,768]{1,0:T(8,128)(2,1)S(1)}, bf16[384,768]{1,0:T(8,128)(2,1)S(1)}, u32[]{:S(2)}, u32[]{:S(2)}) collective-permute-start(bf16[384,768]{1,0:T(8,128)(2,1)S(1)} %shard_map.219.refs_7_.refs_9_.refs_11_), channel_id=1, source_target_pairs={{0,1},{1,0},{2,3},{3,2},{4,5},{5,4},{6,7},{7,6},{8,9},{9,8},{10,11... | collective-permute-start | bytes 1769480 | tf_op jit(solution)/shard_map/ppermute | solution.py:21
  83.6 12.4 %collective-permute-start.26 = (bf16[128,768]{1,0:T(8,128)(2,1)S(1)}, bf16[128,768]{1,0:T(8,128)(2,1)S(1)}, u32[]{:S(2)}, u32[]{:S(2)}) collective-permute-start(bf16[128,768]{1,0:T(8,128)(2,1)S(1)} %shard_map.218.refs_4_.refs_0_), channel_id=1, source_target_pairs={{0,8},{4,12},{8,0},{12,4},{1,9},{5,13},{9,1},{13,5},{2,10},{6,14},... | collective-permute-start | bytes 589832 | tf_op jit(solution)/shard_map/ppermute | solution.py:21
  97.0 9.6 %collective-permute-start.28 = (bf16[128,768]{1,0:T(8,128)(2,1)S(1)}, bf16[128,768]{1,0:T(8,128)(2,1)S(1)}, u32[]{:S(2)}, u32[]{:S(2)}) collective-permute-start(bf16[128,768]{1,0:T(8,128)(2,1)S(1)} %get-tuple-element.127.refs_1_.refs_0_), channel_id=1, source_target_pairs={{0,4},{4,0},{8,12},{12,8},{1,5},{5,1},{9,13},{13,9},{2,6},{6,2},{1... | collective-permute-start | bytes 589832 | tf_op jit(solution)/shard_map/ppermute | solution.py:21
  106.7 9.7 %collective-permute-start.31 = (bf16[128,768]{1,0:T(8,128)(2,1)S(1)}, bf16[128,768]{1,0:T(8,128)(2,1)S(1)}, u32[]{:S(2)}, u32[]{:S(2)}) collective-permute-start(bf16[128,768]{1,0:T(8,128)(2,1)S(1)} %shard_map.222.refs_1_.refs_5_), channel_id=1, source_target_pairs={{0,8},{4,12},{8,0},{12,4},{1,9},{5,13},{9,1},{13,5},{2,10},{6,14},... | collective-permute-start | bytes 589832 | tf_op jit(solution)/shard_map/ppermute | solution.py:21
  126.5 11.5 %collective-permute-start.35 = (bf16[128,768]{1,0:T(8,128)(2,1)S(1)}, bf16[128,768]{1,0:T(8,128)(2,1)S(1)}, u32[]{:S(2)}, u32[]{:S(2)}) collective-permute-start(bf16[128,768]{1,0:T(8,128)(2,1)S(1)} %shard_map.227.refs_2_.refs_0_), channel_id=1, source_target_pairs={{0,8},{4,12},{8,0},{12,4},{1,9},{5,13},{9,1},{13,5},{2,10},{6,14},... | collective-permute-start | bytes 589832 | tf_op jit(solution)/shard_map/ppermute | solution.py:21
  127.9 8.5 %collective-permute-start.37 = (bf16[96,768]{1,0:T(8,128)(2,1)S(1)}, bf16[96,768]{1,0:T(8,128)(2,1)S(1)}, u32[]{:S(2)}, u32[]{:S(2)}) collective-permute-start(bf16[96,768]{1,0:T(8,128)(2,1)S(1)} %get-tuple-element.141), channel_id=1, source_target_pairs={{0,2},{1,3},{2,0},{3,1},{4,6},{5,7},{6,4},{7,5},{8,10},{9,11},{10,... | collective-permute-start | bytes 442376 | tf_op jit(solution)/shard_map/ppermute | solution.py:21
  148.0 11.6 %collective-permute-start.42 = (bf16[128,768]{1,0:T(8,128)(2,1)S(1)}, bf16[128,768]{1,0:T(8,128)(2,1)S(1)}, u32[]{:S(2)}, u32[]{:S(2)}) collective-permute-start(bf16[128,768]{1,0:T(8,128)(2,1)S(1)} %shard_map.233.refs_1_.refs_2_.refs_0_), channel_id=1, source_target_pairs={{0,8},{4,12},{8,0},{12,4},{1,9},{5,13},{9,1},{13,5},{2,10},{6,14},... | collective-permute-start | bytes 589832 | tf_op jit(solution)/shard_map/ppermute | solution.py:21
  169.6 12.2 %collective-permute-start.52 = (bf16[192,768]{1,0:T(8,128)(2,1)S(1)}, bf16[192,768]{1,0:T(8,128)(2,1)S(1)}, u32[]{:S(2)}, u32[]{:S(2)}) collective-permute-start(bf16[192,768]{1,0:T(8,128)(2,1)S(1)} %get-tuple-element.169), channel_id=1, source_target_pairs={{0,2},{1,3},{2,0},{3,1},{4,6},{5,7},{6,4},{7,5},{8,10},{9,11},{10,... | collective-permute-start | bytes 884744 | tf_op jit(solution)/shard_map/ppermute | solution.py:21
  171.1 10.7 %collective-permute-start.51 = (bf16[128,768]{1,0:T(8,128)(2,1)S(1)}, bf16[128,768]{1,0:T(8,128)(2,1)S(1)}, u32[]{:S(2)}, u32[]{:S(2)}) collective-permute-start(bf16[128,768]{1,0:T(8,128)(2,1)S(1)} %shard_map.242.refs_2_.refs_1_), channel_id=1, source_target_pairs={{0,8},{4,12},{8,0},{12,4},{1,9},{5,13},{9,1},{13,5},{2,10},{6,14},... | collective-permute-start | bytes 589832 | tf_op jit(solution)/shard_map/ppermute | solution.py:21
  187.4 11.6 %collective-permute-start.61 = (bf16[208,768]{1,0:T(8,128)(2,1)S(1)}, bf16[208,768]{1,0:T(8,128)(2,1)S(1)}, u32[]{:S(2)}, u32[]{:S(2)}) collective-permute-start(bf16[208,768]{1,0:T(8,128)(2,1)S(1)} %get-tuple-element.193), channel_id=1, source_target_pairs={{0,2},{1,3},{2,0},{3,1},{4,6},{5,7},{6,4},{7,5},{8,10},{9,11},{10,... | collective-permute-start | bytes 958472 | tf_op jit(solution)/shard_map/ppermute | solution.py:21
  188.4 23.5 %collective-permute-start.64 = (bf16[288,768]{1,0:T(8,128)(2,1)S(1)}, bf16[288,768]{1,0:T(8,128)(2,1)S(1)}, u32[]{:S(2)}, u32[]{:S(2)}) collective-permute-start(bf16[288,768]{1,0:T(8,128)(2,1)S(1)} %shard_map.253.refs_0_.refs_1_.refs_2_), channel_id=1, source_target_pairs={{0,16},{16,0},{1,17},{17,1},{2,18},{18,2},{3,19},{19,3},{4,20},{20... | collective-permute-start | bytes 1327112 | tf_op jit(solution)/shard_map/ppermute | solution.py:21
  199.1 14.4 %collective-permute-start.62 = (bf16[208,768]{1,0:T(8,128)(2,1)S(1)}, bf16[208,768]{1,0:T(8,128)(2,1)S(1)}, u32[]{:S(2)}, u32[]{:S(2)}) collective-permute-start(bf16[208,768]{1,0:T(8,128)(2,1)S(1)} %shard_map.251.refs_0_), channel_id=1, source_target_pairs={{0,16},{16,0},{1,17},{17,1},{2,18},{18,2},{3,19},{19,3},{4,20},{20... | collective-permute-start | bytes 958472 | tf_op jit(solution)/shard_map/ppermute | solution.py:21
  200.2 11.7 %collective-permute-start.65 = (bf16[96,768]{1,0:T(8,128)(2,1)S(1)}, bf16[96,768]{1,0:T(8,128)(2,1)S(1)}, u32[]{:S(2)}, u32[]{:S(2)}) collective-permute-start(bf16[96,768]{1,0:T(8,128)(2,1)S(1)} %shard_map.255.refs_3_), channel_id=1, source_target_pairs={{0,16},{16,0},{1,17},{17,1},{2,18},{18,2},{3,19},{19,3},{4,20},{20... | collective-permute-start | bytes 442376 | tf_op jit(solution)/shard_map/ppermute | solution.py:21
  201.8 9.5 %collective-permute-start.59 = (bf16[384,128]{1,0:T(8,128)(2,1)S(1)}, bf16[384,128]{1,0:T(8,128)(2,1)S(1)}, u32[]{:S(2)}, u32[]{:S(2)}) collective-permute-start(bf16[384,128]{1,0:T(8,128)(2,1)S(1)} %shard_map.247.refs_2_), channel_id=1, source_target_pairs={{0,0},{1,4},{2,8},{3,12},{4,1},{5,5},{6,9},{7,13},{8,2},{9,6},{10,... | collective-permute-start | bytes 294920 | tf_op jit(solution)/shard_map/ppermute | solution.py:27
  (50 other events, 341.8 us)

commit v6 on v5

--- a/solution.py
+++ b/solution.py
@@ -433,9 +433,16 @@
     grads_ref[...] = grads
     dx = heads_back(grads, w)
     place = sc[0] ^ sc[1]
-    pick_features(place, m, da + dx, outs[0])
-    for k in range(1, n):
-        pick_features(place ^ k, m, dx, outs[k])
+    piece = outs[0].shape[1]
+    low_dx = dx.astype(BF16)
+    for j in range(m):
+
+        @pl.when(place == j)
+        def _():
+            outs[0][...] = (da + dx)[:, j * piece : (j + 1) * piece]
+            for k in range(1, n):
+                at = (j ^ k) * piece
+                outs[k][...] = low_dx[:, at : at + piece]
 
 
 def k_total(ins, outs, scr):
@@ -521,13 +528,17 @@
         at += rows
 
 
-def k_feed_outputs(ins, outs, scr):
+def k_feed_output(ins, outs, scr):
     half = ins[0].shape[0]
     for layer in range(2):
-        for i, out in enumerate(outs):
-            for j in range(2):
-                at = 4 * layer + 2 * i + j
-                out[layer, j * half : (j + 1) * half, :] = f32(ins[at]) + f32(ins[8 + at])
+        for j in range(2):
+            total = f32(ins[2 * layer + j]) + f32(ins[4 + 2 * layer + j])
+            outs[0][layer, j * half : (j + 1) * half, :] = total
+
+
+def with_token(kernel, ins, outs, scr):
+    kernel(ins, outs[:-1], scr)
+    outs[-1][...] = jnp.zeros(outs[-1].shape, F32)
 
 
 def k_attend_outputs(ins, outs, scr):
@@ -638,7 +649,7 @@
     down0_along = along_of(down0)
     (low,) = call(k_turned, [sds((tokens, piece), BF16)], [whole(cotangent.T)], after=[z], final=True)
     cotan = turned(low)
-    z = pair_sum(z, [*down0_along, cotan])
+    z = pair_sum(z, down0_along)
     up0 = gathered([up0], [up0_along], after=[z])
     down0 = gathered(down0, down0_along, after=[z])
     attn1_along = along_of(attn1)
@@ -667,6 +678,7 @@
         partial(k_feed, m, 1),
         feed_out,
         [*both(z), unit_b0, *up1, *down1, rowwise, prm],
+        after=[cotan],
     )
     (again,) = held([cotan], [f])
     cotan = [cotan, None] + [exchange(again, "row", k) for k in range(2, n)]
@@ -789,26 +801,42 @@
 
     first = [halves_of(a) + [b] for a, b in zip(most0_terms, rest0_terms)]
     second = [[t[side] for t in terms1] for side in range(2)]
-    grad_down, grad_up = call(
-        k_feed_outputs,
-        [sds((layers, piece, hidden), F32)] * 2,
-        [*first[0], *second[0], *first[1], *second[1]],
+    def feed_terms(which):
+        return [
+            halves[2 * which + j]
+            for side in range(2)
+            for halves in (first[side], second[side])
+            for j in range(2)
+        ]
+
+    mark = sds((8, 128), F32)
+    feed_grad = sds((layers, piece, hidden), F32)
+    grad_down, down_token = call(
+        partial(with_token, k_feed_output),
+        [feed_grad, mark],
+        feed_terms(0),
         after=[token],
-        final=True,
-    )
-    grad_attn, grad_qv, grad_out, grad_gain, grad_shift, grad_b_up, grad_b_down = call(
-        k_attend_outputs,
-        [
-            sds(w_attn.shape, F32),
-            sds(b_qv.shape, F32),
-            sds(b_out.shape, F32),
-            sds(ln_gain.shape, F32),
-            sds(ln_bias.shape, F32),
-            sds(b_up.shape, F32),
-            sds(b_down.shape, F32),
-        ],
+        final=1,
+    )
+    (
+        grad_attn,
+        grad_qv,
+        grad_out,
+        grad_gain,
+        grad_shift,
+        grad_b_up,
+        grad_b_down,
+        attend_token,
+    ) = call(
+        partial(with_token, k_attend_outputs),
+        [sds(a.shape, F32) for a in (w_attn, b_qv, b_out, ln_gain, ln_bias, b_up, b_down)]
+        + [mark],
         [t[side] for terms in (attn0_terms, attn1_terms) for side in range(2) for t in terms],
-        final=True,
+        after=[down_token],
+        final=7,
+    )
+    (grad_up,) = call(
+        k_feed_output, [feed_grad], feed_terms(1), after=[attend_token], final=True
     )
     return (
         out_hidden.T,

time: 216 us -> 214 us (level)
  waiting for transfers between devices: 126 us -> 116 us
  starting transfers between devices: 61 us -> 68.8 us
    ppermute x63, waiting for transfers between devices: 111 us -> 97.1 us  [exchange(): return lax.ppermute(x, axis, [(i, i ^ bit) for i in range(n)])]
    ppermute x63, starting transfers between devices: 49.7 us -> 56.8 us  [exchange(): return lax.ppermute(x, axis, [(i, i ^ bit) for i in range(n)])]
    ppermute x3, waiting for transfers between devices: 14.4 us -> 19.1 us  [turned(): return lax.ppermute(x, ('row', 'col'), pairs)]
    pallas_call x54 -> x55, Pallas kernels: 25.6 us -> 26.1 us  [call(): pl.pallas_call(body, grid=(1,), out_shape=outs, in_specs=specs + [pl.Bloc...]
  transfers between devices with their start and end apart: 66 -> 66, of which waited for: 46 -> 41; matrix products, arithmetic and copies ran while one was open for 0% -> 0% of each run, Pallas kernels for 2% -> 3%
where the time goes in v6:
time: 214 us; the launch traced here: 213 us
  waiting for transfers between devices  116 us (54%)
  starting transfers between devices  68.8 us (32%)
  Pallas kernels  26.1 us (12%)
    ppermute x63, waiting for transfers between devices, exchange(): return lax.ppermute(x, axis, [(i, i ^ bit) for i in range(n)])  97.1 us
    ppermute x63, starting transfers between devices, exchange(): return lax.ppermute(x, axis, [(i, i ^ bit) for i in range(n)])  56.8 us
    pallas_call x55, Pallas kernels, call(): pl.pallas_call(body, grid=(1,), out_shape=outs, in_specs=specs + [pl.Bloc...  26.1 us
    ppermute x3, waiting for transfers between devices, turned(): return lax.ppermute(x, ('row', 'col'), pairs)  19.1 us
    ppermute x3, starting transfers between devices, turned(): return lax.ppermute(x, ('row', 'col'), pairs)  12 us
  transfers between devices with their start and end apart: 66, of which 41 were waited for; matrix products, arithmetic and copies ran while one was open for 0% of the time, Pallas kernels for 3%

profile of v6, /device:TPU:2, one launch (start us, length us, event | category | flops | bytes accessed | tf_op | source)
XLA Modules:
  0.0 213.4 jit_solution(12399326409942024742)
XLA Ops:
  3.2 4.5 %collective-permute-start = (bf16[128,192]{1,0:T(8,128)(2,1)}, bf16[128,192]{1,0:T(8,128)(2,1)S(1)}, u32[]{:S(2)}, u32[]{:S(2)}) collective-permute-start(bf16[128,192]{1,0:T(8,128)(2,1)} %get-tuple-element.111), channel_id=1, source_target_pairs={{0,0},{1,4},{2,8},{3,12},{4,1},{5,5},{6,9},{7,13},{8,2},{9,6},{10,... | collective-permute-start | bytes 147464 | tf_op jit(solution)/shard_map/ppermute | solution.py:27
  7.8 5.3 %collective-permute-done.refs_1_ = bf16[128,192]{1,0:T(8,128)(2,1)S(1)} collective-permute-done((bf16[128,192]{1,0:T(8,128)(2,1)}, bf16[128,192]{1,0:T(8,128)(2,1)S(1)}, u32[]{:S(2)}, u32[]{:S(2)}) %collective-permute-start) | collective-permute-done | bytes 49184 | tf_op jit(solution)/shard_map/ppermute | solution.py:27
  14.2 3.1 %collective-permute-start.3 = (bf16[128,192]{1,0:T(8,128)(2,1)S(1)}, bf16[128,192]{1,0:T(8,128)(2,1)S(1)}, u32[]{:S(2)}, u32[]{:S(2)}) collective-permute-start(bf16[128,192]{1,0:T(8,128)(2,1)S(1)} %collective-permute-done.refs_1_), channel_id=1, source_target_pairs={{0,12},{4,8},{8,4},{12,0},{1,13},{5,9},{9,5},{13,1},{2,14},{6,10},... | collective-permute-start | bytes 147464 | tf_op jit(solution)/shard_map/ppermute | solution.py:21
  22.5 3.3 %collective-permute-done.6.refs_4_.refs_1_ = bf16[192,768]{1,0:T(8,128)(2,1)S(1)} collective-permute-done((bf16[192,768]{1,0:T(8,128)(2,1)S(1)}, bf16[192,768]{1,0:T(8,128)(2,1)S(1)}, u32[]{:S(2)}, u32[]{:S(2)}) %collective-permute-start.6) | collective-permute-done | bytes 294944 | tf_op jit(solution)/shard_map/ppermute | solution.py:21
  31.3 4.7 %collective-permute-done.10.refs_3_ = bf16[96,768]{1,0:T(8,128)(2,1)S(1)} collective-permute-done((bf16[96,768]{1,0:T(8,128)(2,1)S(1)}, bf16[96,768]{1,0:T(8,128)(2,1)S(1)}, u32[]{:S(2)}, u32[]{:S(2)}) %collective-permute-start.10) | collective-permute-done | bytes 147488 | tf_op jit(solution)/shard_map/ppermute | solution.py:21
  41.4 4.7 %collective-permute-done.14.refs_13_.refs_2_ = bf16[96,768]{1,0:T(8,128)(2,1)S(1)} collective-permute-done((bf16[96,768]{1,0:T(8,128)(2,1)S(1)}, bf16[96,768]{1,0:T(8,128)(2,1)S(1)}, u32[]{:S(2)}, u32[]{:S(2)}) %collective-permute-start.14) | collective-permute-done | bytes 147488 | tf_op jit(solution)/shard_map/ppermute | solution.py:21
  48.2 2.9 %collective-permute-done.11.refs_1_ = bf16[128,768]{1,0:T(8,128)(2,1)S(1)} collective-permute-done((bf16[128,768]{1,0:T(8,128)(2,1)S(1)}, bf16[128,768]{1,0:T(8,128)(2,1)S(1)}, u32[]{:S(2)}, u32[]{:S(2)}) %collective-permute-start.11) | collective-permute-done | bytes 196640 | tf_op jit(solution)/shard_map/ppermute | solution.py:21
  52.7 5.8 %collective-permute-done.18.refs_3_.refs_2_ = bf16[96,768]{1,0:T(8,128)(2,1)S(1)} collective-permute-done((bf16[96,768]{1,0:T(8,128)(2,1)S(1)}, bf16[96,768]{1,0:T(8,128)(2,1)S(1)}, u32[]{:S(2)}, u32[]{:S(2)}) %collective-permute-start.18) | collective-permute-done | bytes 147488 | tf_op jit(solution)/shard_map/ppermute | solution.py:21
  62.2 4.6 %collective-permute-done.20.refs_10_.refs_3_ = bf16[96,768]{1,0:T(8,128)(2,1)S(1)} collective-permute-done((bf16[96,768]{1,0:T(8,128)(2,1)S(1)}, bf16[96,768]{1,0:T(8,128)(2,1)S(1)}, u32[]{:S(2)}, u32[]{:S(2)}) %collective-permute-start.20) | collective-permute-done | bytes 147488 | tf_op jit(solution)/shard_map/ppermute | solution.py:21
  68.4 2.8 %collective-permute-done.19.refs_2_ = bf16[128,768]{1,0:T(8,128)(2,1)S(1)} collective-permute-done((bf16[128,768]{1,0:T(8,128)(2,1)S(1)}, bf16[128,768]{1,0:T(8,128)(2,1)S(1)}, u32[]{:S(2)}, u32[]{:S(2)}) %collective-permute-start.19) | collective-permute-done | bytes 196640 | tf_op jit(solution)/shard_map/ppermute | solution.py:21
  73.7 5.8 %collective-permute-done.23.refs_2_.refs_3_ = bf16[96,768]{1,0:T(8,128)(2,1)S(1)} collective-permute-done((bf16[96,768]{1,0:T(8,128)(2,1)S(1)}, bf16[96,768]{1,0:T(8,128)(2,1)S(1)}, u32[]{:S(2)}, u32[]{:S(2)}) %collective-permute-start.23) | collective-permute-done | bytes 147488 | tf_op jit(solution)/shard_map/ppermute | solution.py:21
  81.4 4.0 %collective-permute-start.27 = (bf16[128,192]{1,0:T(8,128)(2,1)S(1)}, bf16[128,192]{1,0:T(8,128)(2,1)S(1)}, u32[]{:S(2)}, u32[]{:S(2)}) collective-permute-start(bf16[128,192]{1,0:T(8,128)(2,1)S(1)} %shard_map.219), channel_id=1, source_target_pairs={{0,0},{1,4},{2,8},{3,12},{4,1},{5,5},{6,9},{7,13},{8,2},{9,6},{10,... | collective-permute-start | bytes 147464 | tf_op jit(solution)/shard_map/ppermute | solution.py:27
  85.5 10.2 %collective-permute-done.27.refs_13_.refs_0_.refs_1_ = bf16[128,192]{1,0:T(8,128)(2,1)S(1)} collective-permute-done((bf16[128,192]{1,0:T(8,128)(2,1)S(1)}, bf16[128,192]{1,0:T(8,128)(2,1)S(1)}, u32[]{:S(2)}, u32[]{:S(2)}) %collective-permute-start.27) | collective-permute-done | bytes 49184 | tf_op jit(solution)/shard_map/ppermute | solution.py:27
  97.3 3.0 %collective-permute-start.29 = (bf16[128,192]{1,0:T(8,128)(2,1)S(1)}, bf16[128,192]{1,0:T(8,128)(2,1)S(1)}, u32[]{:S(2)}, u32[]{:S(2)}) collective-permute-start(bf16[128,192]{1,0:T(8,128)(2,1)S(1)} %shard_map.221.refs_0_), channel_id=1, source_target_pairs={{0,8},{4,12},{8,0},{12,4},{1,9},{5,13},{9,1},{13,5},{2,10},{6,14},... | collective-permute-start | bytes 147464 | tf_op jit(solution)/shard_map/ppermute | solution.py:21
  100.3 3.9 %collective-permute-done.30.refs_3_.refs_4_ = bf16[128,192]{1,0:T(8,128)(2,1)S(1)} collective-permute-done((bf16[128,192]{1,0:T(8,128)(2,1)S(1)}, bf16[128,192]{1,0:T(8,128)(2,1)S(1)}, u32[]{:S(2)}, u32[]{:S(2)}) %collective-permute-start.30) | collective-permute-done | bytes 49184 | tf_op jit(solution)/shard_map/ppermute | solution.py:21
  117.0 7.2 %collective-permute-done.33.refs_1_ = bf16[128,768]{1,0:T(8,128)(2,1)S(1)} collective-permute-done((bf16[128,768]{1,0:T(8,128)(2,1)S(1)}, bf16[128,768]{1,0:T(8,128)(2,1)S(1)}, u32[]{:S(2)}, u32[]{:S(2)}) %collective-permute-start.33) | collective-permute-done | bytes 196640 | tf_op jit(solution)/shard_map/ppermute | solution.py:21
  125.4 3.3 %collective-permute-start.36 = (bf16[96,768]{1,0:T(8,128)(2,1)S(1)}, bf16[96,768]{1,0:T(8,128)(2,1)S(1)}, u32[]{:S(2)}, u32[]{:S(2)}) collective-permute-start(bf16[96,768]{1,0:T(8,128)(2,1)S(1)} %get-tuple-element.141), channel_id=1, source_target_pairs={{0,2},{1,3},{2,0},{3,1},{4,6},{5,7},{6,4},{7,5},{8,10},{9,11},{10,... | collective-permute-start | bytes 442376 | tf_op jit(solution)/shard_map/ppermute | solution.py:21
  128.7 4.6 %collective-permute-done.36.refs_11_.refs_1_ = bf16[96,768]{1,0:T(8,128)(2,1)S(1)} collective-permute-done((bf16[96,768]{1,0:T(8,128)(2,1)S(1)}, bf16[96,768]{1,0:T(8,128)(2,1)S(1)}, u32[]{:S(2)}, u32[]{:S(2)}) %collective-permute-start.36) | collective-permute-done | bytes 147488 | tf_op jit(solution)/shard_map/ppermute | solution.py:21
  147.3 2.8 %collective-permute-start.42 = (bf16[128,768]{1,0:T(8,128)(2,1)S(1)}, bf16[128,768]{1,0:T(8,128)(2,1)S(1)}, u32[]{:S(2)}, u32[]{:S(2)}) collective-permute-start(bf16[128,768]{1,0:T(8,128)(2,1)S(1)} %shard_map.233.refs_1_.refs_2_.refs_0_), channel_id=1, source_target_pairs={{0,8},{4,12},{8,0},{12,4},{1,9},{5,13},{9,1},{13,5},{2,10},{6,14},... | collective-permute-start | bytes 589832 | tf_op jit(solution)/shard_map/ppermute | solution.py:21
  165.4 2.8 %collective-permute-done.49.refs_3_.refs_1_ = bf16[96,768]{1,0:T(8,128)(2,1)S(1)} collective-permute-done((bf16[96,768]{1,0:T(8,128)(2,1)S(1)}, bf16[96,768]{1,0:T(8,128)(2,1)S(1)}, u32[]{:S(2)}, u32[]{:S(2)}) %collective-permute-start.49) | collective-permute-done | bytes 147488 | tf_op jit(solution)/shard_map/ppermute | solution.py:21
  175.6 5.4 %collective-permute-done.53.refs_13_.refs_4_ = bf16[96,768]{1,0:T(8,128)(2,1)S(1)} collective-permute-done((bf16[96,768]{1,0:T(8,128)(2,1)S(1)}, bf16[96,768]{1,0:T(8,128)(2,1)S(1)}, u32[]{:S(2)}, u32[]{:S(2)}) %collective-permute-start.53) | collective-permute-done | bytes 147488 | tf_op jit(solution)/shard_map/ppermute | solution.py:21
  194.5 3.5 %collective-permute-done.57.refs_2_ = bf16[128,192]{1,0:T(8,128)(2,1)S(1)} collective-permute-done((bf16[128,192]{1,0:T(8,128)(2,1)S(1)}, bf16[128,192]{1,0:T(8,128)(2,1)S(1)}, u32[]{:S(2)}, u32[]{:S(2)}) %collective-permute-start.57) | collective-permute-done | bytes 49184 | tf_op jit(solution)/shard_map/ppermute | solution.py:21
  200.3 3.5 %collective-permute-start.59 = (bf16[384,128]{1,0:T(8,128)(2,1)S(1)}, bf16[384,128]{1,0:T(8,128)(2,1)S(1)}, u32[]{:S(2)}, u32[]{:S(2)}) collective-permute-start(bf16[384,128]{1,0:T(8,128)(2,1)S(1)} %shard_map.247.refs_2_), channel_id=1, source_target_pairs={{0,0},{1,4},{2,8},{3,12},{4,1},{5,5},{6,9},{7,13},{8,2},{9,6},{10,... | collective-permute-start | bytes 294920 | tf_op jit(solution)/shard_map/ppermute | solution.py:27
  205.7 3.6 %collective-permute-done.59.refs_0_ = bf16[384,128]{1,0:T(8,128)(2,1)S(1)} collective-permute-done((bf16[384,128]{1,0:T(8,128)(2,1)S(1)}, bf16[384,128]{1,0:T(8,128)(2,1)S(1)}, u32[]{:S(2)}, u32[]{:S(2)}) %collective-permute-start.59) | collective-permute-done | bytes 98336 | tf_op jit(solution)/shard_map/ppermute | solution.py:27
  (179 shorter events, 106.9 us)
Async XLA Ops:
  3.2 9.9 %collective-permute-start = (bf16[128,192]{1,0:T(8,128)(2,1)}, bf16[128,192]{1,0:T(8,128)(2,1)S(1)}, u32[]{:S(2)}, u32[]{:S(2)}) collective-permute-start(bf16[128,192]{1,0:T(8,128)(2,1)} %get-tuple-element.111), channel_id=1, source_target_pairs={{0,0},{1,4},{2,8},{3,12},{4,1},{5,5},{6,9},{7,13},{8,2},{9,6},{10,... | collective-permute-start | bytes 147464 | tf_op jit(solution)/shard_map/ppermute | solution.py:27
  7.7 14.8 %collective-permute-start.5 = (bf16[208,768]{1,0:T(8,128)(2,1)}, bf16[208,768]{1,0:T(8,128)(2,1)S(1)}, u32[]{:S(2)}, u32[]{:S(2)}) collective-permute-start(bf16[208,768]{1,0:T(8,128)(2,1)} %get-tuple-element.112.refs_2_.refs_5_), channel_id=1, source_target_pairs={{0,2},{1,3},{2,0},{3,1},{4,6},{5,7},{6,4},{7,5},{8,10},{9,11},{10,... | collective-permute-start | bytes 958472 | tf_op jit(solution)/shard_map/ppermute | solution.py:21
  14.1 11.6 %collective-permute-start.6 = (bf16[192,768]{1,0:T(8,128)(2,1)S(1)}, bf16[192,768]{1,0:T(8,128)(2,1)S(1)}, u32[]{:S(2)}, u32[]{:S(2)}) collective-permute-start(bf16[192,768]{1,0:T(8,128)(2,1)S(1)} %shard_map.205.refs_0_), channel_id=1, source_target_pairs={{0,2},{1,3},{2,0},{3,1},{4,6},{5,7},{6,4},{7,5},{8,10},{9,11},{10,... | collective-permute-start | bytes 884744 | tf_op jit(solution)/shard_map/ppermute | solution.py:21
  29.2 9.2 %collective-permute-start.8 = (bf16[128,768]{1,0:T(8,128)(2,1)S(1)}, bf16[128,768]{1,0:T(8,128)(2,1)S(1)}, u32[]{:S(2)}, u32[]{:S(2)}) collective-permute-start(bf16[128,768]{1,0:T(8,128)(2,1)S(1)} %get-tuple-element.115.refs_0_.refs_1_), channel_id=1, source_target_pairs={{0,4},{4,0},{8,12},{12,8},{1,5},{5,1},{9,13},{13,9},{2,6},{6,2},{1... | collective-permute-start | bytes 589832 | tf_op jit(solution)/shard_map/ppermute | solution.py:21
  29.3 9.0 %collective-permute-start.9 = (bf16[96,768]{1,0:T(8,128)(2,1)S(1)}, bf16[96,768]{1,0:T(8,128)(2,1)S(1)}, u32[]{:S(2)}, u32[]{:S(2)}) collective-permute-start(bf16[96,768]{1,0:T(8,128)(2,1)S(1)} %get-tuple-element.114.refs_7_.refs_0_), channel_id=1, source_target_pairs={{0,2},{1,3},{2,0},{3,1},{4,6},{5,7},{6,4},{7,5},{8,10},{9,11},{10,... | collective-permute-start | bytes 442376 | tf_op jit(solution)/shard_map/ppermute | solution.py:21
  38.5 12.7 %collective-permute-start.12 = (bf16[384,768]{1,0:T(8,128)(2,1)S(1)}, bf16[384,768]{1,0:T(8,128)(2,1)S(1)}, u32[]{:S(2)}, u32[]{:S(2)}) collective-permute-start(bf16[384,768]{1,0:T(8,128)(2,1)S(1)} %shard_map.210.refs_3_.refs_5_.refs_4_.refs_6_), channel_id=1, source_target_pairs={{0,1},{1,0},{2,3},{3,2},{4,5},{5,4},{6,7},{7,6},{8,9},{9,8},{10,11... | collective-permute-start | bytes 1769480 | tf_op jit(solution)/shard_map/ppermute | solution.py:21
  38.6 12.6 %collective-permute-start.13 = (bf16[384,768]{1,0:T(8,128)(2,1)S(1)}, bf16[384,768]{1,0:T(8,128)(2,1)S(1)}, u32[]{:S(2)}, u32[]{:S(2)}) collective-permute-start(bf16[384,768]{1,0:T(8,128)(2,1)S(1)} %shard_map.211.refs_7_.refs_9_.refs_8_.refs_10_), channel_id=1, source_target_pairs={{0,1},{1,0},{2,3},{3,2},{4,5},{5,4},{6,7},{7,6},{8,9},{9,8},{10,11... | collective-permute-start | bytes 1769480 | tf_op jit(solution)/shard_map/ppermute | solution.py:21
  39.2 12.0 %collective-permute-start.11 = (bf16[128,768]{1,0:T(8,128)(2,1)S(1)}, bf16[128,768]{1,0:T(8,128)(2,1)S(1)}, u32[]{:S(2)}, u32[]{:S(2)}) collective-permute-start(bf16[128,768]{1,0:T(8,128)(2,1)S(1)} %shard_map.209.refs_2_.refs_4_.refs_0_), channel_id=1, source_target_pairs={{0,8},{4,12},{8,0},{12,4},{1,9},{5,13},{9,1},{13,5},{2,10},{6,14},... | collective-permute-start | bytes 589832 | tf_op jit(solution)/shard_map/ppermute | solution.py:21
  59.7 11.5 %collective-permute-start.19 = (bf16[128,768]{1,0:T(8,128)(2,1)S(1)}, bf16[128,768]{1,0:T(8,128)(2,1)S(1)}, u32[]{:S(2)}, u32[]{:S(2)}) collective-permute-start(bf16[128,768]{1,0:T(8,128)(2,1)S(1)} %shard_map.214.refs_1_), channel_id=1, source_target_pairs={{0,8},{4,12},{8,0},{12,4},{1,9},{5,13},{9,1},{13,5},{2,10},{6,14},... | collective-permute-start | bytes 589832 | tf_op jit(solution)/shard_map/ppermute | solution.py:21
  80.7 15.0 %collective-permute-start.26 = (bf16[384,768]{1,0:T(8,128)(2,1)S(1)}, bf16[384,768]{1,0:T(8,128)(2,1)S(1)}, u32[]{:S(2)}, u32[]{:S(2)}) collective-permute-start(bf16[384,768]{1,0:T(8,128)(2,1)S(1)} %shard_map.218.refs_7_.refs_9_.refs_11_), channel_id=1, source_target_pairs={{0,1},{1,0},{2,3},{3,2},{4,5},{5,4},{6,7},{7,6},{8,9},{9,8},{10,11... | collective-permute-start | bytes 1769480 | tf_op jit(solution)/shard_map/ppermute | solution.py:21
  80.7 15.0 %collective-permute-start.25 = (bf16[128,768]{1,0:T(8,128)(2,1)S(1)}, bf16[128,768]{1,0:T(8,128)(2,1)S(1)}, u32[]{:S(2)}, u32[]{:S(2)}) collective-permute-start(bf16[128,768]{1,0:T(8,128)(2,1)S(1)} %shard_map.217.refs_4_.refs_0_), channel_id=1, source_target_pairs={{0,8},{4,12},{8,0},{12,4},{1,9},{5,13},{9,1},{13,5},{2,10},{6,14},... | collective-permute-start | bytes 589832 | tf_op jit(solution)/shard_map/ppermute | solution.py:21
  81.4 14.3 %collective-permute-start.27 = (bf16[128,192]{1,0:T(8,128)(2,1)S(1)}, bf16[128,192]{1,0:T(8,128)(2,1)S(1)}, u32[]{:S(2)}, u32[]{:S(2)}) collective-permute-start(bf16[128,192]{1,0:T(8,128)(2,1)S(1)} %shard_map.219), channel_id=1, source_target_pairs={{0,0},{1,4},{2,8},{3,12},{4,1},{5,5},{6,9},{7,13},{8,2},{9,6},{10,... | collective-permute-start | bytes 147464 | tf_op jit(solution)/shard_map/ppermute | solution.py:27
  96.7 8.8 %collective-permute-start.28 = (bf16[128,768]{1,0:T(8,128)(2,1)S(1)}, bf16[128,768]{1,0:T(8,128)(2,1)S(1)}, u32[]{:S(2)}, u32[]{:S(2)}) collective-permute-start(bf16[128,768]{1,0:T(8,128)(2,1)S(1)} %get-tuple-element.128.refs_1_.refs_0_), channel_id=1, source_target_pairs={{0,4},{4,0},{8,12},{12,8},{1,5},{5,1},{9,13},{13,9},{2,6},{6,2},{1... | collective-permute-start | bytes 589832 | tf_op jit(solution)/shard_map/ppermute | solution.py:21
  124.3 11.5 %collective-permute-start.35 = (bf16[128,768]{1,0:T(8,128)(2,1)S(1)}, bf16[128,768]{1,0:T(8,128)(2,1)S(1)}, u32[]{:S(2)}, u32[]{:S(2)}) collective-permute-start(bf16[128,768]{1,0:T(8,128)(2,1)S(1)} %shard_map.227.refs_2_.refs_0_), channel_id=1, source_target_pairs={{0,8},{4,12},{8,0},{12,4},{1,9},{5,13},{9,1},{13,5},{2,10},{6,14},... | collective-permute-start | bytes 589832 | tf_op jit(solution)/shard_map/ppermute | solution.py:21
  138.3 8.9 %collective-permute-start.39 = (bf16[384,768]{1,0:T(8,128)(2,1)S(1)}, bf16[384,768]{1,0:T(8,128)(2,1)S(1)}, u32[]{:S(2)}, u32[]{:S(2)}) collective-permute-start(bf16[384,768]{1,0:T(8,128)(2,1)S(1)} %get-tuple-element.148), channel_id=1, source_target_pairs={{0,1},{1,0},{2,3},{3,2},{4,5},{5,4},{6,7},{7,6},{8,9},{9,8},{10,11... | collective-permute-start | bytes 1769480 | tf_op jit(solution)/shard_map/ppermute | solution.py:21
  138.4 8.9 %collective-permute-start.38 = (bf16[128,768]{1,0:T(8,128)(2,1)S(1)}, bf16[128,768]{1,0:T(8,128)(2,1)S(1)}, u32[]{:S(2)}, u32[]{:S(2)}) collective-permute-start(bf16[128,768]{1,0:T(8,128)(2,1)S(1)} %get-tuple-element.143.refs_1_.refs_2_.refs_0_), channel_id=1, source_target_pairs={{0,4},{4,0},{8,12},{12,8},{1,5},{5,1},{9,13},{13,9},{2,6},{6,2},{1... | collective-permute-start | bytes 589832 | tf_op jit(solution)/shard_map/ppermute | solution.py:21
  147.3 12.3 %collective-permute-start.42 = (bf16[128,768]{1,0:T(8,128)(2,1)S(1)}, bf16[128,768]{1,0:T(8,128)(2,1)S(1)}, u32[]{:S(2)}, u32[]{:S(2)}) collective-permute-start(bf16[128,768]{1,0:T(8,128)(2,1)S(1)} %shard_map.233.refs_1_.refs_2_.refs_0_), channel_id=1, source_target_pairs={{0,8},{4,12},{8,0},{12,4},{1,9},{5,13},{9,1},{13,5},{2,10},{6,14},... | collective-permute-start | bytes 589832 | tf_op jit(solution)/shard_map/ppermute | solution.py:21
  169.8 11.3 %collective-permute-start.52 = (bf16[192,768]{1,0:T(8,128)(2,1)S(1)}, bf16[192,768]{1,0:T(8,128)(2,1)S(1)}, u32[]{:S(2)}, u32[]{:S(2)}) collective-permute-start(bf16[192,768]{1,0:T(8,128)(2,1)S(1)} %get-tuple-element.170), channel_id=1, source_target_pairs={{0,2},{1,3},{2,0},{3,1},{4,6},{5,7},{6,4},{7,5},{8,10},{9,11},{10,... | collective-permute-start | bytes 884744 | tf_op jit(solution)/shard_map/ppermute | solution.py:21
  170.4 10.7 %collective-permute-start.51 = (bf16[128,768]{1,0:T(8,128)(2,1)S(1)}, bf16[128,768]{1,0:T(8,128)(2,1)S(1)}, u32[]{:S(2)}, u32[]{:S(2)}) collective-permute-start(bf16[128,768]{1,0:T(8,128)(2,1)S(1)} %shard_map.242.refs_2_.refs_1_), channel_id=1, source_target_pairs={{0,8},{4,12},{8,0},{12,4},{1,9},{5,13},{9,1},{13,5},{2,10},{6,14},... | collective-permute-start | bytes 589832 | tf_op jit(solution)/shard_map/ppermute | solution.py:21
  171.8 9.1 %collective-permute-start.53 = (bf16[96,768]{1,0:T(8,128)(2,1)S(1)}, bf16[96,768]{1,0:T(8,128)(2,1)S(1)}, u32[]{:S(2)}, u32[]{:S(2)}) collective-permute-start(bf16[96,768]{1,0:T(8,128)(2,1)S(1)} %get-tuple-element.171), channel_id=1, source_target_pairs={{0,2},{1,3},{2,0},{3,1},{4,6},{5,7},{6,4},{7,5},{8,10},{9,11},{10,... | collective-permute-start | bytes 442376 | tf_op jit(solution)/shard_map/ppermute | solution.py:21
  186.6 11.6 %collective-permute-start.61 = (bf16[208,768]{1,0:T(8,128)(2,1)S(1)}, bf16[208,768]{1,0:T(8,128)(2,1)S(1)}, u32[]{:S(2)}, u32[]{:S(2)}) collective-permute-start(bf16[208,768]{1,0:T(8,128)(2,1)S(1)} %get-tuple-element.194), channel_id=1, source_target_pairs={{0,2},{1,3},{2,0},{3,1},{4,6},{5,7},{6,4},{7,5},{8,10},{9,11},{10,... | collective-permute-start | bytes 958472 | tf_op jit(solution)/shard_map/ppermute | solution.py:21
  188.2 21.7 %collective-permute-start.63 = (bf16[288,768]{1,0:T(8,128)(2,1)S(1)}, bf16[288,768]{1,0:T(8,128)(2,1)S(1)}, u32[]{:S(2)}, u32[]{:S(2)}) collective-permute-start(bf16[288,768]{1,0:T(8,128)(2,1)S(1)} %shard_map.252.refs_0_.refs_1_), channel_id=1, source_target_pairs={{0,16},{16,0},{1,17},{17,1},{2,18},{18,2},{3,19},{19,3},{4,20},{20... | collective-permute-start | bytes 1327112 | tf_op jit(solution)/shard_map/ppermute | solution.py:21
  198.3 12.9 %collective-permute-start.62 = (bf16[208,768]{1,0:T(8,128)(2,1)S(1)}, bf16[208,768]{1,0:T(8,128)(2,1)S(1)}, u32[]{:S(2)}, u32[]{:S(2)}) collective-permute-start(bf16[208,768]{1,0:T(8,128)(2,1)S(1)} %shard_map.251.refs_0_), channel_id=1, source_target_pairs={{0,16},{16,0},{1,17},{17,1},{2,18},{18,2},{3,19},{19,3},{4,20},{20... | collective-permute-start | bytes 958472 | tf_op jit(solution)/shard_map/ppermute | solution.py:21
  200.3 9.0 %collective-permute-start.59 = (bf16[384,128]{1,0:T(8,128)(2,1)S(1)}, bf16[384,128]{1,0:T(8,128)(2,1)S(1)}, u32[]{:S(2)}, u32[]{:S(2)}) collective-permute-start(bf16[384,128]{1,0:T(8,128)(2,1)S(1)} %shard_map.247.refs_2_), channel_id=1, source_target_pairs={{0,0},{1,4},{2,8},{3,12},{4,1},{5,5},{6,9},{7,13},{8,2},{9,6},{10,... | collective-permute-start | bytes 294920 | tf_op jit(solution)/shard_map/ppermute | solution.py:27
  (50 other events, 344.1 us)

commit v7 on v6

--- a/solution.py
+++ b/solution.py
@@ -650,8 +650,15 @@
     (low,) = call(k_turned, [sds((tokens, piece), BF16)], [whole(cotangent.T)], after=[z], final=True)
     cotan = turned(low)
     z = pair_sum(z, down0_along)
-    up0 = gathered([up0], [up0_along], after=[z])
-    down0 = gathered(down0, down0_along, after=[z])
+    together = pack(4 * piece, [whole(a) for a in [up0, *down0, up0_along, *down0_along]], [z])
+    near = exchange(together, "col", 1)
+    up0, down0 = [
+        [
+            (a, (piece, hidden), (i, 0))
+            for a, i in ((together, k), (near, k), (together, 2 + k), (near, 2 + k))
+        ]
+        for k in range(2)
+    ]
     attn1_along = along_of(attn1)
     f, unit_a0, h0, g0, slope0 = call(
         partial(k_feed, m, 0),

time: 214 us -> 214 us (level)
    ppermute x63 -> x62, starting transfers between devices: 56.8 us -> 56.4 us  [exchange(): return lax.ppermute(x, axis, [(i, i ^ bit) for i in range(n)])]
    ppermute x63 -> x62, waiting for transfers between devices: 97.1 us -> 97.4 us  [exchange(): return lax.ppermute(x, axis, [(i, i ^ bit) for i in range(n)])]
    pallas_call x55 -> x54, Pallas kernels: 26.1 us -> 26.1 us  [call(): pl.pallas_call(body, grid=(1,), out_shape=outs, in_specs=specs + [pl.Bloc...]
  transfers between devices with their start and end apart: 66 -> 65, of which waited for: 41 -> 41; matrix products, arithmetic and copies ran while one was open for 0% -> 0% of each run, Pallas kernels for 3% -> 3%
where the time goes in v7:
time: 214 us; the launch traced here: 213 us
  waiting for transfers between devices  117 us (55%)
  starting transfers between devices  68.4 us (32%)
  Pallas kernels  26.1 us (12%)
    ppermute x62, waiting for transfers between devices, exchange(): return lax.ppermute(x, axis, [(i, i ^ bit) for i in range(n)])  97.4 us
    ppermute x62, starting transfers between devices, exchange(): return lax.ppermute(x, axis, [(i, i ^ bit) for i in range(n)])  56.4 us
    pallas_call x54, Pallas kernels, call(): pl.pallas_call(body, grid=(1,), out_shape=outs, in_specs=specs + [pl.Bloc...  26.1 us
    ppermute x3, waiting for transfers between devices, turned(): return lax.ppermute(x, ('row', 'col'), pairs)  19.1 us
    ppermute x3, starting transfers between devices, turned(): return lax.ppermute(x, ('row', 'col'), pairs)  12 us
  transfers between devices with their start and end apart: 65, of which 41 were waited for; matrix products, arithmetic and copies ran while one was open for 0% of the time, Pallas kernels for 3%

profile of v7, /device:TPU:2, one launch (start us, length us, event | category | flops | bytes accessed | tf_op | source)
XLA Modules:
  0.0 213.2 jit_solution(2653791588899560207)
XLA Ops:
  3.2 4.5 %collective-permute-start = (bf16[128,192]{1,0:T(8,128)(2,1)}, bf16[128,192]{1,0:T(8,128)(2,1)S(1)}, u32[]{:S(2)}, u32[]{:S(2)}) collective-permute-start(bf16[128,192]{1,0:T(8,128)(2,1)} %get-tuple-element.111), channel_id=1, source_target_pairs={{0,0},{1,4},{2,8},{3,12},{4,1},{5,5},{6,9},{7,13},{8,2},{9,6},{10,... | collective-permute-start | bytes 147464 | tf_op jit(solution)/shard_map/ppermute | solution.py:27
  7.8 5.3 %collective-permute-done.refs_1_ = bf16[128,192]{1,0:T(8,128)(2,1)S(1)} collective-permute-done((bf16[128,192]{1,0:T(8,128)(2,1)}, bf16[128,192]{1,0:T(8,128)(2,1)S(1)}, u32[]{:S(2)}, u32[]{:S(2)}) %collective-permute-start) | collective-permute-done | bytes 49184 | tf_op jit(solution)/shard_map/ppermute | solution.py:27
  14.2 3.1 %collective-permute-start.3 = (bf16[128,192]{1,0:T(8,128)(2,1)S(1)}, bf16[128,192]{1,0:T(8,128)(2,1)S(1)}, u32[]{:S(2)}, u32[]{:S(2)}) collective-permute-start(bf16[128,192]{1,0:T(8,128)(2,1)S(1)} %collective-permute-done.refs_1_), channel_id=1, source_target_pairs={{0,12},{4,8},{8,4},{12,0},{1,13},{5,9},{9,5},{13,1},{2,14},{6,10},... | collective-permute-start | bytes 147464 | tf_op jit(solution)/shard_map/ppermute | solution.py:21
  22.5 3.3 %collective-permute-done.6.refs_4_.refs_3_ = bf16[192,768]{1,0:T(8,128)(2,1)S(1)} collective-permute-done((bf16[192,768]{1,0:T(8,128)(2,1)S(1)}, bf16[192,768]{1,0:T(8,128)(2,1)S(1)}, u32[]{:S(2)}, u32[]{:S(2)}) %collective-permute-start.6) | collective-permute-done | bytes 294944 | tf_op jit(solution)/shard_map/ppermute | solution.py:21
  31.3 4.7 %collective-permute-done.10.refs_3_.refs_5_ = bf16[96,768]{1,0:T(8,128)(2,1)S(1)} collective-permute-done((bf16[96,768]{1,0:T(8,128)(2,1)S(1)}, bf16[96,768]{1,0:T(8,128)(2,1)S(1)}, u32[]{:S(2)}, u32[]{:S(2)}) %collective-permute-start.10) | collective-permute-done | bytes 147488 | tf_op jit(solution)/shard_map/ppermute | solution.py:21
  40.9 4.7 %collective-permute-done.13.refs_13_.refs_2_ = bf16[96,768]{1,0:T(8,128)(2,1)S(1)} collective-permute-done((bf16[96,768]{1,0:T(8,128)(2,1)S(1)}, bf16[96,768]{1,0:T(8,128)(2,1)S(1)}, u32[]{:S(2)}, u32[]{:S(2)}) %collective-permute-start.13) | collective-permute-done | bytes 147488 | tf_op jit(solution)/shard_map/ppermute | solution.py:21
  48.0 3.0 %collective-permute-done.11.refs_1_ = bf16[128,768]{1,0:T(8,128)(2,1)S(1)} collective-permute-done((bf16[128,768]{1,0:T(8,128)(2,1)S(1)}, bf16[128,768]{1,0:T(8,128)(2,1)S(1)}, u32[]{:S(2)}, u32[]{:S(2)}) %collective-permute-start.11) | collective-permute-done | bytes 196640 | tf_op jit(solution)/shard_map/ppermute | solution.py:21
  52.6 5.8 %collective-permute-done.17.refs_3_.refs_2_ = bf16[96,768]{1,0:T(8,128)(2,1)S(1)} collective-permute-done((bf16[96,768]{1,0:T(8,128)(2,1)S(1)}, bf16[96,768]{1,0:T(8,128)(2,1)S(1)}, u32[]{:S(2)}, u32[]{:S(2)}) %collective-permute-start.17) | collective-permute-done | bytes 147488 | tf_op jit(solution)/shard_map/ppermute | solution.py:21
  62.0 4.6 %collective-permute-done.19.refs_10_.refs_3_ = bf16[96,768]{1,0:T(8,128)(2,1)S(1)} collective-permute-done((bf16[96,768]{1,0:T(8,128)(2,1)S(1)}, bf16[96,768]{1,0:T(8,128)(2,1)S(1)}, u32[]{:S(2)}, u32[]{:S(2)}) %collective-permute-start.19) | collective-permute-done | bytes 147488 | tf_op jit(solution)/shard_map/ppermute | solution.py:21
  68.2 2.8 %collective-permute-done.18.refs_2_ = bf16[128,768]{1,0:T(8,128)(2,1)S(1)} collective-permute-done((bf16[128,768]{1,0:T(8,128)(2,1)S(1)}, bf16[128,768]{1,0:T(8,128)(2,1)S(1)}, u32[]{:S(2)}, u32[]{:S(2)}) %collective-permute-start.18) | collective-permute-done | bytes 196640 | tf_op jit(solution)/shard_map/ppermute | solution.py:21
  73.6 5.8 %collective-permute-done.22.refs_2_.refs_3_ = bf16[96,768]{1,0:T(8,128)(2,1)S(1)} collective-permute-done((bf16[96,768]{1,0:T(8,128)(2,1)S(1)}, bf16[96,768]{1,0:T(8,128)(2,1)S(1)}, u32[]{:S(2)}, u32[]{:S(2)}) %collective-permute-start.22) | collective-permute-done | bytes 147488 | tf_op jit(solution)/shard_map/ppermute | solution.py:21
  81.3 4.1 %collective-permute-start.26 = (bf16[128,192]{1,0:T(8,128)(2,1)S(1)}, bf16[128,192]{1,0:T(8,128)(2,1)S(1)}, u32[]{:S(2)}, u32[]{:S(2)}) collective-permute-start(bf16[128,192]{1,0:T(8,128)(2,1)S(1)} %shard_map.218), channel_id=1, source_target_pairs={{0,0},{1,4},{2,8},{3,12},{4,1},{5,5},{6,9},{7,13},{8,2},{9,6},{10,... | collective-permute-start | bytes 147464 | tf_op jit(solution)/shard_map/ppermute | solution.py:27
  85.3 10.2 %collective-permute-done.26.refs_13_.refs_0_.refs_1_ = bf16[128,192]{1,0:T(8,128)(2,1)S(1)} collective-permute-done((bf16[128,192]{1,0:T(8,128)(2,1)S(1)}, bf16[128,192]{1,0:T(8,128)(2,1)S(1)}, u32[]{:S(2)}, u32[]{:S(2)}) %collective-permute-start.26) | collective-permute-done | bytes 49184 | tf_op jit(solution)/shard_map/ppermute | solution.py:27
  97.1 3.0 %collective-permute-start.28 = (bf16[128,192]{1,0:T(8,128)(2,1)S(1)}, bf16[128,192]{1,0:T(8,128)(2,1)S(1)}, u32[]{:S(2)}, u32[]{:S(2)}) collective-permute-start(bf16[128,192]{1,0:T(8,128)(2,1)S(1)} %shard_map.220.refs_0_), channel_id=1, source_target_pairs={{0,8},{4,12},{8,0},{12,4},{1,9},{5,13},{9,1},{13,5},{2,10},{6,14},... | collective-permute-start | bytes 147464 | tf_op jit(solution)/shard_map/ppermute | solution.py:21
  100.2 3.9 %collective-permute-done.29.refs_3_.refs_4_ = bf16[128,192]{1,0:T(8,128)(2,1)S(1)} collective-permute-done((bf16[128,192]{1,0:T(8,128)(2,1)S(1)}, bf16[128,192]{1,0:T(8,128)(2,1)S(1)}, u32[]{:S(2)}, u32[]{:S(2)}) %collective-permute-start.29) | collective-permute-done | bytes 49184 | tf_op jit(solution)/shard_map/ppermute | solution.py:21
  116.8 7.2 %collective-permute-done.32.refs_1_ = bf16[128,768]{1,0:T(8,128)(2,1)S(1)} collective-permute-done((bf16[128,768]{1,0:T(8,128)(2,1)S(1)}, bf16[128,768]{1,0:T(8,128)(2,1)S(1)}, u32[]{:S(2)}, u32[]{:S(2)}) %collective-permute-start.32) | collective-permute-done | bytes 196640 | tf_op jit(solution)/shard_map/ppermute | solution.py:21
  125.2 3.3 %collective-permute-start.35 = (bf16[96,768]{1,0:T(8,128)(2,1)S(1)}, bf16[96,768]{1,0:T(8,128)(2,1)S(1)}, u32[]{:S(2)}, u32[]{:S(2)}) collective-permute-start(bf16[96,768]{1,0:T(8,128)(2,1)S(1)} %get-tuple-element.141), channel_id=1, source_target_pairs={{0,2},{1,3},{2,0},{3,1},{4,6},{5,7},{6,4},{7,5},{8,10},{9,11},{10,... | collective-permute-start | bytes 442376 | tf_op jit(solution)/shard_map/ppermute | solution.py:21
  128.6 4.6 %collective-permute-done.35.refs_11_.refs_1_ = bf16[96,768]{1,0:T(8,128)(2,1)S(1)} collective-permute-done((bf16[96,768]{1,0:T(8,128)(2,1)S(1)}, bf16[96,768]{1,0:T(8,128)(2,1)S(1)}, u32[]{:S(2)}, u32[]{:S(2)}) %collective-permute-start.35) | collective-permute-done | bytes 147488 | tf_op jit(solution)/shard_map/ppermute | solution.py:21
  147.2 2.7 %collective-permute-start.41 = (bf16[128,768]{1,0:T(8,128)(2,1)S(1)}, bf16[128,768]{1,0:T(8,128)(2,1)S(1)}, u32[]{:S(2)}, u32[]{:S(2)}) collective-permute-start(bf16[128,768]{1,0:T(8,128)(2,1)S(1)} %shard_map.232.refs_1_.refs_2_.refs_0_), channel_id=1, source_target_pairs={{0,8},{4,12},{8,0},{12,4},{1,9},{5,13},{9,1},{13,5},{2,10},{6,14},... | collective-permute-start | bytes 589832 | tf_op jit(solution)/shard_map/ppermute | solution.py:21
  165.2 2.8 %collective-permute-done.48.refs_3_.refs_1_ = bf16[96,768]{1,0:T(8,128)(2,1)S(1)} collective-permute-done((bf16[96,768]{1,0:T(8,128)(2,1)S(1)}, bf16[96,768]{1,0:T(8,128)(2,1)S(1)}, u32[]{:S(2)}, u32[]{:S(2)}) %collective-permute-start.48) | collective-permute-done | bytes 147488 | tf_op jit(solution)/shard_map/ppermute | solution.py:21
  175.4 5.4 %collective-permute-done.52.refs_13_.refs_4_ = bf16[96,768]{1,0:T(8,128)(2,1)S(1)} collective-permute-done((bf16[96,768]{1,0:T(8,128)(2,1)S(1)}, bf16[96,768]{1,0:T(8,128)(2,1)S(1)}, u32[]{:S(2)}, u32[]{:S(2)}) %collective-permute-start.52) | collective-permute-done | bytes 147488 | tf_op jit(solution)/shard_map/ppermute | solution.py:21
  194.4 3.5 %collective-permute-done.56.refs_2_ = bf16[128,192]{1,0:T(8,128)(2,1)S(1)} collective-permute-done((bf16[128,192]{1,0:T(8,128)(2,1)S(1)}, bf16[128,192]{1,0:T(8,128)(2,1)S(1)}, u32[]{:S(2)}, u32[]{:S(2)}) %collective-permute-start.56) | collective-permute-done | bytes 49184 | tf_op jit(solution)/shard_map/ppermute | solution.py:21
  200.2 3.4 %collective-permute-start.58 = (bf16[384,128]{1,0:T(8,128)(2,1)S(1)}, bf16[384,128]{1,0:T(8,128)(2,1)S(1)}, u32[]{:S(2)}, u32[]{:S(2)}) collective-permute-start(bf16[384,128]{1,0:T(8,128)(2,1)S(1)} %shard_map.246.refs_2_), channel_id=1, source_target_pairs={{0,0},{1,4},{2,8},{3,12},{4,1},{5,5},{6,9},{7,13},{8,2},{9,6},{10,... | collective-permute-start | bytes 294920 | tf_op jit(solution)/shard_map/ppermute | solution.py:27
  205.5 3.6 %collective-permute-done.58.refs_0_ = bf16[384,128]{1,0:T(8,128)(2,1)S(1)} collective-permute-done((bf16[384,128]{1,0:T(8,128)(2,1)S(1)}, bf16[384,128]{1,0:T(8,128)(2,1)S(1)}, u32[]{:S(2)}, u32[]{:S(2)}) %collective-permute-start.58) | collective-permute-done | bytes 98336 | tf_op jit(solution)/shard_map/ppermute | solution.py:27
  (176 shorter events, 106.6 us)
Async XLA Ops:
  3.2 9.9 %collective-permute-start = (bf16[128,192]{1,0:T(8,128)(2,1)}, bf16[128,192]{1,0:T(8,128)(2,1)S(1)}, u32[]{:S(2)}, u32[]{:S(2)}) collective-permute-start(bf16[128,192]{1,0:T(8,128)(2,1)} %get-tuple-element.111), channel_id=1, source_target_pairs={{0,0},{1,4},{2,8},{3,12},{4,1},{5,5},{6,9},{7,13},{8,2},{9,6},{10,... | collective-permute-start | bytes 147464 | tf_op jit(solution)/shard_map/ppermute | solution.py:27
  7.7 14.8 %collective-permute-start.5 = (bf16[208,768]{1,0:T(8,128)(2,1)}, bf16[208,768]{1,0:T(8,128)(2,1)S(1)}, u32[]{:S(2)}, u32[]{:S(2)}) collective-permute-start(bf16[208,768]{1,0:T(8,128)(2,1)} %get-tuple-element.112.refs_2_.refs_5_), channel_id=1, source_target_pairs={{0,2},{1,3},{2,0},{3,1},{4,6},{5,7},{6,4},{7,5},{8,10},{9,11},{10,... | collective-permute-start | bytes 958472 | tf_op jit(solution)/shard_map/ppermute | solution.py:21
  14.1 11.6 %collective-permute-start.6 = (bf16[192,768]{1,0:T(8,128)(2,1)S(1)}, bf16[192,768]{1,0:T(8,128)(2,1)S(1)}, u32[]{:S(2)}, u32[]{:S(2)}) collective-permute-start(bf16[192,768]{1,0:T(8,128)(2,1)S(1)} %shard_map.205.refs_0_), channel_id=1, source_target_pairs={{0,2},{1,3},{2,0},{3,1},{4,6},{5,7},{6,4},{7,5},{8,10},{9,11},{10,... | collective-permute-start | bytes 884744 | tf_op jit(solution)/shard_map/ppermute | solution.py:21
  29.2 9.2 %collective-permute-start.8 = (bf16[128,768]{1,0:T(8,128)(2,1)S(1)}, bf16[128,768]{1,0:T(8,128)(2,1)S(1)}, u32[]{:S(2)}, u32[]{:S(2)}) collective-permute-start(bf16[128,768]{1,0:T(8,128)(2,1)S(1)} %get-tuple-element.115.refs_0_.refs_1_), channel_id=1, source_target_pairs={{0,4},{4,0},{8,12},{12,8},{1,5},{5,1},{9,13},{13,9},{2,6},{6,2},{1... | collective-permute-start | bytes 589832 | tf_op jit(solution)/shard_map/ppermute | solution.py:21
  29.3 9.0 %collective-permute-start.9 = (bf16[96,768]{1,0:T(8,128)(2,1)S(1)}, bf16[96,768]{1,0:T(8,128)(2,1)S(1)}, u32[]{:S(2)}, u32[]{:S(2)}) collective-permute-start(bf16[96,768]{1,0:T(8,128)(2,1)S(1)} %get-tuple-element.114.refs_7_.refs_1_), channel_id=1, source_target_pairs={{0,2},{1,3},{2,0},{3,1},{4,6},{5,7},{6,4},{7,5},{8,10},{9,11},{10,... | collective-permute-start | bytes 442376 | tf_op jit(solution)/shard_map/ppermute | solution.py:21
  38.5 12.5 %collective-permute-start.12 = (bf16[768,768]{1,0:T(8,128)(2,1)S(1)}, bf16[768,768]{1,0:T(8,128)(2,1)S(1)}, u32[]{:S(2)}, u32[]{:S(2)}) collective-permute-start(bf16[768,768]{1,0:T(8,128)(2,1)S(1)} %shard_map.210.refs_3_.refs_5_.refs_7_.refs_9_.refs_4_.refs_6_.refs_8_.refs_10_), channel_id=1, source_target_pairs={{0,1},{1,0},{2,3},{3,2},{4,5},{5,4},{6,7},{7,6},{8,9},{9,8},{10,11... | collective-permute-start | bytes 3538952 | tf_op jit(solution)/shard_map/ppermute | solution.py:21
  38.6 12.4 %collective-permute-start.11 = (bf16[128,768]{1,0:T(8,128)(2,1)S(1)}, bf16[128,768]{1,0:T(8,128)(2,1)S(1)}, u32[]{:S(2)}, u32[]{:S(2)}) collective-permute-start(bf16[128,768]{1,0:T(8,128)(2,1)S(1)} %shard_map.209.refs_6_.refs_0_), channel_id=1, source_target_pairs={{0,8},{4,12},{8,0},{12,4},{1,9},{5,13},{9,1},{13,5},{2,10},{6,14},... | collective-permute-start | bytes 589832 | tf_op jit(solution)/shard_map/ppermute | solution.py:21
  59.5 11.5 %collective-permute-start.18 = (bf16[128,768]{1,0:T(8,128)(2,1)S(1)}, bf16[128,768]{1,0:T(8,128)(2,1)S(1)}, u32[]{:S(2)}, u32[]{:S(2)}) collective-permute-start(bf16[128,768]{1,0:T(8,128)(2,1)S(1)} %shard_map.213.refs_1_), channel_id=1, source_target_pairs={{0,8},{4,12},{8,0},{12,4},{1,9},{5,13},{9,1},{13,5},{2,10},{6,14},... | collective-permute-start | bytes 589832 | tf_op jit(solution)/shard_map/ppermute | solution.py:21
  80.5 15.0 %collective-permute-start.25 = (bf16[384,768]{1,0:T(8,128)(2,1)S(1)}, bf16[384,768]{1,0:T(8,128)(2,1)S(1)}, u32[]{:S(2)}, u32[]{:S(2)}) collective-permute-start(bf16[384,768]{1,0:T(8,128)(2,1)S(1)} %shard_map.217.refs_7_.refs_9_.refs_11_), channel_id=1, source_target_pairs={{0,1},{1,0},{2,3},{3,2},{4,5},{5,4},{6,7},{7,6},{8,9},{9,8},{10,11... | collective-permute-start | bytes 1769480 | tf_op jit(solution)/shard_map/ppermute | solution.py:21
  80.6 15.0 %collective-permute-start.24 = (bf16[128,768]{1,0:T(8,128)(2,1)S(1)}, bf16[128,768]{1,0:T(8,128)(2,1)S(1)}, u32[]{:S(2)}, u32[]{:S(2)}) collective-permute-start(bf16[128,768]{1,0:T(8,128)(2,1)S(1)} %shard_map.216.refs_4_.refs_0_), channel_id=1, source_target_pairs={{0,8},{4,12},{8,0},{12,4},{1,9},{5,13},{9,1},{13,5},{2,10},{6,14},... | collective-permute-start | bytes 589832 | tf_op jit(solution)/shard_map/ppermute | solution.py:21
  81.3 14.3 %collective-permute-start.26 = (bf16[128,192]{1,0:T(8,128)(2,1)S(1)}, bf16[128,192]{1,0:T(8,128)(2,1)S(1)}, u32[]{:S(2)}, u32[]{:S(2)}) collective-permute-start(bf16[128,192]{1,0:T(8,128)(2,1)S(1)} %shard_map.218), channel_id=1, source_target_pairs={{0,0},{1,4},{2,8},{3,12},{4,1},{5,5},{6,9},{7,13},{8,2},{9,6},{10,... | collective-permute-start | bytes 147464 | tf_op jit(solution)/shard_map/ppermute | solution.py:27
  96.6 8.8 %collective-permute-start.27 = (bf16[128,768]{1,0:T(8,128)(2,1)S(1)}, bf16[128,768]{1,0:T(8,128)(2,1)S(1)}, u32[]{:S(2)}, u32[]{:S(2)}) collective-permute-start(bf16[128,768]{1,0:T(8,128)(2,1)S(1)} %get-tuple-element.128.refs_1_.refs_0_), channel_id=1, source_target_pairs={{0,4},{4,0},{8,12},{12,8},{1,5},{5,1},{9,13},{13,9},{2,6},{6,2},{1... | collective-permute-start | bytes 589832 | tf_op jit(solution)/shard_map/ppermute | solution.py:21
  105.5 8.5 %collective-permute-start.30 = (bf16[128,768]{1,0:T(8,128)(2,1)S(1)}, bf16[128,768]{1,0:T(8,128)(2,1)S(1)}, u32[]{:S(2)}, u32[]{:S(2)}) collective-permute-start(bf16[128,768]{1,0:T(8,128)(2,1)S(1)} %shard_map.221.refs_1_.refs_5_), channel_id=1, source_target_pairs={{0,8},{4,12},{8,0},{12,4},{1,9},{5,13},{9,1},{13,5},{2,10},{6,14},... | collective-permute-start | bytes 589832 | tf_op jit(solution)/shard_map/ppermute | solution.py:21
  124.1 11.5 %collective-permute-start.34 = (bf16[128,768]{1,0:T(8,128)(2,1)S(1)}, bf16[128,768]{1,0:T(8,128)(2,1)S(1)}, u32[]{:S(2)}, u32[]{:S(2)}) collective-permute-start(bf16[128,768]{1,0:T(8,128)(2,1)S(1)} %shard_map.226.refs_2_.refs_0_), channel_id=1, source_target_pairs={{0,8},{4,12},{8,0},{12,4},{1,9},{5,13},{9,1},{13,5},{2,10},{6,14},... | collective-permute-start | bytes 589832 | tf_op jit(solution)/shard_map/ppermute | solution.py:21
  138.1 9.0 %collective-permute-start.38 = (bf16[384,768]{1,0:T(8,128)(2,1)S(1)}, bf16[384,768]{1,0:T(8,128)(2,1)S(1)}, u32[]{:S(2)}, u32[]{:S(2)}) collective-permute-start(bf16[384,768]{1,0:T(8,128)(2,1)S(1)} %get-tuple-element.148), channel_id=1, source_target_pairs={{0,1},{1,0},{2,3},{3,2},{4,5},{5,4},{6,7},{7,6},{8,9},{9,8},{10,11... | collective-permute-start | bytes 1769480 | tf_op jit(solution)/shard_map/ppermute | solution.py:21
  138.2 8.9 %collective-permute-start.37 = (bf16[128,768]{1,0:T(8,128)(2,1)S(1)}, bf16[128,768]{1,0:T(8,128)(2,1)S(1)}, u32[]{:S(2)}, u32[]{:S(2)}) collective-permute-start(bf16[128,768]{1,0:T(8,128)(2,1)S(1)} %get-tuple-element.143.refs_1_.refs_2_.refs_0_), channel_id=1, source_target_pairs={{0,4},{4,0},{8,12},{12,8},{1,5},{5,1},{9,13},{13,9},{2,6},{6,2},{1... | collective-permute-start | bytes 589832 | tf_op jit(solution)/shard_map/ppermute | solution.py:21
  147.2 12.3 %collective-permute-start.41 = (bf16[128,768]{1,0:T(8,128)(2,1)S(1)}, bf16[128,768]{1,0:T(8,128)(2,1)S(1)}, u32[]{:S(2)}, u32[]{:S(2)}) collective-permute-start(bf16[128,768]{1,0:T(8,128)(2,1)S(1)} %shard_map.232.refs_1_.refs_2_.refs_0_), channel_id=1, source_target_pairs={{0,8},{4,12},{8,0},{12,4},{1,9},{5,13},{9,1},{13,5},{2,10},{6,14},... | collective-permute-start | bytes 589832 | tf_op jit(solution)/shard_map/ppermute | solution.py:21
  169.7 11.4 %collective-permute-start.51 = (bf16[192,768]{1,0:T(8,128)(2,1)S(1)}, bf16[192,768]{1,0:T(8,128)(2,1)S(1)}, u32[]{:S(2)}, u32[]{:S(2)}) collective-permute-start(bf16[192,768]{1,0:T(8,128)(2,1)S(1)} %get-tuple-element.170), channel_id=1, source_target_pairs={{0,2},{1,3},{2,0},{3,1},{4,6},{5,7},{6,4},{7,5},{8,10},{9,11},{10,... | collective-permute-start | bytes 884744 | tf_op jit(solution)/shard_map/ppermute | solution.py:21
  170.3 10.7 %collective-permute-start.50 = (bf16[128,768]{1,0:T(8,128)(2,1)S(1)}, bf16[128,768]{1,0:T(8,128)(2,1)S(1)}, u32[]{:S(2)}, u32[]{:S(2)}) collective-permute-start(bf16[128,768]{1,0:T(8,128)(2,1)S(1)} %shard_map.241.refs_2_.refs_1_), channel_id=1, source_target_pairs={{0,8},{4,12},{8,0},{12,4},{1,9},{5,13},{9,1},{13,5},{2,10},{6,14},... | collective-permute-start | bytes 589832 | tf_op jit(solution)/shard_map/ppermute | solution.py:21
  171.7 9.1 %collective-permute-start.52 = (bf16[96,768]{1,0:T(8,128)(2,1)S(1)}, bf16[96,768]{1,0:T(8,128)(2,1)S(1)}, u32[]{:S(2)}, u32[]{:S(2)}) collective-permute-start(bf16[96,768]{1,0:T(8,128)(2,1)S(1)} %get-tuple-element.171), channel_id=1, source_target_pairs={{0,2},{1,3},{2,0},{3,1},{4,6},{5,7},{6,4},{7,5},{8,10},{9,11},{10,... | collective-permute-start | bytes 442376 | tf_op jit(solution)/shard_map/ppermute | solution.py:21
  186.4 11.6 %collective-permute-start.60 = (bf16[208,768]{1,0:T(8,128)(2,1)S(1)}, bf16[208,768]{1,0:T(8,128)(2,1)S(1)}, u32[]{:S(2)}, u32[]{:S(2)}) collective-permute-start(bf16[208,768]{1,0:T(8,128)(2,1)S(1)} %get-tuple-element.194), channel_id=1, source_target_pairs={{0,2},{1,3},{2,0},{3,1},{4,6},{5,7},{6,4},{7,5},{8,10},{9,11},{10,... | collective-permute-start | bytes 958472 | tf_op jit(solution)/shard_map/ppermute | solution.py:21
  188.1 21.7 %collective-permute-start.62 = (bf16[288,768]{1,0:T(8,128)(2,1)S(1)}, bf16[288,768]{1,0:T(8,128)(2,1)S(1)}, u32[]{:S(2)}, u32[]{:S(2)}) collective-permute-start(bf16[288,768]{1,0:T(8,128)(2,1)S(1)} %shard_map.251.refs_0_.refs_1_), channel_id=1, source_target_pairs={{0,16},{16,0},{1,17},{17,1},{2,18},{18,2},{3,19},{19,3},{4,20},{20... | collective-permute-start | bytes 1327112 | tf_op jit(solution)/shard_map/ppermute | solution.py:21
  198.1 12.8 %collective-permute-start.61 = (bf16[208,768]{1,0:T(8,128)(2,1)S(1)}, bf16[208,768]{1,0:T(8,128)(2,1)S(1)}, u32[]{:S(2)}, u32[]{:S(2)}) collective-permute-start(bf16[208,768]{1,0:T(8,128)(2,1)S(1)} %shard_map.250.refs_0_), channel_id=1, source_target_pairs={{0,16},{16,0},{1,17},{17,1},{2,18},{18,2},{3,19},{19,3},{4,20},{20... | collective-permute-start | bytes 958472 | tf_op jit(solution)/shard_map/ppermute | solution.py:21
  200.2 8.9 %collective-permute-start.58 = (bf16[384,128]{1,0:T(8,128)(2,1)S(1)}, bf16[384,128]{1,0:T(8,128)(2,1)S(1)}, u32[]{:S(2)}, u32[]{:S(2)}) collective-permute-start(bf16[384,128]{1,0:T(8,128)(2,1)S(1)} %shard_map.246.refs_2_), channel_id=1, source_target_pairs={{0,0},{1,4},{2,8},{3,12},{4,1},{5,5},{6,9},{7,13},{8,2},{9,6},{10,... | collective-permute-start | bytes 294920 | tf_op jit(solution)/shard_map/ppermute | solution.py:27
  (49 other events, 335.9 us)
